TPU v7x, 32 devices: a whole 2x2x4 slice. The times are simulated.
32 devices in a mesh: band: 8 (over z, y), lon: 4 (over x, core).
Axes of the slice: x: 2, y: 2, z: 4, core: 2. Of those that a mesh axis runs over, the one named last changes fastest.
Arguments:
- source: bfloat16 [4096, 8, 128], P(('band', 'lon')), may hold values from -6 to 6
- routes: int32 [4096, 2], P(('band', 'lon')), may hold values from 0 to 11, as said below
- slot_weights: bfloat16 [32, 12, 32, 128, 128], P(('band', 'lon')), may hold values from -0.5 to 0.5
- window: int32 [32, 12, 32], P(('band', 'lon')), may hold values from 0 to 255
- stem_weight: bfloat16 [9, 8, 128], replicated, may hold values from -0.75 to 0.75
- stem_bias: float32 [128], replicated, may hold values from -3 to 3
- mix_weight: bfloat16 [9, 128, 128], replicated, may hold values from -0.1875 to 0.1875
- mix_bias: float32 [128], replicated, may hold values from -3 to 3
Outputs:
- features: bfloat16 [512, 2048, 128], P('band', 'lon')
Inputs may be any that keep to these rules, and one draw needn't show every extreme that they name: `routes`: each cell block names 2 different codes, never a band outside the grid. Among one device's blocks no code is named more than 32 times, and the device's own tile (code 4) exactly 32 times except in the first and last band. A device of another band names only longitude offsets 0, 1 and 3. A device of the first band names each code of band offsets 0 and +1 exactly 32 times; one of the last band each code of band offsets -1 and 0 exactly 32 times.
All inputs are finite; a program needn't handle non-finite values.
Results may differ from a plain program's by a relative error of at most 0.0056.
Values may be sent and summed in bfloat16 or wider, within the bound.
No kernel may reach another device: no remote copies, remote signals or barrier semaphores. Data moves between devices by JAX's collectives and lax.ppermute only.
A program may use at most 128 MiB of HBM per device.

v0:
```python
import jax
import jax.numpy as jnp
from jax import lax
from jax.sharding import PartitionSpec as P

ROWS_DEV = 64
COLS_DEV = 512


def shifted(block, axis, distance):
    devices = range(lax.axis_size(axis))
    route = [(i - distance, i) for i in devices if i - distance in devices]
    return lax.ppermute(block, axis, route)


def extended(block, sides, width, periodic):
    for axis, dim in sides:
        count = lax.axis_size(axis)
        forward = [(i, i + 1) for i in range(count - 1)]
        if periodic:
            forward.append((count - 1, 0))
        backward = [(target, source) for source, target in forward]
        low = lax.ppermute(
            lax.slice_in_dim(block, block.shape[dim] - width, None, axis=dim), axis, forward
        )
        high = lax.ppermute(lax.slice_in_dim(block, 0, width, axis=dim), axis, backward)
        block = jnp.concatenate([low, block, high], axis=dim)
    return block


def stem_conv(padded, weight, rows, cols):
    stacked = jnp.concatenate(
        [padded[:, tap // 3 : tap // 3 + rows, tap % 3 : tap % 3 + cols] for tap in range(9)],
        axis=0,
    )
    flat_weight = weight.reshape(9 * weight.shape[1], weight.shape[2])
    return jnp.einsum("fhw,fc->hwc", stacked, flat_weight, preferred_element_type=jnp.float32)


def mix_conv(padded, weight):
    kernel = weight.reshape(3, 3, weight.shape[1], weight.shape[2])
    result = lax.conv_general_dilated(
        padded[None],
        kernel,
        (1, 1),
        "VALID",
        dimension_numbers=("NHWC", "HWIO", "NHWC"),
        preferred_element_type=jnp.float32,
    )
    return result[0]


def on_device(source, routes, slot_weights, window, stem_weight, stem_bias, mix_weight, mix_bias):
    n_band = lax.axis_size("band")
    n_lon = lax.axis_size("lon")
    lon_here = lax.axis_index("lon")
    blk_dev, fields, cells = source.shape
    nbr = slot_weights.shape[1]
    cap = slot_weights.shape[2]
    pixels = slot_weights.shape[4]
    top = routes.shape[1]
    rows = ROWS_DEV
    cols = COLS_DEV
    nwin = rows * cols // pixels
    flat_dest = routes.reshape(-1)
    onehot = (flat_dest[:, None] == jnp.arange(nbr, dtype=jnp.int32)[None, :]).astype(jnp.int32)
    before = jnp.cumsum(onehot, axis=0) - onehot
    rank = jnp.sum(before * onehot, axis=1)
    target_slot = flat_dest * cap + rank
    select = (jnp.arange(nbr * cap, dtype=jnp.int32)[:, None] == target_slot[None, :]).astype(
        jnp.bfloat16
    )
    repeated = jnp.repeat(source.reshape(blk_dev, fields * cells), top, axis=0)
    outgoing = jnp.dot(select, repeated, preferred_element_type=jnp.float32).astype(jnp.bfloat16)
    outgoing = outgoing.reshape(3, n_lon, cap, fields, cells)
    lanes = jnp.arange(n_lon, dtype=jnp.int32)
    to_absolute = (lanes - lon_here) % n_lon
    to_relative = (lon_here - lanes) % n_lon
    absolute = jnp.take(outgoing, to_absolute, axis=1)
    arrived = lax.all_to_all(absolute, "lon", split_axis=1, concat_axis=1, tiled=True)
    arrived = jnp.take(arrived, to_relative, axis=1)
    from_north = shifted(arrived[0], "band", -1)
    from_south = shifted(arrived[2], "band", 1)
    incoming = jnp.stack([from_north, arrived[1], from_south], axis=0)
    incoming = incoming.reshape(nbr, cap, fields, cells)
    contrib = jnp.einsum(
        "qcfk,qckp->qcfp", incoming, slot_weights[0], preferred_element_type=jnp.float32
    ).astype(jnp.bfloat16)
    place = (jnp.arange(nwin, dtype=jnp.int32)[:, None] == window[0].reshape(-1)[None, :]).astype(
        jnp.bfloat16
    )
    summed = jnp.dot(
        place, contrib.reshape(nbr * cap, fields * pixels), preferred_element_type=jnp.float32
    )
    field = summed.reshape(rows, cols // pixels, fields, pixels).transpose(2, 0, 1, 3)
    field = field.reshape(fields, rows, cols).astype(jnp.bfloat16)
    with_rows = extended(field, (("band", 1),), 2, False)
    full = extended(with_rows, (("lon", 2),), 2, True)
    hidden = jax.nn.silu(stem_conv(full, stem_weight, rows + 2, cols + 2) + stem_bias)
    global_rows = lax.axis_index("band") * rows - 1 + jnp.arange(rows + 2, dtype=jnp.int32)
    valid = (global_rows >= 0) & (global_rows < rows * n_band)
    hidden_full = jnp.where(valid[:, None, None], hidden, 0.0).astype(jnp.bfloat16)
    result = mix_conv(hidden_full, mix_weight) + mix_bias
    return result.astype(jnp.bfloat16)


def solution(mesh):
    in_specs = (
        P(("band", "lon"), None, None),
        P(("band", "lon"), None),
        P(("band", "lon"), None, None, None, None),
        P(("band", "lon"), None, None),
        P(),
        P(),
        P(),
        P(),
    )
    out_specs = P("band", "lon", None)
    return jax.shard_map(
        on_device, mesh=mesh, in_specs=in_specs, out_specs=out_specs, check_vma=False
    )
```

profile of v0, /device:TPU:0, one launch (start us, length us, event | category | flops | bytes accessed | tf_op | source)
XLA Modules:
  0.0 149.9 jit_solution(468723010692043261)
XLA Ops:
  0.0 0.8 copy.14
  2.1 1.0 copy.40
  4.9 1.0 select_bitcast_fusion.1
  5.9 4.2 %all-to-all-start = ((bf16[3,4,32,8,128]{4,3,2,0,1:T(8,128)(2,1)}), bf16[3,4,32,8,128]{4,3,2,0,1:T(8,128)(2,1)S(1)}, u32[]{:S(2)}, u32[]{:S(2)}) async-start(bf16[3,4,32,8,128]{4,3,2,0,1:T(8,128)(2,1)} %select_bitcast_fusion.1), calls=%async_computation | async-start | bytes 1572864 | tf_op jit(solution)/shard_map/all_to_all | solution.py:80
  10.2 11.6 %all-to-all-done = bf16[3,4,32,8,128]{4,3,2,0,1:T(8,128)(2,1)S(1)} async-done(((bf16[3,4,32,8,128]{4,3,2,0,1:T(8,128)(2,1)}), bf16[3,4,32,8,128]{4,3,2,0,1:T(8,128)(2,1)S(1)}, u32[]{:S(2)}, u32[]{:S(2)}) %all-to-all-start) | async-done | bytes 786464 | tf_op jit(solution)/shard_map/all_to_all | solution.py:80
  22.7 1.3 collective-permute-start
  24.0 4.8 %collective-permute-start.1 = (bf16[4,32,8,128]{3,2,1,0:T(8,128)(2,1)S(1)}, bf16[4,32,8,128]{3,2,1,0:T(8,128)(2,1)S(1)}, u32[]{:S(2)}, u32[]{:S(2)}) collective-permute-start(bf16[4,32,8,128]{3,2,1,0:T(8,128)(2,1)S(1)} %get-tuple-element.7), channel_id=1, source_target_pairs={{0,4},{4,8},{8,12},{12,16},{16,20},{20,24},{24,28},{1,5},{5,9},{9,... | collective-permute-start | bytes 786440 | tf_op jit(solution)/shard_map/ppermute | solution.py:13
  28.9 4.0 %collective-permute-done = bf16[4,32,8,128]{3,2,1,0:T(8,128)(2,1)S(1)} collective-permute-done((bf16[4,32,8,128]{3,2,1,0:T(8,128)(2,1)S(1)}, bf16[4,32,8,128]{3,2,1,0:T(8,128)(2,1)S(1)}, u32[]{:S(2)}, u32[]{:S(2)}) %collective-permute-start) | collective-permute-done | bytes 262176 | tf_op jit(solution)/shard_map/ppermute | solution.py:13
  32.9 5.8 %collective-permute-done.1 = bf16[4,32,8,128]{3,2,1,0:T(8,128)(2,1)S(1)} collective-permute-done((bf16[4,32,8,128]{3,2,1,0:T(8,128)(2,1)S(1)}, bf16[4,32,8,128]{3,2,1,0:T(8,128)(2,1)S(1)}, u32[]{:S(2)}, u32[]{:S(2)}) %collective-permute-start.1) | collective-permute-done | bytes 262176 | tf_op jit(solution)/shard_map/ppermute | solution.py:13
  38.8 6.3 %fusion.13 = bf16[12,32,8,128]{3,2,1,0:T(8,128)(2,1)S(1)} fusion(bf16[12,32,8,128]{3,2,1,0:T(8,128)(2,1)S(1)} %bitcast.86, bf16[1,12,32,128,128]{4,3,2,1,0:T(8,128)(2,1)} %param.12), kind=kOutput, calls=%fused_computation.18 | convolution fusion | flops 101056512 | bytes 14155776 | tf_op jit(solution)/shard_map/qcfk,qckp->qcfp/dot_general | solution.py:86
  46.8 4.4 %collective-permute-start.2 = (bf16[8,2,512]{2,0,1:T(8,128)(2,1)S(1)}, bf16[8,2,512]{2,0,1:T(8,128)(2,1)S(1)}, u32[]{:S(2)}, u32[]{:S(2)}) collective-permute-start(bf16[8,2,512]{2,0,1:T(8,128)(2,1)S(1)} %get-tuple-element.12), channel_id=1, source_target_pairs={{0,4},{4,8},{8,12},{12,16},{16,20},{20,24},{24,28},{1,5},{5,9},{9,... | collective-permute-start | bytes 49160 | tf_op jit(solution)/shard_map/ppermute | solution.py:23
  51.2 1.3 collective-permute-start.3
  52.7 4.2 %collective-permute-done.3 = bf16[8,2,512]{2,0,1:T(8,128)(2,1)S(1)} collective-permute-done((bf16[8,2,512]{2,0,1:T(8,128)(2,1)S(1)}, bf16[8,2,512]{2,0,1:T(8,128)(2,1)S(1)}, u32[]{:S(2)}, u32[]{:S(2)}) %collective-permute-start.3) | collective-permute-done | bytes 16416 | tf_op jit(solution)/shard_map/ppermute | solution.py:26
  57.1 1.7 %collective-permute-start.5 = (bf16[8,68,2]{2,0,1:T(8,128)(2,1)S(1)}, bf16[8,68,2]{2,0,1:T(8,128)(2,1)S(1)}, u32[]{:S(2)}, u32[]{:S(2)}) collective-permute-start(bf16[8,68,2]{2,0,1:T(8,128)(2,1)S(1)} %get-tuple-element.9), channel_id=1, source_target_pairs={{1,0},{2,1},{3,2},{0,3},{5,4},{6,5},{7,6},{4,7},{9,8},{10,9},{11,1... | collective-permute-start | bytes 6536 | tf_op jit(solution)/shard_map/ppermute | solution.py:26
  58.8 3.3 %collective-permute-done.4 = bf16[8,68,2]{2,0,1:T(8,128)(2,1)S(1)} collective-permute-done((bf16[8,68,2]{2,0,1:T(8,128)(2,1)S(1)}, bf16[8,68,2]{2,0,1:T(8,128)(2,1)S(1)}, u32[]{:S(2)}, u32[]{:S(2)}) %collective-permute-start.4) | collective-permute-done | bytes 2208 | tf_op jit(solution)/shard_map/ppermute | solution.py:23
  65.0 9.6 %fusion.11 = bf16[66,1,514,128]{3,2,0,1:T(8,128)(2,1)} fusion(f32[128]{0:T(128)S(1)} %copy-done.4, bf16[72,66,514]{2,0,1:T(8,128)(2,1)S(1)} %fusion.26, pred[66]{0:T(512)(128)(4,1)S(1)} %compare_and_fusion.2, bf16[9,8,128]{2,1,0:T(8,128)(2,1)S(1)} %copy-done.3), kind=kOutput, calls=%fused_computation.16 | convolution fusion | flops 655683072 | bytes 13588610 | tf_op jit(solution)/shard_map/fhw,fc->hwc/dot_general | solution.py:37
  74.7 7.5 %pad = bf16[66,1,520,128]{3,2,0,1:T(8,128)(2,1)} pad(bf16[66,1,514,128]{3,2,0,1:T(8,128)(2,1)} %fusion.11, bf16[]{:T(256)} %constant.62), padding=0_0x0_0x0_6x0_0 | pad | bytes 17470466 | tf_op jit(solution)/shard_map/broadcast_in_dim | solution.py:43
  82.2 13.8 %reshape.97 = bf16[66,1,8,65,128]{4,3,2,0,1:T(8,128)(2,1)} reshape(bf16[66,1,520,128]{3,2,0,1:T(8,128)(2,1)} %pad) | data formatting | bytes 17571840 | tf_op jit(solution)/shard_map/conv_general_dilated | solution.py:42
  96.0 8.6 %copy.25 = bf16[66,1,8,65,128]{4,2,3,0,1:T(8,128)(2,1)} copy(bf16[66,1,8,65,128]{4,3,2,0,1:T(8,128)(2,1)} %reshape.97) | data formatting | bytes 17571840 | tf_op jit(solution)/shard_map/conv_general_dilated | solution.py:42
  104.5 1.0 slice.103
  105.6 22.3 %convolution_select_fusion = f32[64,8,65,128]{3,1,2,0:T(8,128)S(1)} fusion(bf16[3,3,128,128]{3,2,1,0:T(8,128)(2,1)S(1)} %bitcast.84, bf16[66,1,7,2,128]{4,2,3,0,1:T(8,128)(2,1)S(1)} %slice.103, bf16[66,1,8,65,128]{4,2,3,0,1:T(8,128)(2,1)} %copy.25, pred[8,65]{0,1:T(8,128)(4,1)S(1)} %copy-done.5), kind=kOutput, calls=%fused_computation.10 | convolution fusion | flops 9846099968 | bytes 26357256 | tf_op jit(solution)/shard_map/conv_general_dilated | solution.py:42
  127.9 5.3 %copy.26 = f32[64,8,65,128]{3,0,2,1:T(8,128)S(1)} copy(f32[64,8,65,128]{3,1,2,0:T(8,128)S(1)} %convolution_select_fusion) | data formatting | bytes 34078720 | tf_op jit(solution)/shard_map/conv_general_dilated | solution.py:42
  133.2 4.5 %fusion.2 = bf16[64,512,128]{2,0,1:T(8,128)(2,1)} fusion(f32[64,1,520,128]{3,0,2,1:T(8,128)S(1)} %bitcast.85, f32[128]{0:T(128)S(1)} %copy-done.2), kind=kLoop, calls=%fused_computation.7 | loop fusion | flops 8388608 | bytes 25166336 | tf_op jit(solution)/shard_map/convert_element_type | solution.py:104
  137.7 12.2 %copy.27 = bf16[64,512,128]{2,1,0:T(8,128)(2,1)} copy(bf16[64,512,128]{2,0,1:T(8,128)(2,1)} %fusion.2) | data formatting | bytes 16777216 | tf_op jit(solution)/shard_map/convert_element_type | solution.py:104
  (67 shorter events, 9.0 us)
Async XLA Ops:
  0.0 105.6 %copy-start = (bf16[9,128,128]{2,1,0:T(8,128)(2,1)S(1)}, bf16[9,128,128]{2,1,0:T(8,128)(2,1)}, u32[]{:S(2)}) copy-start(bf16[9,128,128]{2,1,0:T(8,128)(2,1)} %param.16) | copy-start | bytes 884740
  3.6 25.2 %copy-start.1 = (s32[1,12,32]{2,0,1:T(1,128)S(1)}, s32[1,12,32]{2,0,1:T(1,128)}, u32[]{:S(2)}) copy-start(s32[1,12,32]{2,0,1:T(1,128)} %param.13) | copy-start | bytes 4612
  5.9 15.9 %all-to-all-start = ((bf16[3,4,32,8,128]{4,3,2,0,1:T(8,128)(2,1)}), bf16[3,4,32,8,128]{4,3,2,0,1:T(8,128)(2,1)S(1)}, u32[]{:S(2)}, u32[]{:S(2)}) async-start(bf16[3,4,32,8,128]{4,3,2,0,1:T(8,128)(2,1)} %select_bitcast_fusion.1), calls=%async_computation | async-start | bytes 1572864 | tf_op jit(solution)/shard_map/all_to_all | solution.py:80
  22.7 10.2 %collective-permute-start = (bf16[4,32,8,128]{3,2,1,0:T(8,128)(2,1)S(1)}, bf16[4,32,8,128]{3,2,1,0:T(8,128)(2,1)S(1)}, u32[]{:S(2)}, u32[]{:S(2)}) collective-permute-start(bf16[4,32,8,128]{3,2,1,0:T(8,128)(2,1)S(1)} %get-tuple-element.6), channel_id=1, source_target_pairs={{4,0},{8,4},{12,8},{16,12},{20,16},{24,20},{28,24},{5,1},{9,5},{13... | collective-permute-start | bytes 786440 | tf_op jit(solution)/shard_map/ppermute | solution.py:13
  24.0 14.7 %collective-permute-start.1 = (bf16[4,32,8,128]{3,2,1,0:T(8,128)(2,1)S(1)}, bf16[4,32,8,128]{3,2,1,0:T(8,128)(2,1)S(1)}, u32[]{:S(2)}, u32[]{:S(2)}) collective-permute-start(bf16[4,32,8,128]{3,2,1,0:T(8,128)(2,1)S(1)} %get-tuple-element.7), channel_id=1, source_target_pairs={{0,4},{4,8},{8,12},{12,16},{16,20},{20,24},{24,28},{1,5},{5,9},{9,... | collective-permute-start | bytes 786440 | tf_op jit(solution)/shard_map/ppermute | solution.py:13
  46.8 5.8 %collective-permute-start.2 = (bf16[8,2,512]{2,0,1:T(8,128)(2,1)S(1)}, bf16[8,2,512]{2,0,1:T(8,128)(2,1)S(1)}, u32[]{:S(2)}, u32[]{:S(2)}) collective-permute-start(bf16[8,2,512]{2,0,1:T(8,128)(2,1)S(1)} %get-tuple-element.12), channel_id=1, source_target_pairs={{0,4},{4,8},{8,12},{12,16},{16,20},{20,24},{24,28},{1,5},{5,9},{9,... | collective-permute-start | bytes 49160 | tf_op jit(solution)/shard_map/ppermute | solution.py:23
  51.2 5.6 %collective-permute-start.3 = (bf16[8,2,512]{2,0,1:T(8,128)(2,1)S(1)}, bf16[8,2,512]{2,0,1:T(8,128)(2,1)S(1)}, u32[]{:S(2)}, u32[]{:S(2)}) collective-permute-start(bf16[8,2,512]{2,0,1:T(8,128)(2,1)S(1)} %get-tuple-element.11), channel_id=1, source_target_pairs={{4,0},{8,4},{12,8},{16,12},{20,16},{24,20},{28,24},{5,1},{9,5},{13... | collective-permute-start | bytes 49160 | tf_op jit(solution)/shard_map/ppermute | solution.py:26
  57.0 5.1 %collective-permute-start.4 = (bf16[8,68,2]{2,0,1:T(8,128)(2,1)S(1)}, bf16[8,68,2]{2,0,1:T(8,128)(2,1)S(1)}, u32[]{:S(2)}, u32[]{:S(2)}) collective-permute-start(bf16[8,68,2]{2,0,1:T(8,128)(2,1)S(1)} %get-tuple-element.10), channel_id=1, source_target_pairs={{0,1},{1,2},{2,3},{3,0},{4,5},{5,6},{6,7},{7,4},{8,9},{9,10},{10,1... | collective-permute-start | bytes 6536 | tf_op jit(solution)/shard_map/ppermute | solution.py:23
  57.1 5.3 %collective-permute-start.5 = (bf16[8,68,2]{2,0,1:T(8,128)(2,1)S(1)}, bf16[8,68,2]{2,0,1:T(8,128)(2,1)S(1)}, u32[]{:S(2)}, u32[]{:S(2)}) collective-permute-start(bf16[8,68,2]{2,0,1:T(8,128)(2,1)S(1)} %get-tuple-element.9), channel_id=1, source_target_pairs={{1,0},{2,1},{3,2},{0,3},{5,4},{6,5},{7,6},{4,7},{9,8},{10,9},{11,1... | collective-permute-start | bytes 6536 | tf_op jit(solution)/shard_map/ppermute | solution.py:26
  62.4 2.6 %copy-start.3 = (bf16[9,8,128]{2,1,0:T(8,128)(2,1)S(1)}, bf16[9,8,128]{2,1,0:T(8,128)(2,1)}, u32[]{:S(2)}) copy-start(bf16[9,8,128]{2,1,0:T(8,128)(2,1)} %param.14) | copy-start | bytes 55300
  62.4 2.6 %copy-start.4 = (f32[128]{0:T(128)S(1)}, f32[128]{0:T(128)}, u32[]{:S(2)}) copy-start(f32[128]{0:T(128)} %param.15) | copy-start | bytes 1540
  96.0 9.6 %copy-start.5 = (pred[8,65]{0,1:T(8,128)(4,1)S(1)}, pred[8,65]{0,1:T(8,128)(4,1)}, u32[]{:S(2)}) copy-start(pred[8,65]{0,1:T(8,128)(4,1)} %constant.66) | copy-start | bytes 1564
  127.9 5.3 %copy-start.2 = (f32[128]{0:T(128)S(1)}, f32[128]{0:T(128)}, u32[]{:S(2)}) copy-start(f32[128]{0:T(128)} %param.17) | copy-start | bytes 1540
where the time goes:
time: 151 us; the launch traced here: 150 us
  local copies, waits for them, and re-layouts  55.4 us (37%)
  matrix products  39.1 us (26%)
  waiting for transfers between devices  29 us (19%)
  starting transfers between devices  17.7 us (12%)
  other arithmetic  8.25 us (5%)
    conv_general_dilated x4, local copies, waits for them, and re-layouts, mix_conv(): lax.conv_general_dilated(padded[None], kernel, (1, 1), 'VALID', dimension...  28.7 us
    conv_general_dilated x1, matrix products, mix_conv(): lax.conv_general_dilated(padded[None], kernel, (1, 1), 'VALID', dimension...  22.3 us
    convert_element_type x1, local copies, waits for them, and re-layouts, on_device(): return result.astype(jnp.bfloat16)  12.2 us
    all_to_all x1, waiting for transfers between devices, on_device(): lax.all_to_all(absolute, 'lon', split_axis=1, concat_axis=1, tiled=True)  11.6 us
    ppermute x2, waiting for transfers between devices, shifted(): return lax.ppermute(block, axis, route)  9.8 us
    dot_general x1, matrix products, stem_conv(): jnp.einsum('fhw,fc->hwc', stacked, flat_weight, preferred_element_type=jn...  9.62 us
    broadcast_in_dim x1, local copies, waits for them, and re-layouts, mix_conv(): padded[None]  7.5 us
    dot_general x1, matrix products, on_device(): jnp.einsum('qcfk,qckp->qcfp', incoming, slot_weights[0], preferred_elemen...  6.35 us
  transfers between devices with their start and end apart: 7, of which 6 were waited for; matrix products, arithmetic and copies ran while one was open for 0% of the time, Pallas kernels for 0%

commit v1 on v0

v1 whole, which is shorter than its diff:
```python
import functools

import jax
import jax.numpy as jnp
from jax import lax
from jax.experimental import pallas as pl
from jax.experimental.pallas import tpu as pltpu
from jax.sharding import PartitionSpec as P

ROWS = 64
COLS = 512
PAIRS = COLS // 2
HROWS = 264
LANES = 384
STEP = 6
BLOCKS = (ROWS + 2) // STEP
SCALE = 1.0 / 2.0
BF = jnp.bfloat16
F32 = jnp.float32
VM = pl.BlockSpec(memory_space=pltpu.VMEM)
SM = pl.BlockSpec(memory_space=pltpu.SMEM)
ANY = pl.BlockSpec(memory_space=pl.ANY)


def params(mib):
    return pltpu.CompilerParams(vmem_limit_bytes=mib << 20)


def cost(flops, size):
    return pl.CostEstimate(flops=flops, bytes_accessed=size, transcendentals=0)


def swap_core(n_band, n_lon):
    return [(b * n_lon + l, b * n_lon + (l ^ 1)) for b in range(n_band) for l in range(n_lon)]


def swap_x(n_band, n_lon):
    return [(b * n_lon + l, b * n_lon + n_lon - 1 - l) for b in range(n_band) for l in range(n_lon)]


def swap_a(n_band, n_lon):
    return [(b * n_lon + l, (b ^ 1) * n_lon + l) for b in range(n_band) for l in range(n_lon)]


def swap_b(n_band, n_lon, across):
    pairs = []
    for b in range(n_band):
        partner = b + 1 if b % 2 else b - 1
        for l in range(n_lon):
            if 0 <= partner < n_band:
                pairs.append((b * n_lon + l, partner * n_lon + l))
            elif across:
                pairs.append((b * n_lon + l, b * n_lon + (l + 2) % n_lon))
    return pairs


def swap_far(n_band, n_lon):
    pairs = []
    for b, c in ((0, 1), (1, 0), (n_band - 1, n_band - 2), (n_band - 2, n_band - 1)):
        pairs += [(b * n_lon + l, c * n_lon + (l + 2) % n_lon) for l in range(n_lon)]
    return pairs


def pack_kernel(pos_ref, routes_ref, src_ref, own_ref, core_ref, x_ref, far_ref, buf, table, count):
    band = pos_ref[0]
    lon = pos_ref[1]
    a_dir = 1 - 2 * (band % 2)
    core_dl = 1 + 2 * (lon % 2)
    for q in range(12):
        db, dl = q // 4 - 1, q % 4
        if db == 0:
            way = 1
        else:
            way = jnp.where(a_dir == db, 0, 2)
        if dl == 0:
            group = way
        elif dl == 2:
            group = 2 if db == 0 else 9
        else:
            group = jnp.where(core_dl == dl, 3, 6) + way
        table[q] = group * 32
        count[q] = 0
    buf[...] = jnp.zeros_like(buf)

    def one(j, carry):
        block = src_ref[j]
        for t in range(2):
            q = routes_ref[t, j]
            rank = count[q]
            count[q] = rank + 1
            buf[table[q] + rank] = block
        return carry

    lax.fori_loop(0, src_ref.shape[0], one, 0, unroll=8)
    own_ref[...] = buf[0:96]
    core_ref[...] = buf[96:192]
    x_ref[...] = buf[192:288]
    far_ref[...] = buf[288:320]


def pack(pos, routes, source):
    fields, cells = source.shape[1:]
    shape = lambda n: jax.ShapeDtypeStruct((n, fields, cells), BF)
    return pl.pallas_call(
        pack_kernel,
        in_specs=[SM, SM, VM],
        out_specs=[VM] * 4,
        out_shape=[shape(96), shape(96), shape(96), shape(32)],
        scratch_shapes=[
            pltpu.VMEM((320, fields, cells), BF),
            pltpu.SMEM((12,), jnp.int32),
            pltpu.SMEM((12,), jnp.int32),
        ],
        compiler_params=params(16),
        cost_estimate=cost(0, 1 << 20),
        name="pack",
    )(pos, routes, source)


def prep_kernel(stem_ref, mix_ref, ws_ref, wm_ref):
    zero8 = jnp.zeros((8, 128), F32)
    taps = [stem_ref[t].astype(F32) * SCALE for t in range(9)]
    for i in range(STEP):
        for par in range(2):
            rows = []
            for d in range(4):
                for row in range(8):
                    a, b = row - i, d - par
                    rows.append(taps[3 * a + b] if 0 <= a < 3 and 0 <= b < 3 else zero8)
            lane = (2 * i + par) * 128
            ws_ref[:, lane : lane + 128] = jnp.concatenate(rows, axis=0).astype(BF)
    zero = jnp.zeros((128, 128), BF)
    for a in range(3):
        for par in range(2):
            for d in range(4):
                b = d - par
                wm_ref[a, d * 128 : d * 128 + 128, par * 128 : par * 128 + 128] = (
                    mix_ref[3 * a + b] if 0 <= b < 3 else zero
                )


def prep(stem_weight, mix_weight):
    return pl.pallas_call(
        prep_kernel,
        in_specs=[VM] * 2,
        out_specs=[VM] * 2,
        out_shape=[
            jax.ShapeDtypeStruct((256, STEP * 256), BF),
            jax.ShapeDtypeStruct((3, 512, 256), BF),
        ],
        compiler_params=params(16),
        cost_estimate=cost(0, 2 << 20),
        name="prep",
    )(stem_weight, mix_weight)


def contrib_kernel(pieces, first, codes_ref, win_ref, *refs):
    arrays = refs[: len(pieces)]
    refs = refs[len(pieces) :]
    if first:
        w_ref, out_ref, inc, acc = refs
    else:
        w_ref, start_ref, pos_ref, fld_ref, a_ref, b_ref, inc, acc = refs
    g = pl.program_id(0)

    @pl.when(g == 0)
    def _():
        if first:
            acc[...] = jnp.zeros_like(acc)
        else:
            acc[...] = start_ref[...]

    number = 0
    for array, groups in zip(arrays, pieces):
        for i in groups:

            @pl.when(g == number)
            def _(array=array, i=i):
                inc[...] = array[i * 32 : i * 32 + 32]

            number += 1
    q = codes_ref[g]
    for s in range(32):
        part = jnp.dot(inc[s], w_ref[0, 0, s], preferred_element_type=F32).astype(BF).astype(F32)
        w = win_ref[q, s]
        place = (w % 4) * ROWS + w // 4
        acc[place] = acc[place] + part

    @pl.when(g == number - 1)
    def _():
        if first:
            out_ref[...] = acc[...]
        else:
            for cb in range(4):
                rows = acc[cb * ROWS : (cb + 1) * ROWS].reshape(ROWS * 8, 128)
                fld_ref[:, cb * 128 : cb * 128 + 128] = rows.astype(BF)
            even = pos_ref[0] % 2 == 0
            top, bottom = fld_ref[0:16], fld_ref[ROWS * 8 - 16 : ROWS * 8]
            a_ref[...] = jnp.where(even, bottom, top)
            b_ref[...] = jnp.where(even, top, bottom)


def contrib(first, codes, win, arrays, pieces, weights, extra=()):
    groups = sum(len(p) for p in pieces)
    whole = lambda a: pl.BlockSpec(a.shape, lambda g, *_: (0,) * a.ndim)
    if first:
        out_shape = jax.ShapeDtypeStruct((ROWS * 4, 8, 128), F32)
        out_specs = pl.BlockSpec((ROWS * 4, 8, 128), lambda g, *_: (0, 0, 0))
        extra_specs = []
    else:
        out_shape = [
            jax.ShapeDtypeStruct((ROWS * 8, COLS), BF),
            jax.ShapeDtypeStruct((16, COLS), BF),
            jax.ShapeDtypeStruct((16, COLS), BF),
        ]
        out_specs = [pl.BlockSpec(o.shape, lambda g, *_: (0, 0)) for o in out_shape]
        extra_specs = [whole(extra[0]), SM]
    spec = pltpu.PrefetchScalarGridSpec(
        num_scalar_prefetch=2,
        grid=(groups,),
        in_specs=[whole(a) for a in arrays]
        + [pl.BlockSpec((1, 1, 32, 128, 128), lambda g, codes, win: (0, codes[g], 0, 0, 0))]
        + extra_specs,
        out_specs=out_specs,
        scratch_shapes=[pltpu.VMEM((32, 8, 128), BF), pltpu.VMEM((ROWS * 4, 8, 128), F32)],
    )
    return pl.pallas_call(
        functools.partial(contrib_kernel, pieces, first),
        grid_spec=spec,
        out_shape=out_shape,
        compiler_params=params(24),
        cost_estimate=cost(groups * 32 * 2 * 8 * 128 * 128, groups << 20),
        name="contrib_near" if first else "contrib_far",
    )(codes, win, *arrays, weights, *extra)


def tall(fld_ref, a, b, even):
    north = jnp.where(even, b, a)
    south = jnp.where(even, a, b)
    return jnp.concatenate([north, fld_ref[...], south], axis=0)


def edge_kernel(pos_ref, fld_ref, a_ref, b_ref, edge_ref):
    even = pos_ref[0] % 2 == 0
    whole = tall(fld_ref, a_ref[...], b_ref[...], even)
    rank = lax.broadcasted_iota(jnp.int32, (16, COLS), 0)
    col = lax.broadcasted_iota(jnp.int32, (16, COLS), 1)
    pick = ((rank < 2) & (col == rank)) | ((rank >= 2) & (rank < 4) & (col == COLS - 4 + rank))
    pick = jnp.where(pick, 1.0, 0.0).astype(BF)
    edge_ref[...] = lax.dot_general(
        pick, whole, (((1,), (1,)), ((), ())), preferred_element_type=F32
    ).astype(BF)


def edges(pos, fld, a, b):
    return pl.pallas_call(
        edge_kernel,
        in_specs=[SM, VM, VM, VM],
        out_specs=VM,
        out_shape=jax.ShapeDtypeStruct((16, (ROWS + 4) * 8), BF),
        compiler_params=params(8),
        cost_estimate=cost(0, 1 << 20),
        name="edges",
    )(pos, fld, a, b)


def build(pos_ref, fld_ref, a_ref, b_ref, core_ref, x_ref, g):
    whole = tall(fld_ref, a_ref[...], b_ref[...], pos_ref[0] % 2 == 0)
    even = pos_ref[1] % 2 == 0
    core, x = core_ref[...].astype(F32), x_ref[...].astype(F32)
    right, left = jnp.where(even, core, x), jnp.where(even, x, core)
    c = lax.broadcasted_iota(jnp.int32, (256, 256), 0)
    lane = lax.broadcasted_iota(jnp.int32, (256, 256), 1)
    j, d = lane % 128, lane // 128
    hr = lax.broadcasted_iota(jnp.int32, (16, 256), 0)
    hl = lax.broadcasted_iota(jnp.int32, (16, 256), 1)

    def halo(side, base):
        hot = ((hl % 128) == 0) & (hr == hl // 128 + base)
        return lax.dot_general(
            side.astype(BF),
            jnp.where(hot, 1.0, 0.0).astype(BF),
            (((0,), (0,)), ((), ())),
            preferred_element_type=F32,
        )

    def moved(half, shift):
        hot = jnp.where(c == 2 * j + d + shift, 1.0, 0.0).astype(BF)
        return jnp.dot(whole[:, half * 256 : half * 256 + 256], hot, preferred_element_type=F32)

    tiles = {
        (0, 0): moved(0, -2) + halo(left, 2),
        (0, 1): moved(0, 254) + moved(1, -2),
        (0, 2): moved(1, 254),
        (1, 0): moved(0, 0),
        (1, 1): moved(1, 0),
        (1, 2): halo(right, 0),
    }
    for (pair, tile), value in tiles.items():
        value = value.astype(BF)
        for half in range(2):
            d0 = (2 * pair + half) * 64
            part = value[:, half * 128 : half * 128 + 128]
            for m in range(BLOCKS):
                g[m, d0 : d0 + 64, tile * 128 : tile * 128 + 128] = part[48 * m : 48 * m + 64]


def conv_kernel(
    last,
    pos_ref,
    fld_ref,
    a_ref,
    b_ref,
    core_ref,
    x_ref,
    ws_ref,
    bs_ref,
    wm_ref,
    bm_ref,
    out_ref,
    g,
    hs,
    vs,
    ys,
    yb,
    sem,
):
    s = pl.program_id(0)

    @pl.when(s == 0)
    def _():
        build(pos_ref, fld_ref, a_ref, b_ref, core_ref, x_ref, g)

    band = pos_ref[0]
    keep_first = jnp.where((s == 0) & (band == 0), 0.0, 1.0)
    keep_last = jnp.where((s == BLOCKS - 1) & (band == last), 0.0, 1.0)
    x = g[s][:, :HROWS]
    for i in range(STEP):
        t = lax.dot_general(
            x,
            ws_ref[:, i * 256 : i * 256 + 256],
            (((0,), (0,)), ((), ())),
            preferred_element_type=F32,
        )
        t = t + bs_ref[...]
        h = t + t * jnp.tanh(t)
        if i == 0:
            h = h * keep_first
        if i == STEP - 1:
            h = h * keep_last
        hs[6 * s + 2 + i, 0] = h[:, :128]
        hs[6 * s + 2 + i, 1] = h[:, 128:]
    parts = [(0, 0), (1, 0), (0, 1), (1, 1)]
    for r in range(STEP + 2):
        for k, (par, shift) in enumerate(parts):
            vs[r, :, k * 128 : k * 128 + 128] = hs[6 * s + r, par, shift : shift + PAIRS, :].astype(BF)
    slot = s % 2

    def copy(at, slot):
        return pltpu.make_async_copy(
            yb.at[slot], out_ref.at[pl.ds(6 * at - 2, 6)], sem.at[slot]
        )

    first = pltpu.make_async_copy(yb.at[0, pl.ds(2, 4)], out_ref.at[pl.ds(0, 4)], sem.at[0])

    @pl.when(s == 2)
    def _():
        first.wait()

    @pl.when(s > 2)
    def _():
        copy(s - 2, slot).wait()

    for h in range(STEP):
        lhs = jnp.concatenate([vs[h + a] for a in range(3)], axis=1)
        y = jnp.dot(lhs, wm_ref[...].reshape(1536, 256), preferred_element_type=F32)
        for par in range(2):
            ys[h, pl.ds(par, PAIRS, stride=2), :] = y[:, par * 128 : par * 128 + 128] + bm_ref[...]
        yb[slot, h] = ys[h].astype(BF)

    @pl.when(s == 0)
    def _():
        first.start()

    @pl.when(s > 0)
    def _():
        copy(s, slot).start()

    @pl.when(s == BLOCKS - 1)
    def _():
        copy(s - 1, 1 - slot).wait()
        copy(s, slot).wait()


def conv(n_band, pos, fld, a, b, core, x, ws, bs, wm, bm):
    channels = bm.shape[-1]
    return pl.pallas_call(
        functools.partial(conv_kernel, n_band - 1),
        grid=(BLOCKS,),
        in_specs=[SM] + [VM] * 9,
        out_specs=ANY,
        out_shape=jax.ShapeDtypeStruct((ROWS, COLS, channels), BF),
        scratch_shapes=[
            pltpu.VMEM((BLOCKS, 256, LANES), BF),
            pltpu.VMEM((ROWS + 4, 2, HROWS, 128), F32),
            pltpu.VMEM((STEP + 2, PAIRS, 512), BF),
            pltpu.VMEM((STEP, COLS, channels), F32),
            pltpu.VMEM((2, STEP, COLS, channels), BF),
            pltpu.SemaphoreType.DMA((2,)),
        ],
        compiler_params=params(56),
        cost_estimate=cost(2 * ROWS * COLS * 9 * 128 * 128, 12 << 20),
        name="conv",
    )(pos, fld, a, b, core, x, ws, bs, wm, bm)


def on_device(source, routes, slot_weights, window, stem_weight, stem_bias, mix_weight, mix_bias):
    n_band = lax.axis_size("band")
    n_lon = lax.axis_size("lon")
    axes = ("band", "lon")
    band = lax.axis_index("band")
    lon = lax.axis_index("lon")

    def move(value, pairs):
        return lax.ppermute(value, axes, pairs)

    pos = jnp.stack([band, lon]).astype(jnp.int32)
    core_dl = jnp.where(lon % 2 == 0, 3, 1)
    x_dl = 4 - core_dl
    a_base = jnp.where(band % 2 == 0, 0, 8)
    b_base = 8 - a_base
    rim = (band == 0) | (band == n_band - 1)
    far_code = jnp.where(band < n_band // 2, 10, 2)
    near_codes = jnp.stack([4 + 0 * lon, 4 + core_dl, 4 + x_dl]).astype(jnp.int32)
    far_codes = jnp.stack(
        [
            a_base,
            a_base + core_dl,
            a_base + x_dl,
            jnp.where(rim, 6, b_base),
            b_base + core_dl,
            b_base + x_dl,
            far_code,
        ]
    ).astype(jnp.int32)

    own, to_core, to_x, to_far = pack(pos, routes.T, source)
    core = move(to_core, swap_core(n_band, n_lon))
    x = move(to_x, swap_x(n_band, n_lon))
    far = move(to_far, swap_far(n_band, n_lon))
    a_out = jnp.concatenate([own[0:32], core[0:32], x[0:32]], axis=0)
    b_out = jnp.concatenate([own[64:96], core[64:96], x[64:96]], axis=0)
    a_in = move(a_out, swap_a(n_band, n_lon))
    b_in = move(b_out, swap_b(n_band, n_lon, True))
    ws, wm = prep(stem_weight, mix_weight)
    win = window[0]
    near = contrib(True, near_codes, win, [own, core, x], [(1,)] * 3, slot_weights)
    fld, a_row, b_row = contrib(
        False,
        far_codes,
        win,
        [a_in, b_in, far],
        [(0, 1, 2), (0, 1, 2), (0,)],
        slot_weights,
        (near, pos),
    )
    a_halo = move(a_row, swap_a(n_band, n_lon))
    b_halo = move(b_row, swap_b(n_band, n_lon, False))
    edge = edges(pos, fld, a_halo, b_halo)
    core_edge = move(edge, swap_core(n_band, n_lon))
    x_edge = move(edge, swap_x(n_band, n_lon))
    bs = SCALE * jnp.concatenate([stem_bias, stem_bias])[None]
    return conv(n_band, pos, fld, a_halo, b_halo, core_edge, x_edge, ws, bs, wm, mix_bias[None])


def solution(mesh):
    both = ("band", "lon")
    in_specs = (
        P(both, None, None),
        P(both, None),
        P(both, None, None, None, None),
        P(both, None, None),
        P(),
        P(),
        P(),
        P(),
    )
    return jax.shard_map(
        on_device, mesh=mesh, in_specs=in_specs, out_specs=P("band", "lon", None), check_vma=False
    )
```

time: 151 us -> 73.6 us (0.49)
  the two profiles are of different devices: /device:TPU:0 before, /device:TPU:5 now
where the time goes in v1:
time: 73.6 us; the launch traced here: 73.3 us
  Pallas kernels  38.1 us (52%)
  starting transfers between devices  13.4 us (18%)
  local copies, waits for them, and re-layouts  11.9 us (16%)
  waiting for transfers between devices  8.83 us (12%)
  other arithmetic  0.79 us (1%)
    pallas_call x1, Pallas kernels, conv(): pl.pallas_call(functools.partial(conv_kernel, n_band - 1), grid=(BLOCKS,)...  28.8 us
    ppermute x9, starting transfers between devices, move(): return lax.ppermute(value, axes, pairs)  13.4 us
    unnamed x31, local copies, waits for them, and re-layouts  11.8 us
    ppermute x9, waiting for transfers between devices, move(): return lax.ppermute(value, axes, pairs)  8.83 us
    pallas_call x2, Pallas kernels, contrib(): pl.pallas_call(functools.partial(contrib_kernel, pieces, first), grid_spe...  6.47 us
    pallas_call x1, Pallas kernels, pack(): pl.pallas_call(pack_kernel, in_specs=[SM, SM, VM], out_specs=[VM] * 4, ou...  1.82 us
  transfers between devices with their start and end apart: 9, of which 2 were waited for; matrix products, arithmetic and copies ran while one was open for 2% of the time, Pallas kernels for 3%

profile of v1, /device:TPU:5, one launch (start us, length us, event | category | flops | bytes accessed | tf_op | source)
XLA Modules:
  0.0 73.3 jit_solution(9650093764149405085)
XLA Ops:
  0.1 0.9 %copy-done.4 = bf16[128,8,128]{2,1,0:T(8,128)(2,1)S(1)} copy-done((bf16[128,8,128]{2,1,0:T(8,128)(2,1)S(1)}, bf16[128,8,128]{2,1,0:T(8,128)(2,1)}, u32[]{:S(2)}) %copy-start.4) | copy-done | bytes 262168
  1.0 0.7 copy-done.9
  1.7 1.8 %pack.1 = (bf16[96,8,128]{2,1,0:T(8,128)(2,1)S(1)}, bf16[96,8,128]{2,1,0:T(8,128)(2,1)S(1)}, bf16[96,8,128]{2,1,0:T(8,128)(2,1)S(1)}, bf16[32,8,128]{2,1,0:T(8,128)(2,1)S(1)}) custom-call(s32[2]{0:T(128)S(1)} %pad_add_fusion.pos_ref.refs_5_, s32[2,128]{1,0:T(2,128)S(1)} %bitcast.19, bf16[128,8,128]{2,1,0:T(8,128)(2,1)S(1)} %copy-done.4), custom_call_target="tpu_custom_call" | custom-call | bytes 1048576 | tf_op jit(solution)/shard_map/pack/pallas_call | solution.py:104
  3.5 0.7 %collective-permute-start = (bf16[96,8,128]{2,1,0:T(8,128)(2,1)S(1)}, bf16[96,8,128]{2,1,0:T(8,128)(2,1)S(1)}, u32[]{:S(2)}, u32[]{:S(2)}) collective-permute-start(bf16[96,8,128]{2,1,0:T(8,128)(2,1)S(1)} %get-tuple-element.15), channel_id=1, source_target_pairs={{0,1},{1,0},{2,3},{3,2},{4,5},{5,4},{6,7},{7,6},{8,9},{9,8},{10,11... | collective-permute-start | bytes 589832 | tf_op jit(solution)/shard_map/ppermute | solution.py:425
  4.3 1.2 %collective-permute-start.1 = (bf16[96,8,128]{2,1,0:T(8,128)(2,1)S(1)}, bf16[96,8,128]{2,1,0:T(8,128)(2,1)S(1)}, u32[]{:S(2)}, u32[]{:S(2)}) collective-permute-start(bf16[96,8,128]{2,1,0:T(8,128)(2,1)S(1)} %get-tuple-element.16), channel_id=1, source_target_pairs={{0,3},{1,2},{2,1},{3,0},{4,7},{5,6},{6,5},{7,4},{8,11},{9,10},{10,... | collective-permute-start | bytes 589832 | tf_op jit(solution)/shard_map/ppermute | solution.py:425
  5.5 5.4 %collective-permute-done.1.refs_2_ = bf16[96,8,128]{2,1,0:T(8,128)(2,1)S(1)} collective-permute-done((bf16[96,8,128]{2,1,0:T(8,128)(2,1)S(1)}, bf16[96,8,128]{2,1,0:T(8,128)(2,1)S(1)}, u32[]{:S(2)}, u32[]{:S(2)}) %collective-permute-start.1) | collective-permute-done | bytes 196640 | tf_op jit(solution)/shard_map/ppermute | solution.py:425
  11.1 2.5 %collective-permute-start.3 = (bf16[96,8,128]{2,1,0:T(8,128)(2,1)S(1)}, bf16[96,8,128]{2,1,0:T(8,128)(2,1)S(1)}, u32[]{:S(2)}, u32[]{:S(2)}) collective-permute-start(bf16[96,8,128]{2,1,0:T(8,128)(2,1)S(1)} %pad_maximum_fusion.1), channel_id=1, source_target_pairs={{0,2},{1,3},{2,0},{3,1},{4,8},{5,9},{6,10},{7,11},{8,4},{9,5},{10,... | collective-permute-start | bytes 589832 | tf_op jit(solution)/shard_map/ppermute | solution.py:425
  13.6 2.1 %collective-permute-start.4 = (bf16[32,8,128]{2,1,0:T(8,128)(2,1)S(1)}, bf16[32,8,128]{2,1,0:T(8,128)(2,1)S(1)}, u32[]{:S(2)}, u32[]{:S(2)}) collective-permute-start(bf16[32,8,128]{2,1,0:T(8,128)(2,1)S(1)} %get-tuple-element.17), channel_id=1, source_target_pairs={{0,6},{1,7},{2,4},{3,5},{4,2},{5,3},{6,0},{7,1},{28,26},{29,27},{3... | collective-permute-start | bytes 196616 | tf_op jit(solution)/shard_map/ppermute | solution.py:425
  15.7 0.7 copy.11
  16.5 4.6 %copy-done = bf16[1,12,32,128,128]{4,3,2,1,0:T(8,128)(2,1)S(1)} copy-done((bf16[1,12,32,128,128]{4,3,2,1,0:T(8,128)(2,1)S(1)}, bf16[1,12,32,128,128]{4,3,2,1,0:T(8,128)(2,1)}, u32[]{:S(2)}) %copy-start) | copy-done | bytes 12582936
  21.1 2.1 %contrib_near.1.refs_4_ = f32[256,8,128]{2,1,0:T(8,128)S(1)} custom-call(s32[3]{0:T(128)S(1)} %pad_add_fusion.1.codes_ref, s32[12,32]{1,0:T(8,128)S(1)} %bitcast.17, bf16[96,8,128]{2,1,0:T(8,128)(2,1)S(1)} %get-tuple-element.14.refs_0_, bf16[96,8,128]{2,1,0:T(8,128)(2,1)S(1)} %collective-permute-done.refs_1_, ...), custom_call_target="tpu_custom_call" | custom-call | flops 25165824 | bytes 3145728 | tf_op jit(solution)/shard_map/contrib_near/pallas_call | solution.py:227
  23.2 2.5 %copy-done.1 = bf16[1,12,32,128,128]{4,3,2,1,0:T(8,128)(2,1)S(1)} copy-done((bf16[1,12,32,128,128]{4,3,2,1,0:T(8,128)(2,1)S(1)}, bf16[1,12,32,128,128]{4,3,2,1,0:T(8,128)(2,1)}, u32[]{:S(2)}) %copy-start.1) | copy-done | bytes 12582936
  25.7 4.4 %contrib_far.1 = (bf16[512,512]{1,0:T(8,128)(2,1)S(1)}, bf16[16,512]{1,0:T(8,128)(2,1)S(1)}, bf16[16,512]{1,0:T(8,128)(2,1)S(1)}) custom-call(s32[7]{0:T(128)S(1)} %stack.52.codes_ref, s32[12,32]{1,0:T(8,128)S(1)} %bitcast.18, bf16[96,8,128]{2,1,0:T(8,128)(2,1)S(1)} %collective-permute-done.2.refs_0_, ...), custom_call_target="tpu_custom_call" | custom-call | flops 58720256 | bytes 7340032 | tf_op jit(solution)/shard_map/contrib_far/pallas_call | solution.py:227
  30.1 2.3 %collective-permute-start.5 = (bf16[16,512]{1,0:T(8,128)(2,1)S(1)}, bf16[16,512]{1,0:T(8,128)(2,1)S(1)}, u32[]{:S(2)}, u32[]{:S(2)}) collective-permute-start(bf16[16,512]{1,0:T(8,128)(2,1)S(1)} %get-tuple-element.19), channel_id=1, source_target_pairs={{0,4},{1,5},{2,6},{3,7},{4,0},{5,1},{6,2},{7,3},{8,12},{9,13},{10,... | collective-permute-start | bytes 49160 | tf_op jit(solution)/shard_map/ppermute | solution.py:425
  32.4 1.9 %collective-permute-start.6 = (bf16[16,512]{1,0:T(8,128)(2,1)S(1)}, bf16[16,512]{1,0:T(8,128)(2,1)S(1)}, u32[]{:S(2)}, u32[]{:S(2)}) collective-permute-start(bf16[16,512]{1,0:T(8,128)(2,1)S(1)} %get-tuple-element.20), channel_id=1, source_target_pairs={{4,8},{5,9},{6,10},{7,11},{8,4},{9,5},{10,6},{11,7},{12,16},{13,17... | collective-permute-start | bytes 49160 | tf_op jit(solution)/shard_map/ppermute | solution.py:425
  34.3 3.4 %collective-permute-done.6.b_ref = bf16[16,512]{1,0:T(8,128)(2,1)S(1)} collective-permute-done((bf16[16,512]{1,0:T(8,128)(2,1)S(1)}, bf16[16,512]{1,0:T(8,128)(2,1)S(1)}, u32[]{:S(2)}, u32[]{:S(2)}) %collective-permute-start.6) | collective-permute-done | bytes 16416 | tf_op jit(solution)/shard_map/ppermute | solution.py:425
  37.8 0.8 %edges.1 = bf16[16,544]{1,0:T(8,128)(2,1)S(1)} custom-call(s32[2]{0:T(128)S(1)} %pad_add_fusion.pos_ref.refs_5_, bf16[512,512]{1,0:T(8,128)(2,1)S(1)} %get-tuple-element.18.fld_ref, bf16[16,512]{1,0:T(8,128)(2,1)S(1)} %collective-permute-done.5.a_ref, bf16[16,512]{1,0:T(8,128)(2,1)S(1)} %collective-permute-done.6.b_ref), custom_call_target="tpu_custom_call" | custom-call | bytes 1048576 | tf_op jit(solution)/shard_map/edges/pallas_call | solution.py:256
  38.6 2.6 %collective-permute-start.8 = (bf16[16,544]{1,0:T(8,128)(2,1)S(1)}, bf16[16,544]{1,0:T(8,128)(2,1)S(1)}, u32[]{:S(2)}, u32[]{:S(2)}) collective-permute-start(bf16[16,544]{1,0:T(8,128)(2,1)S(1)} %edges.1), channel_id=1, source_target_pairs={{0,3},{1,2},{2,1},{3,0},{4,7},{5,6},{6,5},{7,4},{8,11},{9,10},{10,... | collective-permute-start | bytes 52232 | tf_op jit(solution)/shard_map/ppermute | solution.py:425
  41.2 0.6 maximum_multiply_fusion.bs_ref
  41.8 0.2 prep.1
  42.1 0.9 %copy-done.10 = bf16[256,1536]{1,0:T(8,128)(2,1)} copy-done((bf16[256,1536]{1,0:T(8,128)(2,1)}, bf16[256,1536]{1,0:T(8,128)(2,1)S(1)}, u32[]{:S(2)}) %copy-start.10) | copy-done | bytes 786456
  42.9 0.9 %copy-done.11 = bf16[3,512,256]{2,1,0:T(8,128)(2,1)} copy-done((bf16[3,512,256]{2,1,0:T(8,128)(2,1)}, bf16[3,512,256]{2,1,0:T(8,128)(2,1)S(1)}, u32[]{:S(2)}) %copy-start.11) | copy-done | bytes 786456
  43.9 0.6 copy-done.12
  44.5 28.8 %conv.1 = bf16[64,512,128]{2,1,0:T(8,128)(2,1)} custom-call(s32[2]{0:T(128)} %copy-done.8, bf16[512,512]{1,0:T(8,128)(2,1)} %copy-done.2, bf16[16,512]{1,0:T(8,128)(2,1)} %copy-done.6, bf16[16,512]{1,0:T(8,128)(2,1)} %copy-done.7, bf16[16,544]{1,0:T(8,128)(2,1)} %copy-done.13, bf16[16,544]{1,0:T(8,128)(2,1)} %copy-done.12, bf16[256,1536]{1,0:T(8,128)(2,1)} %copy-done.10, ...), custom_call_target="tpu_custom_call" | custom-call | flops 9663676416 | bytes 12582912 | tf_op jit(solution)/shard_map/conv/pallas_call | solution.py:397
  (40 shorter events, 0.5 us)
Async XLA Ops:
  0.1 37.7 %copy-start.8 = (s32[2]{0:T(128)}, s32[2]{0:T(128)S(1)}, u32[]{:S(2)}) copy-start(s32[2]{0:T(128)S(1)} %pad_add_fusion.pos_ref.refs_5_) | copy-start | bytes 28
  0.1 1.0 %copy-start.4 = (bf16[128,8,128]{2,1,0:T(8,128)(2,1)S(1)}, bf16[128,8,128]{2,1,0:T(8,128)(2,1)}, u32[]{:S(2)}) copy-start(bf16[128,8,128]{2,1,0:T(8,128)(2,1)} %src_ref.1) | copy-start | bytes 786436
  1.0 0.7 copy-start.9
  3.5 1.9 %collective-permute-start = (bf16[96,8,128]{2,1,0:T(8,128)(2,1)S(1)}, bf16[96,8,128]{2,1,0:T(8,128)(2,1)S(1)}, u32[]{:S(2)}, u32[]{:S(2)}) collective-permute-start(bf16[96,8,128]{2,1,0:T(8,128)(2,1)S(1)} %get-tuple-element.15), channel_id=1, source_target_pairs={{0,1},{1,0},{2,3},{3,2},{4,5},{5,4},{6,7},{7,6},{8,9},{9,8},{10,11... | collective-permute-start | bytes 589832 | tf_op jit(solution)/shard_map/ppermute | solution.py:425
  4.3 6.6 %collective-permute-start.1 = (bf16[96,8,128]{2,1,0:T(8,128)(2,1)S(1)}, bf16[96,8,128]{2,1,0:T(8,128)(2,1)S(1)}, u32[]{:S(2)}, u32[]{:S(2)}) collective-permute-start(bf16[96,8,128]{2,1,0:T(8,128)(2,1)S(1)} %get-tuple-element.16), channel_id=1, source_target_pairs={{0,3},{1,2},{2,1},{3,0},{4,7},{5,6},{6,5},{7,4},{8,11},{9,10},{10,... | collective-permute-start | bytes 589832 | tf_op jit(solution)/shard_map/ppermute | solution.py:425
  10.9 12.3 %collective-permute-start.2 = (bf16[96,8,128]{2,1,0:T(8,128)(2,1)S(1)}, bf16[96,8,128]{2,1,0:T(8,128)(2,1)S(1)}, u32[]{:S(2)}, u32[]{:S(2)}) collective-permute-start(bf16[96,8,128]{2,1,0:T(8,128)(2,1)S(1)} %pad_maximum_fusion), channel_id=1, source_target_pairs={{0,4},{1,5},{2,6},{3,7},{4,0},{5,1},{6,2},{7,3},{8,12},{9,13},{10,... | collective-permute-start | bytes 589832 | tf_op jit(solution)/shard_map/ppermute | solution.py:425
  11.1 12.2 %collective-permute-start.3 = (bf16[96,8,128]{2,1,0:T(8,128)(2,1)S(1)}, bf16[96,8,128]{2,1,0:T(8,128)(2,1)S(1)}, u32[]{:S(2)}, u32[]{:S(2)}) collective-permute-start(bf16[96,8,128]{2,1,0:T(8,128)(2,1)S(1)} %pad_maximum_fusion.1), channel_id=1, source_target_pairs={{0,2},{1,3},{2,0},{3,1},{4,8},{5,9},{6,10},{7,11},{8,4},{9,5},{10,... | collective-permute-start | bytes 589832 | tf_op jit(solution)/shard_map/ppermute | solution.py:425
  13.6 9.6 %collective-permute-start.4 = (bf16[32,8,128]{2,1,0:T(8,128)(2,1)S(1)}, bf16[32,8,128]{2,1,0:T(8,128)(2,1)S(1)}, u32[]{:S(2)}, u32[]{:S(2)}) collective-permute-start(bf16[32,8,128]{2,1,0:T(8,128)(2,1)S(1)} %get-tuple-element.17), channel_id=1, source_target_pairs={{0,6},{1,7},{2,4},{3,5},{4,2},{5,3},{6,0},{7,1},{28,26},{29,27},{3... | collective-permute-start | bytes 196616 | tf_op jit(solution)/shard_map/ppermute | solution.py:425
  16.5 4.6 %copy-start = (bf16[1,12,32,128,128]{4,3,2,1,0:T(8,128)(2,1)S(1)}, bf16[1,12,32,128,128]{4,3,2,1,0:T(8,128)(2,1)}, u32[]{:S(2)}) copy-start(bf16[1,12,32,128,128]{4,3,2,1,0:T(8,128)(2,1)} %refs_3_.3) | copy-start | bytes 37748740
  21.1 4.6 %copy-start.1 = (bf16[1,12,32,128,128]{4,3,2,1,0:T(8,128)(2,1)S(1)}, bf16[1,12,32,128,128]{4,3,2,1,0:T(8,128)(2,1)}, u32[]{:S(2)}) copy-start(bf16[1,12,32,128,128]{4,3,2,1,0:T(8,128)(2,1)} %refs_3_.3) | copy-start | bytes 37748740
  21.1 20.1 %copy-start.14 = (f32[128]{0:T(128)S(1)}, f32[128]{0:T(128)}, u32[]{:S(2)}) copy-start(f32[128]{0:T(128)} %param.13) | copy-start | bytes 1540
  21.1 20.7 %copy-start.3 = (bf16[9,128,128]{2,1,0:T(8,128)(2,1)S(1)}, bf16[9,128,128]{2,1,0:T(8,128)(2,1)}, u32[]{:S(2)}) copy-start(bf16[9,128,128]{2,1,0:T(8,128)(2,1)} %mix_ref.1) | copy-start | bytes 884740
  21.1 20.7 %copy-start.5 = (bf16[9,8,128]{2,1,0:T(8,128)(2,1)S(1)}, bf16[9,8,128]{2,1,0:T(8,128)(2,1)}, u32[]{:S(2)}) copy-start(bf16[9,8,128]{2,1,0:T(8,128)(2,1)} %stem_ref.1) | copy-start | bytes 55300
  30.1 13.8 %copy-start.2 = (bf16[512,512]{1,0:T(8,128)(2,1)}, bf16[512,512]{1,0:T(8,128)(2,1)S(1)}, u32[]{:S(2)}) copy-start(bf16[512,512]{1,0:T(8,128)(2,1)S(1)} %get-tuple-element.18.fld_ref) | copy-start | bytes 1572868
  30.1 4.2 %collective-permute-start.5 = (bf16[16,512]{1,0:T(8,128)(2,1)S(1)}, bf16[16,512]{1,0:T(8,128)(2,1)S(1)}, u32[]{:S(2)}, u32[]{:S(2)}) collective-permute-start(bf16[16,512]{1,0:T(8,128)(2,1)S(1)} %get-tuple-element.19), channel_id=1, source_target_pairs={{0,4},{1,5},{2,6},{3,7},{4,0},{5,1},{6,2},{7,3},{8,12},{9,13},{10,... | collective-permute-start | bytes 49160 | tf_op jit(solution)/shard_map/ppermute | solution.py:425
  32.4 5.4 %collective-permute-start.6 = (bf16[16,512]{1,0:T(8,128)(2,1)S(1)}, bf16[16,512]{1,0:T(8,128)(2,1)S(1)}, u32[]{:S(2)}, u32[]{:S(2)}) collective-permute-start(bf16[16,512]{1,0:T(8,128)(2,1)S(1)} %get-tuple-element.20), channel_id=1, source_target_pairs={{4,8},{5,9},{6,10},{7,11},{8,4},{9,5},{10,6},{11,7},{12,16},{13,17... | collective-permute-start | bytes 49160 | tf_op jit(solution)/shard_map/ppermute | solution.py:425
  34.3 9.6 %copy-start.6 = (bf16[16,512]{1,0:T(8,128)(2,1)}, bf16[16,512]{1,0:T(8,128)(2,1)S(1)}, u32[]{:S(2)}) copy-start(bf16[16,512]{1,0:T(8,128)(2,1)S(1)} %collective-permute-done.5.a_ref) | copy-start | bytes 49156
  37.8 6.1 %copy-start.7 = (bf16[16,512]{1,0:T(8,128)(2,1)}, bf16[16,512]{1,0:T(8,128)(2,1)S(1)}, u32[]{:S(2)}) copy-start(bf16[16,512]{1,0:T(8,128)(2,1)S(1)} %collective-permute-done.6.b_ref) | copy-start | bytes 49156
  38.6 5.3 %collective-permute-start.8 = (bf16[16,544]{1,0:T(8,128)(2,1)S(1)}, bf16[16,544]{1,0:T(8,128)(2,1)S(1)}, u32[]{:S(2)}, u32[]{:S(2)}) collective-permute-start(bf16[16,544]{1,0:T(8,128)(2,1)S(1)} %edges.1), channel_id=1, source_target_pairs={{0,3},{1,2},{2,1},{3,0},{4,7},{5,6},{6,5},{7,4},{8,11},{9,10},{10,... | collective-permute-start | bytes 52232 | tf_op jit(solution)/shard_map/ppermute | solution.py:425
  41.2 2.7 %collective-permute-start.7 = (bf16[16,544]{1,0:T(8,128)(2,1)S(1)}, bf16[16,544]{1,0:T(8,128)(2,1)S(1)}, u32[]{:S(2)}, u32[]{:S(2)}) collective-permute-start(bf16[16,544]{1,0:T(8,128)(2,1)S(1)} %edges.1), channel_id=1, source_target_pairs={{0,1},{1,0},{2,3},{3,2},{4,5},{5,4},{6,7},{7,6},{8,9},{9,8},{10,11... | collective-permute-start | bytes 52232 | tf_op jit(solution)/shard_map/ppermute | solution.py:425
  42.0 0.9 %copy-start.10 = (bf16[256,1536]{1,0:T(8,128)(2,1)}, bf16[256,1536]{1,0:T(8,128)(2,1)S(1)}, u32[]{:S(2)}) copy-start(bf16[256,1536]{1,0:T(8,128)(2,1)S(1)} %get-tuple-element.21.ws_ref) | copy-start | bytes 2359300
  42.9 0.9 %copy-start.11 = (bf16[3,512,256]{2,1,0:T(8,128)(2,1)}, bf16[3,512,256]{2,1,0:T(8,128)(2,1)S(1)}, u32[]{:S(2)}) copy-start(bf16[3,512,256]{2,1,0:T(8,128)(2,1)S(1)} %get-tuple-element.22.wm_ref) | copy-start | bytes 2359300
  43.9 0.6 copy-start.12
  43.9 0.6 copy-start.13

commit v2 on v1

v2 whole, which is shorter than its diff:
```python
import functools

import jax
import jax.numpy as jnp
from jax import lax
from jax.experimental import pallas as pl
from jax.experimental.pallas import tpu as pltpu
from jax.sharding import PartitionSpec as P

ROWS = 64
COLS = 512
PAIRS = COLS // 2
SUB = 16
HROWS = PAIRS + SUB
PITCH = 2 * SUB + 1
LANES = 384
CHUNK = 256
STEP = 6
BLOCKS = (ROWS + 2) // STEP
SCALE = 1.0 / 2.0
BF = jnp.bfloat16
F32 = jnp.float32
VM = pl.BlockSpec(memory_space=pltpu.VMEM)
SM = pl.BlockSpec(memory_space=pltpu.SMEM)
ANY = pl.BlockSpec(memory_space=pl.ANY)
HBM = pl.BlockSpec(memory_space=pltpu.HBM)


def params(mib):
    return pltpu.CompilerParams(vmem_limit_bytes=mib << 20)


def cost(flops, size):
    return pl.CostEstimate(flops=flops, bytes_accessed=size, transcendentals=0)


def swap_core(n_band, n_lon):
    return [(b * n_lon + l, b * n_lon + (l ^ 1)) for b in range(n_band) for l in range(n_lon)]


def swap_x(n_band, n_lon):
    return [(b * n_lon + l, b * n_lon + n_lon - 1 - l) for b in range(n_band) for l in range(n_lon)]


def swap_a(n_band, n_lon):
    return [(b * n_lon + l, (b ^ 1) * n_lon + l) for b in range(n_band) for l in range(n_lon)]


def swap_b(n_band, n_lon):
    pairs = []
    for b in range(n_band):
        partner = b + 1 if b % 2 else b - 1
        for l in range(n_lon):
            if 0 <= partner < n_band:
                pairs.append((b * n_lon + l, partner * n_lon + l))
            else:
                pairs.append((b * n_lon + l, b * n_lon + (l + 2) % n_lon))
    return pairs


def swap_diagonal(n_band, n_lon):
    return [
        (b * n_lon + l, (b ^ 1) * n_lon + (l + 2) % n_lon) for b in range(n_band) for l in range(n_lon)
    ]


def in_hbm(*arrays):
    return [pltpu.with_memory_space_constraint(a, pltpu.HBM) for a in arrays]


def pack_kernel(
    pos_ref, routes_hbm, src_hbm, own_ref, core_ref, x_ref, far_ref, routes_ref, src_ref, buf, table, count, sem
):
    copies = [
        pltpu.make_async_copy(routes_hbm, routes_ref, sem.at[0]),
        pltpu.make_async_copy(src_hbm, src_ref, sem.at[1]),
    ]
    for copy in copies:
        copy.start()
    band = pos_ref[0]
    lon = pos_ref[1]
    a_dir = 1 - 2 * (band % 2)
    core_dl = 1 + 2 * (lon % 2)
    for q in range(12):
        db, dl = q // 4 - 1, q % 4
        if db == 0:
            way = 1
        else:
            way = jnp.where(a_dir == db, 0, 2)
        if dl == 0:
            group = way
        elif dl == 2:
            group = 2 if db == 0 else 9
        else:
            group = jnp.where(core_dl == dl, 3, 6) + way
        table[q] = group * 32
        count[q] = 0
    buf[...] = jnp.zeros_like(buf)
    for copy in copies:
        copy.wait()

    def one(j, carry):
        block = src_ref[j]
        for t in range(2):
            q = routes_ref[t, j]
            rank = count[q]
            count[q] = rank + 1
            buf[table[q] + rank] = block
        return carry

    lax.fori_loop(0, src_ref.shape[0], one, 0, unroll=8)
    own_ref[...] = buf[0:96]
    core_ref[...] = buf[96:192]
    x_ref[...] = buf[192:288]
    far_ref[...] = buf[288:320]


def pack(pos, routes, source):
    fields, cells = source.shape[1:]
    shape = lambda n: jax.ShapeDtypeStruct((n, fields, cells), BF)
    return pl.pallas_call(
        pack_kernel,
        in_specs=[SM, HBM, HBM],
        out_specs=[VM] * 4,
        out_shape=[shape(96), shape(96), shape(96), shape(32)],
        scratch_shapes=[
            pltpu.SMEM(routes.shape, jnp.int32),
            pltpu.VMEM(source.shape, BF),
            pltpu.VMEM((320, fields, cells), BF),
            pltpu.SMEM((12,), jnp.int32),
            pltpu.SMEM((12,), jnp.int32),
            pltpu.SemaphoreType.DMA((2,)),
        ],
        compiler_params=params(16),
        cost_estimate=cost(0, 1 << 20),
        name="pack",
    )(pos, *in_hbm(routes, source))


def prep_kernel(stem_ref, bias_ref, mix_ref, ws_ref, bs_ref, wm_ref, hot_ref):
    for par in range(2):
        bs_ref[:, par * 128 : par * 128 + 128] = bias_ref[...] * SCALE
    c = lax.broadcasted_iota(jnp.int32, (COLS, 256), 0)
    lane = lax.broadcasted_iota(jnp.int32, (COLS, 256), 1)
    for tile in range(3):
        n = lane % 128 + tile * 128
        j = jnp.where(n < PAIRS, SUB * (n % SUB) + n // SUB, SUB * (n - PAIRS + 1))
        gap = jnp.where(n < HROWS, c - 2 * j - lane // 128, -COLS)
        for pair in range(2):
            hot = jnp.where(gap == 2 * pair - 2, 1.0, 0.0)
            hot_ref[:, (2 * tile + pair) * 256 : (2 * tile + pair) * 256 + 256] = hot.astype(BF)
    zero8 = jnp.zeros((8, 128), F32)
    taps = [stem_ref[t].astype(F32) * SCALE for t in range(9)]
    for i in range(STEP):
        for par in range(2):
            rows = []
            for d in range(4):
                for row in range(8):
                    a, b = row - i, d - par
                    rows.append(taps[3 * a + b] if 0 <= a < 3 and 0 <= b < 3 else zero8)
            lane = (2 * i + par) * 128
            ws_ref[:, lane : lane + 128] = jnp.concatenate(rows, axis=0).astype(BF)
    zero = jnp.zeros((128, 128), BF)
    for b in range(3):
        w = [mix_ref[3 * a + b].astype(F32) for a in range(3)]
        mean = 0.5 * (w[0] + w[2])
        forms = [w[0], mean + 0.5 * w[1], mean - 0.5 * w[1], w[2]]
        for k in range(4):
            for par in range(2):
                d = b + par
                wm_ref[k, d * 128 : d * 128 + 128, par * 128 : par * 128 + 128] = forms[k].astype(BF)
    for k in range(4):
        wm_ref[k, 0:128, 128:256] = zero
        wm_ref[k, 384:512, 0:128] = zero


def prep(stem_weight, stem_bias, mix_weight):
    return pl.pallas_call(
        prep_kernel,
        in_specs=[VM] * 3,
        out_specs=[VM] * 4,
        out_shape=[
            jax.ShapeDtypeStruct((256, STEP * 256), BF),
            jax.ShapeDtypeStruct((1, 256), F32),
            jax.ShapeDtypeStruct((4, 512, 256), BF),
            jax.ShapeDtypeStruct((COLS, 6 * 256), BF),
        ],
        compiler_params=params(12),
        cost_estimate=cost(0, 2 << 20),
        name="prep",
    )(stem_weight, stem_bias[None], mix_weight)


def add_groups(codes_ref, win_ref, w_hbm, w_ref, sem, acc, arrays, number):
    first = number
    copies = [
        pltpu.make_async_copy(w_hbm.at[0, codes_ref[first + g]], w_ref.at[g], sem.at[g])
        for g in range(w_ref.shape[0])
    ]
    for copy in copies:
        copy.start()
    for array, begin, groups in arrays:
        for i in range(groups):
            copies[number - first].wait()
            q = codes_ref[number]
            for s in range(32):
                block = array[(begin + i) * 32 + s]
                part = jnp.dot(block, w_ref[number - first, s], preferred_element_type=F32)
                w = win_ref[0, q, s]
                place = (w % 4) * ROWS + w // 4
                acc[place] = acc[place] + part.astype(BF).astype(F32)
            number += 1


def near_kernel(codes_ref, win_ref, own_ref, core_ref, x_ref, w_hbm, acc, w_ref, sem):
    acc[...] = jnp.zeros_like(acc)
    arrays = [(own_ref, 1, 1), (core_ref, 1, 1), (x_ref, 1, 1)]
    add_groups(codes_ref, win_ref, w_hbm, w_ref, sem, acc, arrays, 0)


def far_kernel(
    codes_ref, win_ref, pos_ref, a_in, b_in, far_in, near_ref, w_hbm, fld_ref, a_ref, b_ref, acc, w_ref, sem
):
    acc[...] = near_ref[...]
    arrays = [(a_in, 0, 3), (b_in, 0, 3), (far_in, 0, 1)]
    add_groups(codes_ref, win_ref, w_hbm, w_ref, sem, acc, arrays, 3)
    for cb in range(4):
        rows = acc[cb * ROWS : (cb + 1) * ROWS].reshape(ROWS * 8, 128)
        fld_ref[:, cb * 128 : cb * 128 + 128] = rows.astype(BF)
    even = pos_ref[0] % 2 == 0
    top, bottom = fld_ref[0:16], fld_ref[ROWS * 8 - 16 : ROWS * 8]
    a_ref[...] = jnp.where(even, bottom, top)
    b_ref[...] = jnp.where(even, top, bottom)


def near_part(codes, win, own, core, x, weights):
    return pl.pallas_call(
        near_kernel,
        in_specs=[SM, SM] + [VM] * 3 + [HBM],
        out_specs=VM,
        out_shape=jax.ShapeDtypeStruct((ROWS * 4, 8, 128), F32),
        scratch_shapes=[
            pltpu.VMEM((3,) + weights.shape[2:], BF),
            pltpu.SemaphoreType.DMA((3,)),
        ],
        compiler_params=params(12),
        cost_estimate=cost(96 * 2 * 8 * 128 * 128, 4 << 20),
        name="near",
    )(codes, win, own, core, x, *in_hbm(weights))


def far_part(codes, win, pos, a, b, far, near, weights):
    return pl.pallas_call(
        far_kernel,
        in_specs=[SM, SM, SM] + [VM] * 4 + [HBM],
        out_specs=[VM] * 3,
        out_shape=[
            jax.ShapeDtypeStruct((ROWS * 8, COLS), BF),
            jax.ShapeDtypeStruct((16, COLS), BF),
            jax.ShapeDtypeStruct((16, COLS), BF),
        ],
        scratch_shapes=[
            pltpu.VMEM((ROWS * 4, 8, 128), F32),
            pltpu.VMEM((7,) + weights.shape[2:], BF),
            pltpu.SemaphoreType.DMA((7,)),
        ],
        compiler_params=params(16),
        cost_estimate=cost(224 * 2 * 8 * 128 * 128, 8 << 20),
        name="far",
    )(codes, win, pos, a, b, far, near, *in_hbm(weights))


def tall(fld_ref, a, b, band, last):
    even = band % 2 == 0
    b = jnp.where((band == 0) | (band == last), jnp.zeros_like(b), b)
    north = jnp.where(even, b, a)
    south = jnp.where(even, a, b)
    return jnp.concatenate([north, fld_ref[...], south], axis=0)


def edge_kernel(last, pos_ref, fld_ref, a_ref, b_ref, edge_ref):
    whole = tall(fld_ref, a_ref[...], b_ref[...], pos_ref[0], last)
    rank = lax.broadcasted_iota(jnp.int32, (16, COLS), 0)
    col = lax.broadcasted_iota(jnp.int32, (16, COLS), 1)
    pick = ((rank < 2) & (col == rank)) | ((rank >= 2) & (rank < 4) & (col == COLS - 4 + rank))
    pick = jnp.where(pick, 1.0, 0.0).astype(BF)
    edge_ref[...] = lax.dot_general(
        pick, whole, (((1,), (1,)), ((), ())), preferred_element_type=F32
    ).astype(BF)


def edges(n_band, pos, fld, a, b):
    return pl.pallas_call(
        functools.partial(edge_kernel, n_band - 1),
        in_specs=[SM, VM, VM, VM],
        out_specs=VM,
        out_shape=jax.ShapeDtypeStruct((16, (ROWS + 4) * 8), BF),
        compiler_params=params(8),
        cost_estimate=cost(0, 1 << 20),
        name="edges",
    )(pos, fld, a, b)


def build(last, pos_ref, fld_ref, a_ref, b_ref, core_ref, x_ref, hot_ref, g):
    whole = tall(fld_ref, a_ref[...], b_ref[...], pos_ref[0], last)
    even = pos_ref[1] % 2 == 0
    core, x = core_ref[...].astype(F32), x_ref[...].astype(F32)
    right, left = jnp.where(even, core, x), jnp.where(even, x, core)
    hr = lax.broadcasted_iota(jnp.int32, (16, 256), 0)
    hl = lax.broadcasted_iota(jnp.int32, (16, 256), 1)

    def halo(side, base, at):
        hot = ((hl % 128) == at) & (hr == hl // 128 + base)
        return lax.dot_general(
            side.astype(BF),
            jnp.where(hot, 1.0, 0.0).astype(BF),
            (((0,), (0,)), ((), ())),
            preferred_element_type=F32,
        )

    def moved(pair, tile):
        at = (2 * tile + pair) * 256
        return jnp.dot(whole, hot_ref[:, at : at + 256], preferred_element_type=F32)

    tiles = {(pair, tile): moved(pair, tile) for pair in range(2) for tile in range(3)}
    tiles[0, 0] = tiles[0, 0] + halo(left, 2, 0)
    tiles[1, 2] = tiles[1, 2] + halo(right, 0, SUB - 1)
    for (pair, tile), value in tiles.items():
        value = value.astype(BF)
        for half in range(2):
            d0 = (2 * pair + half) * 64
            part = value[:, half * 128 : half * 128 + 128]
            for m in range(BLOCKS):
                g[m, d0 : d0 + 64, tile * 128 : tile * 128 + 128] = part[48 * m : 48 * m + 64]


def conv_kernel(
    last,
    pos_ref,
    fld_ref,
    a_ref,
    b_ref,
    core_ref,
    x_ref,
    ws_ref,
    bs_ref,
    wm_ref,
    bm_ref,
    hot_ref,
    out_ref,
    g,
    hs,
    ys,
    yb,
    sem,
):
    s = pl.program_id(0)
    band = pos_ref[0]

    def stem(block, which, low, high):
        x = g[jnp.minimum(block, BLOCKS - 1)][:, :HROWS]
        for i in which:
            t = lax.dot_general(
                x,
                ws_ref[:, i * 256 : i * 256 + 256],
                (((0,), (0,)), ((), ())),
                preferred_element_type=F32,
            )
            t = t + bs_ref[...]
            h = t + t * jnp.tanh(t)
            if i == 0 and low is not None:
                h = h * low
            if i == STEP - 1 and high is not None:
                h = h * high
            hs[block % 2, i] = h.astype(BF)

    @pl.when(s == 0)
    def _():
        build(last, pos_ref, fld_ref, a_ref, b_ref, core_ref, x_ref, hot_ref, g)
        stem(0, range(STEP), jnp.where(band == 0, 0.0, 1.0), None)

    slot = s % 2

    def copy(at, slot):
        return pltpu.make_async_copy(
            yb.at[slot], out_ref.at[pl.ds(6 * at - 2, 6)], sem.at[slot]
        )

    first = pltpu.make_async_copy(yb.at[0, pl.ds(2, 4)], out_ref.at[pl.ds(0, 4)], sem.at[0])

    @pl.when(s == 2)
    def _():
        first.wait()

    @pl.when(s > 2)
    def _():
        copy(s - 2, slot).wait()

    rows = [(1 - slot, 4), (1 - slot, 5)] + [(slot, i) for i in range(STEP)]
    keep_last = jnp.where((s == BLOCKS - 2) & (band == last), 0.0, 1.0)

    def mix(t):
        for c in range(PAIRS // CHUNK):
            row0 = c * CHUNK

            def both(r):
                return jnp.concatenate(
                    [hs[rows[2 * t + r]][row0 + k * SUB : row0 + k * SUB + CHUNK] for k in range(2)],
                    axis=1,
                )

            h = [both(r) for r in range(4)]
            v = [h[0] - h[2], h[1] + h[2], h[2] - h[1], h[1] - h[3]]
            m = [jnp.dot(v[k], wm_ref[k], preferred_element_type=F32) for k in range(4)]
            plus, minus = m[1] + m[2], m[1] - m[2]
            for q, y in enumerate([plus + m[0], minus - m[3]]):
                row = 2 * t + q
                for par in range(2):
                    part = y[:, par * 128 : par * 128 + 128] + bm_ref[...]
                    for k in range(CHUNK // SUB):
                        to = pl.ds(2 * (c * CHUNK // SUB + k) + par, SUB, stride=PITCH)
                        ys[row, to, :] = part[k * SUB : k * SUB + SUB]
        for q in range(2):
            for a in range(SUB):
                yb[slot, 2 * t + q, 2 * SUB * a : 2 * SUB * a + 2 * SUB] = ys[
                    2 * t + q, PITCH * a : PITCH * a + 2 * SUB
                ].astype(BF)

    for t in range(STEP // 2):
        mix(t)
    stem(s + 1, range(STEP), None, keep_last)

    @pl.when(s == 0)
    def _():
        first.start()

    @pl.when(s > 0)
    def _():
        copy(s, slot).start()

    @pl.when(s == BLOCKS - 1)
    def _():
        copy(s - 1, 1 - slot).wait()
        copy(s, slot).wait()


def conv(n_band, pos, fld, a, b, core, x, ws, bs, wm, bm, hot):
    channels = bm.shape[-1]
    return pl.pallas_call(
        functools.partial(conv_kernel, n_band - 1),
        grid=(BLOCKS,),
        in_specs=[SM] + [VM] * 10,
        out_specs=ANY,
        out_shape=jax.ShapeDtypeStruct((ROWS, COLS, channels), BF),
        scratch_shapes=[
            pltpu.VMEM((BLOCKS, 256, LANES), BF),
            pltpu.VMEM((2, STEP, HROWS, 256), BF),
            pltpu.VMEM((STEP, SUB * PITCH, channels), F32),
            pltpu.VMEM((2, STEP, COLS, channels), BF),
            pltpu.SemaphoreType.DMA((2,)),
        ],
        compiler_params=params(20),
        cost_estimate=cost(2 * ROWS * COLS * 9 * 128 * 128, 12 << 20),
        name="conv",
    )(pos, fld, a, b, core, x, ws, bs, wm, bm, hot)


def on_device(source, routes, slot_weights, window, stem_weight, stem_bias, mix_weight, mix_bias):
    n_band = lax.axis_size("band")
    n_lon = lax.axis_size("lon")
    axes = ("band", "lon")
    band = lax.axis_index("band")
    lon = lax.axis_index("lon")

    def move(value, pairs):
        return lax.ppermute(value, axes, pairs)

    pos = jnp.stack([band, lon]).astype(jnp.int32)
    core_dl = jnp.where(lon % 2 == 0, 3, 1)
    x_dl = 4 - core_dl
    a_base = jnp.where(band % 2 == 0, 0, 8)
    b_base = 8 - a_base
    rim = (band == 0) | (band == n_band - 1)
    far_code = jnp.where(band < n_band // 2, 10, 2)
    near = [4 + 0 * lon, 4 + core_dl, 4 + x_dl]
    along_a = [a_base, a_base + core_dl, a_base + x_dl]
    along_b = [jnp.where(rim, 6, b_base), b_base + core_dl, b_base + x_dl]
    codes = jnp.stack(near + along_a + along_b + [far_code]).astype(jnp.int32)

    own, to_core, to_x, to_far = pack(pos, routes.T, source)
    core = move(to_core, swap_core(n_band, n_lon))
    x = move(to_x, swap_x(n_band, n_lon))
    far = move(to_far, swap_diagonal(n_band, n_lon))
    ws, bs, wm, hot = prep(stem_weight, stem_bias, mix_weight)
    core, x, far, ws, bs, wm, hot = lax.optimization_barrier((core, x, far, ws, bs, wm, hot))
    a_out = jnp.concatenate([own[0:32], core[0:32], x[0:32]], axis=0)
    b_out = jnp.concatenate([own[64:96], core[64:96], x[64:96]], axis=0)
    a_in = move(a_out, swap_a(n_band, n_lon))
    b_in = move(b_out, swap_b(n_band, n_lon))
    near = near_part(codes, window, own, core, x, slot_weights)
    a_in, b_in, near = lax.optimization_barrier((a_in, b_in, near))
    fld, a_row, b_row = far_part(codes, window, pos, a_in, b_in, far, near, slot_weights)
    a_halo = move(a_row, swap_a(n_band, n_lon))
    b_halo = move(b_row, swap_b(n_band, n_lon))
    edge = edges(n_band, pos, fld, a_halo, b_halo)
    core_edge = move(edge, swap_core(n_band, n_lon))
    x_edge = move(edge, swap_x(n_band, n_lon))
    return conv(
        n_band, pos, fld, a_halo, b_halo, core_edge, x_edge, ws, bs, wm, mix_bias[None], hot
    )


def solution(mesh):
    both = ("band", "lon")
    in_specs = (
        P(both, None, None),
        P(both, None),
        P(both, None, None, None, None),
        P(both, None, None),
        P(),
        P(),
        P(),
        P(),
    )
    return jax.shard_map(
        on_device, mesh=mesh, in_specs=in_specs, out_specs=P("band", "lon", None), check_vma=False
    )
```

time: 73.6 us -> 57.6 us (0.78)
  the two profiles are of different devices: /device:TPU:5 before, /device:TPU:0 now
where the time goes in v2:
time: 57.6 us; the launch traced here: 57.3 us
  Pallas kernels  30.5 us (53%)
  starting transfers between devices  10.8 us (19%)
  waiting for transfers between devices  10.3 us (18%)
  local copies, waits for them, and re-layouts  4.11 us (7%)
  other arithmetic  1.47 us (3%)
    pallas_call x1, Pallas kernels, conv(): pl.pallas_call(functools.partial(conv_kernel, n_band - 1), grid=(BLOCKS,)...  18.4 us
    ppermute x9, starting transfers between devices, move(): return lax.ppermute(value, axes, pairs)  10.8 us
    ppermute x9, waiting for transfers between devices, move(): return lax.ppermute(value, axes, pairs)  10.3 us
    pallas_call x1, Pallas kernels, far_part(): pl.pallas_call(far_kernel, in_specs=[SM, SM, SM] + [VM] * 4 + [HBM], out_...  4.81 us
    unnamed x13, local copies, waits for them, and re-layouts  4 us
    pallas_call x1, Pallas kernels, near_part(): pl.pallas_call(near_kernel, in_specs=[SM, SM] + [VM] * 3 + [HBM], out_spe...  3.11 us
    pallas_call x1, Pallas kernels, pack(): pl.pallas_call(pack_kernel, in_specs=[SM, HBM, HBM], out_specs=[VM] * 4,...  2.64 us
  transfers between devices with their start and end apart: 9, of which 5 were waited for; matrix products, arithmetic and copies ran while one was open for 3% of the time, Pallas kernels for 7%

profile of v2, /device:TPU:0, one launch (start us, length us, event | category | flops | bytes accessed | tf_op | source)
XLA Modules:
  0.0 57.3 jit_solution(1309927653400663439)
XLA Ops:
  0.1 2.6 %pack.1 = (bf16[96,8,128]{2,1,0:T(8,128)(2,1)S(1)}, bf16[96,8,128]{2,1,0:T(8,128)(2,1)S(1)}, bf16[96,8,128]{2,1,0:T(8,128)(2,1)S(1)}, bf16[32,8,128]{2,1,0:T(8,128)(2,1)S(1)}) custom-call(s32[2]{0:T(128)S(1)} %pad_add_fusion.pos_ref, s32[2,128]{1,0:T(2,128)} %bitcast.16, bf16[128,8,128]{2,1,0:T(8,128)(2,1)} %src_hbm.1), custom_call_target="tpu_custom_call" | custom-call | bytes 1048576 | tf_op jit(solution)/shard_map/pack/pallas_call | solution.py:121
  2.7 4.0 %collective-permute-start.2 = (bf16[32,8,128]{2,1,0:T(8,128)(2,1)S(1)}, bf16[32,8,128]{2,1,0:T(8,128)(2,1)S(1)}, u32[]{:S(2)}, u32[]{:S(2)}) collective-permute-start(bf16[32,8,128]{2,1,0:T(8,128)(2,1)S(1)} %get-tuple-element.29), channel_id=1, source_target_pairs={{0,6},{1,7},{2,4},{3,5},{4,2},{5,3},{6,0},{7,1},{8,14},{9,15},{10,... | collective-permute-start | bytes 196616 | tf_op jit(solution)/shard_map/ppermute | solution.py:476
  6.7 0.6 %collective-permute-start.1 = (bf16[96,8,128]{2,1,0:T(8,128)(2,1)S(1)}, bf16[96,8,128]{2,1,0:T(8,128)(2,1)S(1)}, u32[]{:S(2)}, u32[]{:S(2)}) collective-permute-start(bf16[96,8,128]{2,1,0:T(8,128)(2,1)S(1)} %get-tuple-element.28), channel_id=1, source_target_pairs={{0,3},{1,2},{2,1},{3,0},{4,7},{5,6},{6,5},{7,4},{8,11},{9,10},{10,... | collective-permute-start | bytes 589832 | tf_op jit(solution)/shard_map/ppermute | solution.py:476
  7.4 1.0 %copy-done = bf16[9,128,128]{2,1,0:T(8,128)(2,1)S(1)} copy-done((bf16[9,128,128]{2,1,0:T(8,128)(2,1)S(1)}, bf16[9,128,128]{2,1,0:T(8,128)(2,1)}, u32[]{:S(2)}) %copy-start) | copy-done | bytes 294936
  8.3 0.7 %copy-done.1 = bf16[9,8,128]{2,1,0:T(8,128)(2,1)S(1)} copy-done((bf16[9,8,128]{2,1,0:T(8,128)(2,1)S(1)}, bf16[9,8,128]{2,1,0:T(8,128)(2,1)}, u32[]{:S(2)}) %copy-start.1) | copy-done | bytes 18456
  9.0 0.7 %copy-done.2 = f32[128]{0:T(128)S(1)} copy-done((f32[128]{0:T(128)S(1)}, f32[128]{0:T(128)}, u32[]{:S(2)}) %copy-start.2) | copy-done | bytes 536
  9.7 0.7 %prep.1 = (bf16[256,1536]{1,0:T(8,128)(2,1)S(1)}, f32[1,256]{1,0:T(1,128)S(1)}, bf16[4,512,256]{2,1,0:T(8,128)(2,1)S(1)}, bf16[512,1536]{1,0:T(8,128)(2,1)S(1)}) custom-call(bf16[9,8,128]{2,1,0:T(8,128)(2,1)S(1)} %copy-done.1, f32[1,128]{1,0:T(1,128)S(1)} %bitcast.14, bf16[9,128,128]{2,1,0:T(8,128)(2,1)S(1)} %copy-done), custom_call_target="tpu_custom_call" | custom-call | bytes 2097152 | tf_op jit(solution)/shard_map/prep/pallas_call | solution.py:178
  10.4 1.0 %copy-done.3 = bf16[4,512,256]{2,1,0:T(8,128)(2,1)} copy-done((bf16[4,512,256]{2,1,0:T(8,128)(2,1)}, bf16[4,512,256]{2,1,0:T(8,128)(2,1)S(1)}, u32[]{:S(2)}) %copy-start.3) | copy-done | bytes 1048600
  11.4 1.8 %collective-permute-done.1.x_ref = bf16[96,8,128]{2,1,0:T(8,128)(2,1)S(1)} collective-permute-done((bf16[96,8,128]{2,1,0:T(8,128)(2,1)S(1)}, bf16[96,8,128]{2,1,0:T(8,128)(2,1)S(1)}, u32[]{:S(2)}, u32[]{:S(2)}) %collective-permute-start.1) | collective-permute-done | bytes 196640 | tf_op jit(solution)/shard_map/ppermute | solution.py:476
  13.3 0.7 %pad_maximum_fusion = bf16[96,8,128]{2,1,0:T(8,128)(2,1)} fusion(bf16[32,8,128]{2,1,0:T(8,128)(2,1)S(1)} %get-tuple-element.53, bf16[32,8,128]{2,1,0:T(8,128)(2,1)S(1)} %get-tuple-element.50, bf16[32,8,128]{2,1,0:T(8,128)(2,1)S(1)} %get-tuple-element.48), kind=kLoop, calls=%fused_computation | loop fusion | flops 196608 | bytes 393216 | tf_op jit(solution)/shard_map/concatenate | solution.py:496
  14.5 0.7 %pad_maximum_fusion.1 = bf16[96,8,128]{2,1,0:T(8,128)(2,1)} fusion(bf16[32,8,128]{2,1,0:T(8,128)(2,1)S(1)} %get-tuple-element.54, bf16[32,8,128]{2,1,0:T(8,128)(2,1)S(1)} %get-tuple-element.49, bf16[32,8,128]{2,1,0:T(8,128)(2,1)S(1)} %get-tuple-element.47), kind=kLoop, calls=%fused_computation.1 | loop fusion | flops 196608 | bytes 393216 | tf_op jit(solution)/shard_map/concatenate | solution.py:497
  15.2 0.9 %collective-permute-start.4 = (bf16[96,8,128]{2,1,0:T(8,128)(2,1)}, bf16[96,8,128]{2,1,0:T(8,128)(2,1)S(1)}, u32[]{:S(2)}, u32[]{:S(2)}) collective-permute-start(bf16[96,8,128]{2,1,0:T(8,128)(2,1)} %pad_maximum_fusion.1), channel_id=1, source_target_pairs={{0,2},{1,3},{2,0},{3,1},{4,8},{5,9},{6,10},{7,11},{8,4},{9,5},{10,... | collective-permute-start | bytes 589832 | tf_op jit(solution)/shard_map/ppermute | solution.py:476
  16.0 0.7 %copy.10.win_ref = s32[1,12,32]{2,1,0:T(8,128)S(1)} copy(s32[1,12,32]{2,0,1:T(1,128)} %param.11) | data formatting | bytes 3072 | tf_op args[3]
  16.8 3.1 %near.1.near_ref = f32[256,8,128]{2,1,0:T(8,128)S(1)} custom-call(s32[10]{0:T(128)S(1)} %stack.51.codes_ref, s32[1,12,32]{2,1,0:T(8,128)S(1)} %copy.10.win_ref, bf16[96,8,128]{2,1,0:T(8,128)(2,1)S(1)} %get-tuple-element.26.own_ref, bf16[96,8,128]{2,1,0:T(8,128)(2,1)S(1)} %collective-permute-done.core_ref, ...), custom_call_target="tpu_custom_call" | custom-call | flops 25165824 | bytes 4194304 | tf_op jit(solution)/shard_map/near/pallas_call | solution.py:237
  19.9 3.8 %collective-permute-done.3.a_in = bf16[96,8,128]{2,1,0:T(8,128)(2,1)S(1)} collective-permute-done((bf16[96,8,128]{2,1,0:T(8,128)(2,1)}, bf16[96,8,128]{2,1,0:T(8,128)(2,1)S(1)}, u32[]{:S(2)}, u32[]{:S(2)}) %collective-permute-start.3) | collective-permute-done | bytes 196640 | tf_op jit(solution)/shard_map/ppermute | solution.py:476
  23.8 4.8 %far.1 = (bf16[512,512]{1,0:T(8,128)(2,1)S(1)}, bf16[16,512]{1,0:T(8,128)(2,1)S(1)}, bf16[16,512]{1,0:T(8,128)(2,1)S(1)}) custom-call(s32[10]{0:T(128)S(1)} %stack.51.codes_ref, s32[1,12,32]{2,1,0:T(8,128)S(1)} %copy.10.win_ref, s32[2]{0:T(128)S(1)} %pad_add_fusion.pos_ref, bf16[96,8,128]{2,1,0:T(8,128)(2,1)S(1)} %collective-permute-done.3.a_in, ...), custom_call_target="tpu_custom_call" | custom-call | flops 58720256 | bytes 8388608 | tf_op jit(solution)/shard_map/far/pallas_call | solution.py:253
  28.6 2.4 %collective-permute-start.5 = (bf16[16,512]{1,0:T(8,128)(2,1)S(1)}, bf16[16,512]{1,0:T(8,128)(2,1)S(1)}, u32[]{:S(2)}, u32[]{:S(2)}) collective-permute-start(bf16[16,512]{1,0:T(8,128)(2,1)S(1)} %get-tuple-element.41), channel_id=1, source_target_pairs={{0,4},{1,5},{2,6},{3,7},{4,0},{5,1},{6,2},{7,3},{8,12},{9,13},{10,... | collective-permute-start | bytes 49160 | tf_op jit(solution)/shard_map/ppermute | solution.py:476
  31.0 1.1 %collective-permute-start.6 = (bf16[16,512]{1,0:T(8,128)(2,1)S(1)}, bf16[16,512]{1,0:T(8,128)(2,1)S(1)}, u32[]{:S(2)}, u32[]{:S(2)}) collective-permute-start(bf16[16,512]{1,0:T(8,128)(2,1)S(1)} %get-tuple-element.42), channel_id=1, source_target_pairs={{0,2},{1,3},{2,0},{3,1},{4,8},{5,9},{6,10},{7,11},{8,4},{9,5},{10,... | collective-permute-start | bytes 49160 | tf_op jit(solution)/shard_map/ppermute | solution.py:476
  32.1 0.6 %collective-permute-done.5.a_ref = bf16[16,512]{1,0:T(8,128)(2,1)S(1)} collective-permute-done((bf16[16,512]{1,0:T(8,128)(2,1)S(1)}, bf16[16,512]{1,0:T(8,128)(2,1)S(1)}, u32[]{:S(2)}, u32[]{:S(2)}) %collective-permute-start.5) | collective-permute-done | bytes 16416 | tf_op jit(solution)/shard_map/ppermute | solution.py:476
  32.8 2.0 %collective-permute-done.6.b_ref = bf16[16,512]{1,0:T(8,128)(2,1)S(1)} collective-permute-done((bf16[16,512]{1,0:T(8,128)(2,1)S(1)}, bf16[16,512]{1,0:T(8,128)(2,1)S(1)}, u32[]{:S(2)}, u32[]{:S(2)}) %collective-permute-start.6) | collective-permute-done | bytes 16416 | tf_op jit(solution)/shard_map/ppermute | solution.py:476
  34.8 0.8 %edges.1 = bf16[16,544]{1,0:T(8,128)(2,1)S(1)} custom-call(s32[2]{0:T(128)S(1)} %pad_add_fusion.pos_ref, bf16[512,512]{1,0:T(8,128)(2,1)S(1)} %get-tuple-element.40.fld_ref, bf16[16,512]{1,0:T(8,128)(2,1)S(1)} %collective-permute-done.5.a_ref, bf16[16,512]{1,0:T(8,128)(2,1)S(1)} %collective-permute-done.6.b_ref), custom_call_target="tpu_custom_call" | custom-call | bytes 1048576 | tf_op jit(solution)/shard_map/edges/pallas_call | solution.py:293
  35.7 1.2 %collective-permute-start.7 = (bf16[16,544]{1,0:T(8,128)(2,1)S(1)}, bf16[16,544]{1,0:T(8,128)(2,1)S(1)}, u32[]{:S(2)}, u32[]{:S(2)}) collective-permute-start(bf16[16,544]{1,0:T(8,128)(2,1)S(1)} %edges.1), channel_id=1, source_target_pairs={{0,1},{1,0},{2,3},{3,2},{4,5},{5,4},{6,7},{7,6},{8,9},{9,8},{10,11... | collective-permute-start | bytes 52232 | tf_op jit(solution)/shard_map/ppermute | solution.py:476
  36.9 2.0 %collective-permute-done.8.x_ref = bf16[16,544]{1,0:T(8,128)(2,1)S(1)} collective-permute-done((bf16[16,544]{1,0:T(8,128)(2,1)S(1)}, bf16[16,544]{1,0:T(8,128)(2,1)S(1)}, u32[]{:S(2)}, u32[]{:S(2)}) %collective-permute-start.8) | collective-permute-done | bytes 17440 | tf_op jit(solution)/shard_map/ppermute | solution.py:476
  38.9 18.4 %conv.1 = bf16[64,512,128]{2,1,0:T(8,128)(2,1)} custom-call(s32[2]{0:T(128)S(1)} %pad_add_fusion.pos_ref, bf16[512,512]{1,0:T(8,128)(2,1)S(1)} %get-tuple-element.40.fld_ref, bf16[16,512]{1,0:T(8,128)(2,1)S(1)} %collective-permute-done.5.a_ref, bf16[16,512]{1,0:T(8,128)(2,1)S(1)} %collective-permute-done.6.b_ref, ...), custom_call_target="tpu_custom_call" | custom-call | flops 9663676416 | bytes 12582912 | tf_op jit(solution)/shard_map/conv/pallas_call | solution.py:449
  (19 shorter events, 0.8 us)
Async XLA Ops:
  2.7 8.7 %collective-permute-start.2 = (bf16[32,8,128]{2,1,0:T(8,128)(2,1)S(1)}, bf16[32,8,128]{2,1,0:T(8,128)(2,1)S(1)}, u32[]{:S(2)}, u32[]{:S(2)}) collective-permute-start(bf16[32,8,128]{2,1,0:T(8,128)(2,1)S(1)} %get-tuple-element.29), channel_id=1, source_target_pairs={{0,6},{1,7},{2,4},{3,5},{4,2},{5,3},{6,0},{7,1},{8,14},{9,15},{10,... | collective-permute-start | bytes 196616 | tf_op jit(solution)/shard_map/ppermute | solution.py:476
  6.7 4.7 %collective-permute-start = (bf16[96,8,128]{2,1,0:T(8,128)(2,1)S(1)}, bf16[96,8,128]{2,1,0:T(8,128)(2,1)S(1)}, u32[]{:S(2)}, u32[]{:S(2)}) collective-permute-start(bf16[96,8,128]{2,1,0:T(8,128)(2,1)S(1)} %get-tuple-element.27), channel_id=1, source_target_pairs={{0,1},{1,0},{2,3},{3,2},{4,5},{5,4},{6,7},{7,6},{8,9},{9,8},{10,11... | collective-permute-start | bytes 589832 | tf_op jit(solution)/shard_map/ppermute | solution.py:476
  6.7 6.6 %collective-permute-start.1 = (bf16[96,8,128]{2,1,0:T(8,128)(2,1)S(1)}, bf16[96,8,128]{2,1,0:T(8,128)(2,1)S(1)}, u32[]{:S(2)}, u32[]{:S(2)}) collective-permute-start(bf16[96,8,128]{2,1,0:T(8,128)(2,1)S(1)} %get-tuple-element.28), channel_id=1, source_target_pairs={{0,3},{1,2},{2,1},{3,0},{4,7},{5,6},{6,5},{7,4},{8,11},{9,10},{10,... | collective-permute-start | bytes 589832 | tf_op jit(solution)/shard_map/ppermute | solution.py:476
  7.3 1.0 %copy-start = (bf16[9,128,128]{2,1,0:T(8,128)(2,1)S(1)}, bf16[9,128,128]{2,1,0:T(8,128)(2,1)}, u32[]{:S(2)}) copy-start(bf16[9,128,128]{2,1,0:T(8,128)(2,1)} %mix_ref.1) | copy-start | bytes 884740
  8.3 0.7 %copy-start.1 = (bf16[9,8,128]{2,1,0:T(8,128)(2,1)S(1)}, bf16[9,8,128]{2,1,0:T(8,128)(2,1)}, u32[]{:S(2)}) copy-start(bf16[9,8,128]{2,1,0:T(8,128)(2,1)} %stem_ref.1) | copy-start | bytes 55300
  9.0 0.7 %copy-start.2 = (f32[128]{0:T(128)S(1)}, f32[128]{0:T(128)}, u32[]{:S(2)}) copy-start(f32[128]{0:T(128)} %param.13) | copy-start | bytes 1540
  10.4 1.0 %copy-start.3 = (bf16[4,512,256]{2,1,0:T(8,128)(2,1)}, bf16[4,512,256]{2,1,0:T(8,128)(2,1)S(1)}, u32[]{:S(2)}) copy-start(bf16[4,512,256]{2,1,0:T(8,128)(2,1)S(1)} %get-tuple-element.45.wm_ref) | copy-start | bytes 3145732
  14.0 9.8 %collective-permute-start.3 = (bf16[96,8,128]{2,1,0:T(8,128)(2,1)}, bf16[96,8,128]{2,1,0:T(8,128)(2,1)S(1)}, u32[]{:S(2)}, u32[]{:S(2)}) collective-permute-start(bf16[96,8,128]{2,1,0:T(8,128)(2,1)} %pad_maximum_fusion), channel_id=1, source_target_pairs={{0,4},{1,5},{2,6},{3,7},{4,0},{5,1},{6,2},{7,3},{8,12},{9,13},{10,... | collective-permute-start | bytes 589832 | tf_op jit(solution)/shard_map/ppermute | solution.py:476
  15.2 8.6 %collective-permute-start.4 = (bf16[96,8,128]{2,1,0:T(8,128)(2,1)}, bf16[96,8,128]{2,1,0:T(8,128)(2,1)S(1)}, u32[]{:S(2)}, u32[]{:S(2)}) collective-permute-start(bf16[96,8,128]{2,1,0:T(8,128)(2,1)} %pad_maximum_fusion.1), channel_id=1, source_target_pairs={{0,2},{1,3},{2,0},{3,1},{4,8},{5,9},{6,10},{7,11},{8,4},{9,5},{10,... | collective-permute-start | bytes 589832 | tf_op jit(solution)/shard_map/ppermute | solution.py:476
  19.9 19.0 %copy-start.4 = (bf16[4,512,256]{2,1,0:T(8,128)(2,1)S(1)}, bf16[4,512,256]{2,1,0:T(8,128)(2,1)}, u32[]{:S(2)}) copy-start(bf16[4,512,256]{2,1,0:T(8,128)(2,1)} %copy-done.3) | copy-start | bytes 3145732
  19.9 18.9 %copy-start.5 = (f32[128]{0:T(128)S(1)}, f32[128]{0:T(128)}, u32[]{:S(2)}) copy-start(f32[128]{0:T(128)} %param.15) | copy-start | bytes 1540
  28.6 4.2 %collective-permute-start.5 = (bf16[16,512]{1,0:T(8,128)(2,1)S(1)}, bf16[16,512]{1,0:T(8,128)(2,1)S(1)}, u32[]{:S(2)}, u32[]{:S(2)}) collective-permute-start(bf16[16,512]{1,0:T(8,128)(2,1)S(1)} %get-tuple-element.41), channel_id=1, source_target_pairs={{0,4},{1,5},{2,6},{3,7},{4,0},{5,1},{6,2},{7,3},{8,12},{9,13},{10,... | collective-permute-start | bytes 49160 | tf_op jit(solution)/shard_map/ppermute | solution.py:476
  31.0 3.7 %collective-permute-start.6 = (bf16[16,512]{1,0:T(8,128)(2,1)S(1)}, bf16[16,512]{1,0:T(8,128)(2,1)S(1)}, u32[]{:S(2)}, u32[]{:S(2)}) collective-permute-start(bf16[16,512]{1,0:T(8,128)(2,1)S(1)} %get-tuple-element.42), channel_id=1, source_target_pairs={{0,2},{1,3},{2,0},{3,1},{4,8},{5,9},{6,10},{7,11},{8,4},{9,5},{10,... | collective-permute-start | bytes 49160 | tf_op jit(solution)/shard_map/ppermute | solution.py:476
  35.6 3.3 %collective-permute-start.8 = (bf16[16,544]{1,0:T(8,128)(2,1)S(1)}, bf16[16,544]{1,0:T(8,128)(2,1)S(1)}, u32[]{:S(2)}, u32[]{:S(2)}) collective-permute-start(bf16[16,544]{1,0:T(8,128)(2,1)S(1)} %edges.1), channel_id=1, source_target_pairs={{0,3},{1,2},{2,1},{3,0},{4,7},{5,6},{6,5},{7,4},{8,11},{9,10},{10,... | collective-permute-start | bytes 52232 | tf_op jit(solution)/shard_map/ppermute | solution.py:476
  35.7 3.2 %collective-permute-start.7 = (bf16[16,544]{1,0:T(8,128)(2,1)S(1)}, bf16[16,544]{1,0:T(8,128)(2,1)S(1)}, u32[]{:S(2)}, u32[]{:S(2)}) collective-permute-start(bf16[16,544]{1,0:T(8,128)(2,1)S(1)} %edges.1), channel_id=1, source_target_pairs={{0,1},{1,0},{2,3},{3,2},{4,5},{5,4},{6,7},{7,6},{8,9},{9,8},{10,11... | collective-permute-start | bytes 52232 | tf_op jit(solution)/shard_map/ppermute | solution.py:476

commit v3 on v2

v3 whole, which is shorter than its diff:
```python
import functools

import jax
import jax.numpy as jnp
from jax import lax
from jax.experimental import pallas as pl
from jax.experimental.pallas import tpu as pltpu
from jax.sharding import PartitionSpec as P

ROWS = 64
COLS = 512
PAIRS = COLS // 2
SUB = 16
HROWS = PAIRS + SUB
PITCH = 2 * SUB + 1
LANES = 384
CHUNK = 256
STEP = 6
BLOCKS = (ROWS + 2) // STEP
SCALE = 1.0 / 2.0
BF = jnp.bfloat16
F32 = jnp.float32
VM = pl.BlockSpec(memory_space=pltpu.VMEM)
SM = pl.BlockSpec(memory_space=pltpu.SMEM)
ANY = pl.BlockSpec(memory_space=pl.ANY)
HBM = pl.BlockSpec(memory_space=pltpu.HBM)


def params(mib):
    return pltpu.CompilerParams(vmem_limit_bytes=mib << 20)


def cost(flops, size):
    return pl.CostEstimate(flops=flops, bytes_accessed=size, transcendentals=0)


def swap(n_band, n_lon, way, turn):
    pairs = []
    for b in range(n_band):
        if way == "a":
            partner = b ^ 1
        elif way == "b":
            partner = b + 1 if b % 2 else b - 1
        else:
            partner = b
        for l in range(n_lon):
            target = {"stay": l, "core": l ^ 1, "x": n_lon - 1 - l, "across": (l + 2) % n_lon}[turn]
            if not 0 <= partner < n_band:
                pairs.append((b * n_lon + l, b * n_lon + (l + 2) % n_lon))
            else:
                pairs.append((b * n_lon + l, partner * n_lon + target))
    return pairs


def in_hbm(*arrays):
    return [pltpu.with_memory_space_constraint(a, pltpu.HBM) for a in arrays]


def pack_kernel(
    pos_ref, routes_hbm, src_hbm, *refs
):
    outs, (routes_ref, src_ref, buf, table, count, sem) = refs[:10], refs[10:]
    copies = [
        pltpu.make_async_copy(routes_hbm, routes_ref, sem.at[0]),
        pltpu.make_async_copy(src_hbm, src_ref, sem.at[1]),
    ]
    for copy in copies:
        copy.start()
    band = pos_ref[0]
    lon = pos_ref[1]
    a_dir = 1 - 2 * (band % 2)
    core_dl = 1 + 2 * (lon % 2)
    for q in range(12):
        db, dl = q // 4 - 1, q % 4
        if db == 0:
            way = 0
        else:
            way = jnp.where(a_dir == db, 3, 6)
        if dl == 0:
            group = way
        elif dl == 2:
            group = 6 if db == 0 else 9
        else:
            group = jnp.where(core_dl == dl, 1, 2) + way
        table[q] = group * 32
        count[q] = 0
    buf[...] = jnp.zeros_like(buf)
    for copy in copies:
        copy.wait()

    def one(j, carry):
        block = src_ref[j]
        for t in range(2):
            q = routes_ref[t, j]
            rank = count[q]
            count[q] = rank + 1
            buf[table[q] + rank] = block
        return carry

    lax.fori_loop(0, src_ref.shape[0], one, 0, unroll=8)
    for group, out in enumerate(outs):
        out[...] = buf[group * 32 : group * 32 + 32]


def pack(pos, routes, source):
    fields, cells = source.shape[1:]
    shape = lambda n: jax.ShapeDtypeStruct((n, fields, cells), BF)
    return pl.pallas_call(
        pack_kernel,
        in_specs=[SM, HBM, HBM],
        out_specs=[VM] * 10,
        out_shape=[shape(32)] * 10,
        scratch_shapes=[
            pltpu.SMEM(routes.shape, jnp.int32),
            pltpu.VMEM(source.shape, BF),
            pltpu.VMEM((320, fields, cells), BF),
            pltpu.SMEM((12,), jnp.int32),
            pltpu.SMEM((12,), jnp.int32),
            pltpu.SemaphoreType.DMA((2,)),
        ],
        compiler_params=params(16),
        cost_estimate=cost(0, 1 << 20),
        name="pack",
    )(pos, *in_hbm(routes, source))


def prep_kernel(stem_ref, bias_ref, mix_ref, ws_ref, bs_ref, wm_ref):
    for par in range(2):
        bs_ref[:, par * 128 : par * 128 + 128] = bias_ref[...] * SCALE
    zero8 = jnp.zeros((8, 128), F32)
    taps = [stem_ref[t].astype(F32) * SCALE for t in range(9)]
    for i in range(STEP):
        for par in range(2):
            rows = []
            for d in range(4):
                for row in range(8):
                    a, b = row - i, d - par
                    rows.append(taps[3 * a + b] if 0 <= a < 3 and 0 <= b < 3 else zero8)
            lane = (2 * i + par) * 128
            ws_ref[:, lane : lane + 128] = jnp.concatenate(rows, axis=0).astype(BF)
    zero = jnp.zeros((128, 128), BF)
    for b in range(3):
        w = [mix_ref[3 * a + b].astype(F32) for a in range(3)]
        mean = 0.5 * (w[0] + w[2])
        forms = [w[0], mean + 0.5 * w[1], mean - 0.5 * w[1], w[2]]
        for k in range(4):
            for par in range(2):
                d = b + par
                wm_ref[k, d * 128 : d * 128 + 128, par * 128 : par * 128 + 128] = forms[k].astype(BF)
    for k in range(4):
        wm_ref[k, 0:128, 128:256] = zero
        wm_ref[k, 384:512, 0:128] = zero


def prep(stem_weight, stem_bias, mix_weight):
    return pl.pallas_call(
        prep_kernel,
        in_specs=[VM] * 3,
        out_specs=[VM] * 3,
        out_shape=[
            jax.ShapeDtypeStruct((256, STEP * 256), BF),
            jax.ShapeDtypeStruct((1, 256), F32),
            jax.ShapeDtypeStruct((4, 512, 256), BF),
        ],
        compiler_params=params(12),
        cost_estimate=cost(0, 2 << 20),
        name="prep",
    )(*in_hbm(stem_weight, stem_bias[None], mix_weight))


def add_groups(codes_ref, win_ref, w_hbm, w_ref, sem, inc, acc, arrays, first):
    def copy(g):
        return pltpu.make_async_copy(w_hbm.at[0, codes_ref[first + g]], w_ref.at[g], sem.at[g])

    for g in range(len(arrays)):
        copy(g).start()
    for g, array in enumerate(arrays):
        inc[g] = array[...]

    def group(g, carry):
        copy(g).wait()
        q = codes_ref[first + g]
        for s in range(0, 32, 2):
            pair = jnp.dot(
                inc[g, s : s + 2].reshape(16, 128),
                jnp.concatenate([w_ref[g, s], w_ref[g, s + 1]], axis=1),
                preferred_element_type=F32,
            )
            for i in range(2):
                part = pair[8 * i : 8 * i + 8, 128 * i : 128 * i + 128]
                w = win_ref[0, q, s + i]
                place = (w % 4) * ROWS + w // 4
                acc[place] = acc[place] + part.astype(BF).astype(F32)
        return carry

    lax.fori_loop(0, len(arrays), group, 0)


def near_kernel(codes_ref, win_ref, own_ref, core_ref, x_ref, w_hbm, acc, w_ref, inc, sem):
    acc[...] = jnp.zeros_like(acc)
    add_groups(codes_ref, win_ref, w_hbm, w_ref, sem, inc, acc, [own_ref, core_ref, x_ref], 0)


def far_kernel(codes_ref, win_ref, pos_ref, *refs):
    arrays, (near_ref, w_hbm, fld_ref, a_ref, b_ref, acc, w_ref, inc, sem) = refs[:7], refs[7:]
    acc[...] = near_ref[...]
    add_groups(codes_ref, win_ref, w_hbm, w_ref, sem, inc, acc, arrays, 3)
    for cb in range(4):
        rows = acc[cb * ROWS : (cb + 1) * ROWS].reshape(ROWS * 8, 128)
        fld_ref[:, cb * 128 : cb * 128 + 128] = rows.astype(BF)
    even = pos_ref[0] % 2 == 0
    top, bottom = fld_ref[0:16], fld_ref[ROWS * 8 - 16 : ROWS * 8]
    a_ref[...] = jnp.where(even, bottom, top)
    b_ref[...] = jnp.where(even, top, bottom)


def near_part(codes, win, own, core, x, weights):
    return pl.pallas_call(
        near_kernel,
        in_specs=[SM, SM] + [VM] * 3 + [HBM],
        out_specs=VM,
        out_shape=jax.ShapeDtypeStruct((ROWS * 4, 8, 128), F32),
        scratch_shapes=[
            pltpu.VMEM((3,) + weights.shape[2:], BF),
            pltpu.VMEM((3, 32, 8, 128), BF),
            pltpu.SemaphoreType.DMA((3,)),
        ],
        compiler_params=params(12),
        cost_estimate=cost(96 * 2 * 8 * 128 * 128, 4 << 20),
        name="near",
    )(codes, win, own, core, x, *in_hbm(weights))


def far_part(codes, win, pos, arrays, near, weights):
    return pl.pallas_call(
        far_kernel,
        in_specs=[SM, SM, SM] + [VM] * 8 + [HBM],
        out_specs=[VM] * 3,
        out_shape=[
            jax.ShapeDtypeStruct((ROWS * 8, COLS), BF),
            jax.ShapeDtypeStruct((16, COLS), BF),
            jax.ShapeDtypeStruct((16, COLS), BF),
        ],
        scratch_shapes=[
            pltpu.VMEM((ROWS * 4, 8, 128), F32),
            pltpu.VMEM((7,) + weights.shape[2:], BF),
            pltpu.VMEM((7, 32, 8, 128), BF),
            pltpu.SemaphoreType.DMA((7,)),
        ],
        compiler_params=params(16),
        cost_estimate=cost(224 * 2 * 8 * 128 * 128, 8 << 20),
        name="far",
    )(codes, win, pos, *arrays, near, *in_hbm(weights))


def tall(fld_ref, a, b, band, last):
    even = band % 2 == 0
    b = jnp.where((band == 0) | (band == last), jnp.zeros_like(b), b)
    north = jnp.where(even, b, a)
    south = jnp.where(even, a, b)
    return jnp.concatenate([north, fld_ref[...], south], axis=0)


def edge_kernel(last, pos_ref, fld_ref, a_ref, b_ref, edge_ref):
    whole = tall(fld_ref, a_ref[...], b_ref[...], pos_ref[0], last)
    rank = lax.broadcasted_iota(jnp.int32, (16, COLS), 0)
    col = lax.broadcasted_iota(jnp.int32, (16, COLS), 1)
    pick = ((rank < 2) & (col == rank)) | ((rank >= 2) & (rank < 4) & (col == COLS - 4 + rank))
    pick = jnp.where(pick, 1.0, 0.0).astype(BF)
    edge_ref[...] = lax.dot_general(
        pick, whole, (((1,), (1,)), ((), ())), preferred_element_type=F32
    ).astype(BF)


def edges(n_band, pos, fld, a, b):
    return pl.pallas_call(
        functools.partial(edge_kernel, n_band - 1),
        in_specs=[SM, VM, VM, VM],
        out_specs=VM,
        out_shape=jax.ShapeDtypeStruct((16, (ROWS + 4) * 8), BF),
        compiler_params=params(8),
        cost_estimate=cost(0, 1 << 20),
        name="edges",
    )(pos, fld, a, b)


def spread_kernel(fld_ref, g_ref, hot_ref):
    c = lax.broadcasted_iota(jnp.int32, (COLS, 256), 0)
    lane = lax.broadcasted_iota(jnp.int32, (COLS, 256), 1)
    for tile in range(3):
        n = lane % 128 + tile * 128
        j = jnp.where(n < PAIRS, SUB * (n % SUB) + n // SUB, SUB * (n - PAIRS + 1))
        gap = jnp.where(n < HROWS, c - 2 * j - lane // 128, -COLS)
        for pair in range(2):
            hot = jnp.where(gap == 2 * pair - 2, 1.0, 0.0)
            hot_ref[:, (2 * tile + pair) * 256 : (2 * tile + pair) * 256 + 256] = hot.astype(BF)
    zero = jnp.zeros((16, 256), BF)
    for pair in range(2):
        for tile in range(3):
            at = (2 * tile + pair) * 256
            value = jnp.dot(fld_ref[...], hot_ref[:, at : at + 256], preferred_element_type=F32)
            value = jnp.concatenate([zero, value.astype(BF), zero], axis=0)
            for half in range(2):
                d0 = (2 * pair + half) * 64
                for m in range(BLOCKS):
                    g_ref[m, d0 : d0 + 64, tile * 128 : tile * 128 + 128] = value[
                        48 * m : 48 * m + 64, half * 128 : half * 128 + 128
                    ]


def spread(fld):
    return pl.pallas_call(
        spread_kernel,
        in_specs=[VM],
        out_specs=[VM] * 2,
        out_shape=[
            jax.ShapeDtypeStruct((BLOCKS, 256, LANES), BF),
            jax.ShapeDtypeStruct((COLS, 6 * 256), BF),
        ],
        compiler_params=params(12),
        cost_estimate=cost(2 * 512 * 512 * 1536, 4 << 20),
        name="spread",
    )(fld)


def halos(last, pos_ref, a_ref, b_ref, core_ref, x_ref, hot_ref, rim, left_ref, right_ref):
    band = pos_ref[0]
    a, b = a_ref[...], b_ref[...]
    b = jnp.where((band == 0) | (band == last), jnp.zeros_like(b), b)
    even = band % 2 == 0
    rows = jnp.concatenate([jnp.where(even, b, a), jnp.where(even, a, b)], axis=0)
    rim[...] = jnp.zeros_like(rim)
    for pair in range(2):
        for tile in range(3):
            at = (2 * tile + pair) * 256
            value = jnp.dot(rows, hot_ref[:, at : at + 256], preferred_element_type=F32).astype(BF)
            for half in range(2):
                d0 = (2 * pair + half) * 64
                lanes = slice(tile * 128, tile * 128 + 128)
                part = value[:, half * 128 : half * 128 + 128]
                rim[0, d0 : d0 + 16, lanes] = part[0:16]
                rim[1, d0 + 48 : d0 + 64, lanes] = part[16:32]
    even = pos_ref[1] % 2 == 0
    core, x = core_ref[...].astype(F32), x_ref[...].astype(F32)
    right, left = jnp.where(even, core, x), jnp.where(even, x, core)
    hr = lax.broadcasted_iota(jnp.int32, (16, 256), 0)
    hl = lax.broadcasted_iota(jnp.int32, (16, 256), 1)
    for side, base, at, out in ((left, 2, 0, left_ref), (right, 0, SUB - 1, right_ref)):
        hot = ((hl % 128) == at) & (hr == hl // 128 + base)
        value = lax.dot_general(
            side.astype(BF),
            jnp.where(hot, 1.0, 0.0).astype(BF),
            (((0,), (0,)), ((), ())),
            preferred_element_type=F32,
        ).astype(BF)
        for m in range(BLOCKS):
            for half in range(2):
                out[m, half * 64 : half * 64 + 64] = value[
                    48 * m : 48 * m + 64, half * 128 : half * 128 + 128
                ]


def conv_kernel(
    last,
    pos_ref,
    g_ref,
    a_ref,
    b_ref,
    core_ref,
    x_ref,
    ws_ref,
    bs_ref,
    wm_ref,
    bm_ref,
    hot_ref,
    out_ref,
    rim,
    left_ref,
    right_ref,
    hs,
    ys,
    yb,
    sem,
):
    band = pos_ref[0]

    def stem(block, which, low, high):
        block_in = jnp.minimum(block, BLOCKS - 1)
        edge = jnp.where(block_in == 0, 0, jnp.where(block_in == BLOCKS - 1, 1, 2))
        x = g_ref[block_in] + rim[edge]
        first = jnp.concatenate([x[:128, :128] + left_ref[block_in], x[128:, :128]], axis=0)
        final = jnp.concatenate([x[:128, 256:], x[128:, 256:] + right_ref[block_in]], axis=0)
        x = jnp.concatenate([first, x[:, 128:256], final], axis=1)[:, :HROWS]
        for i in which:
            t = lax.dot_general(
                x,
                ws_ref[:, i * 256 : i * 256 + 256],
                (((0,), (0,)), ((), ())),
                preferred_element_type=F32,
            )
            t = t + bs_ref[...]
            h = t + t * jnp.tanh(t)
            if i == 0 and low is not None:
                h = h * low
            if i == STEP - 1 and high is not None:
                h = h * high
            hs[block % 2, i] = h.astype(BF)

    halos(last, pos_ref, a_ref, b_ref, core_ref, x_ref, hot_ref, rim, left_ref, right_ref)
    stem(0, range(STEP), jnp.where(band == 0, 0.0, 1.0), None)

    def copy(at, slot):
        return pltpu.make_async_copy(
            yb.at[slot], out_ref.at[pl.ds(6 * at - 2, 6)], sem.at[slot]
        )

    first = pltpu.make_async_copy(yb.at[0, pl.ds(2, 4)], out_ref.at[pl.ds(0, 4)], sem.at[0])

    def step(s, carry):
        slot = s % 2

        @pl.when(s == 2)
        def _():
            first.wait()

        @pl.when(s > 2)
        def _():
            copy(s - 2, slot).wait()

        rows = [(1 - slot, 4), (1 - slot, 5)] + [(slot, i) for i in range(STEP)]
        keep_last = jnp.where((s == BLOCKS - 2) & (band == last), 0.0, 1.0)

        def mix(t):
            for c in range(PAIRS // CHUNK):
                row0 = c * CHUNK

                def both(r):
                    return jnp.concatenate(
                        [hs[rows[2 * t + r]][row0 + k * SUB : row0 + k * SUB + CHUNK] for k in range(2)],
                        axis=1,
                    )

                h = [both(r) for r in range(4)]
                v = [h[0] - h[2], h[1] + h[2], h[2] - h[1], h[1] - h[3]]
                m = [jnp.dot(v[k], wm_ref[k], preferred_element_type=F32) for k in range(4)]
                plus, minus = m[1] + m[2], m[1] - m[2]
                for q, y in enumerate([plus + m[0], minus - m[3]]):
                    row = 2 * t + q
                    for par in range(2):
                        part = y[:, par * 128 : par * 128 + 128] + bm_ref[...]
                        for k in range(CHUNK // SUB):
                            to = pl.ds(2 * (c * CHUNK // SUB + k) + par, SUB, stride=PITCH)
                            ys[row, to, :] = part[k * SUB : k * SUB + SUB]
            for q in range(2):
                for a in range(SUB):
                    yb[slot, 2 * t + q, 2 * SUB * a : 2 * SUB * a + 2 * SUB] = ys[
                        2 * t + q, PITCH * a : PITCH * a + 2 * SUB
                    ].astype(BF)

        for t in range(STEP // 2):
            mix(t)
        stem(s + 1, range(STEP), None, keep_last)

        @pl.when(s == 0)
        def _():
            first.start()

        @pl.when(s > 0)
        def _():
            copy(s, slot).start()
        return carry

    lax.fori_loop(0, BLOCKS, step, 0)
    copy(BLOCKS - 2, (BLOCKS - 2) % 2).wait()
    copy(BLOCKS - 1, (BLOCKS - 1) % 2).wait()


def conv(n_band, pos, g, a, b, core, x, ws, bs, wm, bm, hot):
    channels = bm.shape[-1]
    return pl.pallas_call(
        functools.partial(conv_kernel, n_band - 1),
        in_specs=[SM] + [VM] * 10,
        out_specs=ANY,
        out_shape=jax.ShapeDtypeStruct((ROWS, COLS, channels), BF),
        scratch_shapes=[
            pltpu.VMEM((3, 256, LANES), BF),
            pltpu.VMEM((BLOCKS, 128, 128), BF),
            pltpu.VMEM((BLOCKS, 128, 128), BF),
            pltpu.VMEM((2, STEP, HROWS, 256), BF),
            pltpu.VMEM((STEP, SUB * PITCH, channels), F32),
            pltpu.VMEM((2, STEP, COLS, channels), BF),
            pltpu.SemaphoreType.DMA((2,)),
        ],
        compiler_params=params(20),
        cost_estimate=cost(2 * ROWS * COLS * 9 * 128 * 128, 12 << 20),
        name="conv",
    )(pos, g, a, b, core, x, ws, bs, wm, bm, hot)


def on_device(source, routes, slot_weights, window, stem_weight, stem_bias, mix_weight, mix_bias):
    n_band = lax.axis_size("band")
    n_lon = lax.axis_size("lon")
    axes = ("band", "lon")
    band = lax.axis_index("band")
    lon = lax.axis_index("lon")

    def move(value, way, turn):
        return lax.ppermute(value, axes, swap(n_band, n_lon, way, turn))

    pos = jnp.stack([band, lon]).astype(jnp.int32)
    core_dl = jnp.where(lon % 2 == 0, 3, 1)
    x_dl = 4 - core_dl
    a_base = jnp.where(band % 2 == 0, 0, 8)
    b_base = 8 - a_base
    rim = (band == 0) | (band == n_band - 1)
    far_code = jnp.where(band < n_band // 2, 10, 2)
    near = [4 + 0 * lon, 4 + core_dl, 4 + x_dl]
    along_a = [a_base, a_base + core_dl, a_base + x_dl]
    along_b = [jnp.where(rim, 6, b_base), b_base + core_dl, b_base + x_dl]
    codes = jnp.stack(near + along_a + along_b + [far_code]).astype(jnp.int32)

    turns = ("stay", "core", "x")
    out = pack(pos, routes.T, source)
    arrays = [move(out[3 + i], "a", turn) for i, turn in enumerate(turns)]
    arrays += [move(out[6 + i], "b", turn) for i, turn in enumerate(turns)]
    arrays.append(move(out[9], "a", "across"))
    core, x = move(out[1], "", "core"), move(out[2], "", "x")
    near = near_part(codes, window, out[0], core, x, slot_weights)
    fld, a_row, b_row = far_part(codes, window, pos, arrays, near, slot_weights)
    a_halo = move(a_row, "a", "stay")
    b_halo = move(b_row, "b", "stay")
    g, hot = spread(fld)
    a_halo, b_halo, g, hot = lax.optimization_barrier((a_halo, b_halo, g, hot))
    edge = edges(n_band, pos, fld, a_halo, b_halo)
    core_edge = move(edge, "", "core")
    x_edge = move(edge, "", "x")
    ws, bs, wm = prep(stem_weight, stem_bias, mix_weight)
    return conv(
        n_band, pos, g, a_halo, b_halo, core_edge, x_edge, ws, bs, wm, mix_bias[None], hot
    )


def solution(mesh):
    both = ("band", "lon")
    in_specs = (
        P(both, None, None),
        P(both, None),
        P(both, None, None, None, None),
        P(both, None, None),
        P(),
        P(),
        P(),
        P(),
    )
    return jax.shard_map(
        on_device, mesh=mesh, in_specs=in_specs, out_specs=P("band", "lon", None), check_vma=False
    )
```

time: 57.6 us -> 51.5 us (0.89)
  waiting for transfers between devices: 10.3 us -> 2.82 us
  starting transfers between devices: 10.8 us -> 16.8 us
  local copies, waits for them, and re-layouts: 4.11 us -> 0.78 us
  other arithmetic: 1.47 us -> 0.07 us
    ppermute x9 -> x13, waiting for transfers between devices: 10.3 us -> 2.82 us  [move(): return lax.ppermute(value, axes, swap(n_band, n_lon, way, turn))]
    ppermute x9 -> x13, starting transfers between devices: 10.8 us -> 16.8 us  [move(): return lax.ppermute(value, axes, swap(n_band, n_lon, way, turn))]
    unnamed x13 -> x3, local copies, waits for them, and re-layouts: 4 us -> 0.7 us
    concatenate x2 -> x0, other arithmetic: 1.39 us -> none  [the longest x1 0.7 us: on_device(): b_out = jnp.concatenate([own[64:96], core[64:96], x[64:96]], axis=0)]
    pallas_call x4 -> x5, Pallas kernels: 26.6 us -> 27 us  [the longest x1 17.8 us: conv(): pl.pallas_call(functools.partial(conv_kernel, n_band - 1), in_specs=[SM]...]
  transfers between devices with their start and end apart: 9 -> 13, of which waited for: 5 -> 2; matrix products, arithmetic and copies ran while one was open for 3% -> 2% of each run, Pallas kernels for 7% -> 10%
where the time goes in v3:
time: 51.5 us; the launch traced here: 51.2 us
  Pallas kernels  30.7 us (60%)
  starting transfers between devices  16.8 us (33%)
  waiting for transfers between devices  2.82 us (5%)
  local copies, waits for them, and re-layouts  0.78 us (2%)
    pallas_call x1, Pallas kernels, conv(): pl.pallas_call(functools.partial(conv_kernel, n_band - 1), in_specs=[SM]...  17.8 us
    ppermute x13, starting transfers between devices, move(): return lax.ppermute(value, axes, swap(n_band, n_lon, way, turn))  16.8 us
    pallas_call x1, Pallas kernels, far_part(): pl.pallas_call(far_kernel, in_specs=[SM, SM, SM] + [VM] * 8 + [HBM], out_...  4.24 us
    pallas_call x1, Pallas kernels, near_part(): pl.pallas_call(near_kernel, in_specs=[SM, SM] + [VM] * 3 + [HBM], out_spe...  2.85 us
    ppermute x13, waiting for transfers between devices, move(): return lax.ppermute(value, axes, swap(n_band, n_lon, way, turn))  2.82 us
    pallas_call x1, Pallas kernels, pack(): pl.pallas_call(pack_kernel, in_specs=[SM, HBM, HBM], out_specs=[VM] * 10,...  2.64 us
    pallas_call x1, Pallas kernels, prep(): pl.pallas_call(prep_kernel, in_specs=[VM] * 3, out_specs=[VM] * 3, out_sh...  1.25 us
    pallas_call x1, Pallas kernels, spread(): pl.pallas_call(spread_kernel, in_specs=[VM], out_specs=[VM] * 2, out_shap...  1.09 us
  transfers between devices with their start and end apart: 13, of which 2 were waited for; matrix products, arithmetic and copies ran while one was open for 2% of the time, Pallas kernels for 10%

profile of v3, /device:TPU:0, one launch (start us, length us, event | category | flops | bytes accessed | tf_op | source)
XLA Modules:
  0.0 51.2 jit_solution(6577884160239713028)
XLA Ops:
  0.0 0.1 pad_add_fusion.pos_ref
  0.1 2.6 %pack.1 = (bf16[32,8,128]{2,1,0:T(8,128)(2,1)S(1)}, bf16[32,8,128]{2,1,0:T(8,128)(2,1)S(1)}, bf16[32,8,128]{2,1,0:T(8,128)(2,1)S(1)}, bf16[32,8,128]{2,1,0:T(8,1...) custom-call(s32[2]{0:T(128)S(1)} %pad_add_fusion.pos_ref, ...), custom_call_target="tpu_custom_call" | custom-call | bytes 1048576 | tf_op jit(solution)/shard_map/pack/pallas_call | solution.py:108
  2.7 3.0 %collective-permute-start = (bf16[32,8,128]{2,1,0:T(8,128)(2,1)S(1)}, bf16[32,8,128]{2,1,0:T(8,128)(2,1)S(1)}, u32[]{:S(2)}, u32[]{:S(2)}) collective-permute-start(bf16[32,8,128]{2,1,0:T(8,128)(2,1)S(1)} %get-tuple-element.27), channel_id=1, source_target_pairs={{0,4},{1,5},{2,6},{3,7},{4,0},{5,1},{6,2},{7,3},{8,12},{9,13},{10,... | collective-permute-start | bytes 196616 | tf_op jit(solution)/shard_map/ppermute | solution.py:508
  5.8 0.2 collective-permute-start.7
  5.9 1.5 %collective-permute-start.8 = (bf16[32,8,128]{2,1,0:T(8,128)(2,1)S(1)}, bf16[32,8,128]{2,1,0:T(8,128)(2,1)S(1)}, u32[]{:S(2)}, u32[]{:S(2)}) collective-permute-start(bf16[32,8,128]{2,1,0:T(8,128)(2,1)S(1)} %get-tuple-element.36), channel_id=1, source_target_pairs={{0,3},{1,2},{2,1},{3,0},{4,7},{5,6},{6,5},{7,4},{8,11},{9,10},{10,... | collective-permute-start | bytes 196616 | tf_op jit(solution)/shard_map/ppermute | solution.py:508
  7.5 1.6 %collective-permute-start.2 = (bf16[32,8,128]{2,1,0:T(8,128)(2,1)S(1)}, bf16[32,8,128]{2,1,0:T(8,128)(2,1)S(1)}, u32[]{:S(2)}, u32[]{:S(2)}) collective-permute-start(bf16[32,8,128]{2,1,0:T(8,128)(2,1)S(1)} %get-tuple-element.29), channel_id=1, source_target_pairs={{0,7},{1,6},{2,5},{3,4},{4,3},{5,2},{6,1},{7,0},{8,15},{9,14},{10,... | collective-permute-start | bytes 196616 | tf_op jit(solution)/shard_map/ppermute | solution.py:508
  9.1 1.5 %collective-permute-start.3 = (bf16[32,8,128]{2,1,0:T(8,128)(2,1)S(1)}, bf16[32,8,128]{2,1,0:T(8,128)(2,1)S(1)}, u32[]{:S(2)}, u32[]{:S(2)}) collective-permute-start(bf16[32,8,128]{2,1,0:T(8,128)(2,1)S(1)} %get-tuple-element.30), channel_id=1, source_target_pairs={{0,2},{1,3},{2,0},{3,1},{4,8},{5,9},{6,10},{7,11},{8,4},{9,5},{10,... | collective-permute-start | bytes 196616 | tf_op jit(solution)/shard_map/ppermute | solution.py:508
  10.6 0.8 %collective-permute-start.4 = (bf16[32,8,128]{2,1,0:T(8,128)(2,1)S(1)}, bf16[32,8,128]{2,1,0:T(8,128)(2,1)S(1)}, u32[]{:S(2)}, u32[]{:S(2)}) collective-permute-start(bf16[32,8,128]{2,1,0:T(8,128)(2,1)S(1)} %get-tuple-element.31), channel_id=1, source_target_pairs={{0,2},{1,3},{2,0},{3,1},{4,9},{5,8},{6,11},{7,10},{8,5},{9,4},{10,... | collective-permute-start | bytes 196616 | tf_op jit(solution)/shard_map/ppermute | solution.py:508
  11.4 1.2 %collective-permute-start.5 = (bf16[32,8,128]{2,1,0:T(8,128)(2,1)S(1)}, bf16[32,8,128]{2,1,0:T(8,128)(2,1)S(1)}, u32[]{:S(2)}, u32[]{:S(2)}) collective-permute-start(bf16[32,8,128]{2,1,0:T(8,128)(2,1)S(1)} %get-tuple-element.32), channel_id=1, source_target_pairs={{0,2},{1,3},{2,0},{3,1},{4,11},{5,10},{6,9},{7,8},{8,7},{9,6},{10,... | collective-permute-start | bytes 196616 | tf_op jit(solution)/shard_map/ppermute | solution.py:508
  12.6 3.1 %collective-permute-start.6 = (bf16[32,8,128]{2,1,0:T(8,128)(2,1)S(1)}, bf16[32,8,128]{2,1,0:T(8,128)(2,1)S(1)}, u32[]{:S(2)}, u32[]{:S(2)}) collective-permute-start(bf16[32,8,128]{2,1,0:T(8,128)(2,1)S(1)} %get-tuple-element.33), channel_id=1, source_target_pairs={{0,6},{1,7},{2,4},{3,5},{4,2},{5,3},{6,0},{7,1},{8,14},{9,15},{10,... | collective-permute-start | bytes 196616 | tf_op jit(solution)/shard_map/ppermute | solution.py:508
  15.7 0.7 %copy.10.win_ref = s32[1,12,32]{2,1,0:T(8,128)S(1)} copy(s32[1,12,32]{2,0,1:T(1,128)} %param.11) | data formatting | bytes 3072 | tf_op args[3]
  16.4 0.1 stack.51.codes_ref
  16.5 2.9 %near.1.refs_7_ = f32[256,8,128]{2,1,0:T(8,128)S(1)} custom-call(s32[10]{0:T(128)S(1)} %stack.51.codes_ref, s32[1,12,32]{2,1,0:T(8,128)S(1)} %copy.10.win_ref, bf16[32,8,128]{2,1,0:T(8,128)(2,1)S(1)} %get-tuple-element.34.own_ref, bf16[32,8,128]{2,1,0:T(8,128)(2,1)S(1)} %collective-permute-done.7.core_ref, ...), custom_call_target="tpu_custom_call" | custom-call | flops 25165824 | bytes 4194304 | tf_op jit(solution)/shard_map/near/pallas_call | solution.py:218
  19.4 4.2 %far.1 = (bf16[512,512]{1,0:T(8,128)(2,1)S(1)}, bf16[16,512]{1,0:T(8,128)(2,1)S(1)}, bf16[16,512]{1,0:T(8,128)(2,1)S(1)}) custom-call(s32[10]{0:T(128)S(1)} %stack.51.codes_ref, s32[1,12,32]{2,1,0:T(8,128)S(1)} %copy.10.win_ref, s32[2]{0:T(128)S(1)} %pad_add_fusion.pos_ref, bf16[32,8,128]{2,1,0:T(8,128)(2,1)S(1)} %collective-permute-done.refs_0_, ...), custom_call_target="tpu_custom_call" | custom-call | flops 58720256 | bytes 8388608 | tf_op jit(solution)/shard_map/far/pallas_call | solution.py:235
  23.6 2.0 %collective-permute-start.9 = (bf16[16,512]{1,0:T(8,128)(2,1)S(1)}, bf16[16,512]{1,0:T(8,128)(2,1)S(1)}, u32[]{:S(2)}, u32[]{:S(2)}) collective-permute-start(bf16[16,512]{1,0:T(8,128)(2,1)S(1)} %get-tuple-element.37), channel_id=1, source_target_pairs={{0,4},{1,5},{2,6},{3,7},{4,0},{5,1},{6,2},{7,3},{8,12},{9,13},{10,... | collective-permute-start | bytes 49160 | tf_op jit(solution)/shard_map/ppermute | solution.py:508
  25.6 0.8 %collective-permute-start.10 = (bf16[16,512]{1,0:T(8,128)(2,1)S(1)}, bf16[16,512]{1,0:T(8,128)(2,1)S(1)}, u32[]{:S(2)}, u32[]{:S(2)}) collective-permute-start(bf16[16,512]{1,0:T(8,128)(2,1)S(1)} %get-tuple-element.38), channel_id=1, source_target_pairs={{0,2},{1,3},{2,0},{3,1},{4,8},{5,9},{6,10},{7,11},{8,4},{9,5},{10,... | collective-permute-start | bytes 49160 | tf_op jit(solution)/shard_map/ppermute | solution.py:508
  26.5 1.1 %spread.1 = (bf16[11,256,384]{2,1,0:T(8,128)(2,1)S(1)}, bf16[512,1536]{1,0:T(8,128)(2,1)S(1)}) custom-call(bf16[512,512]{1,0:T(8,128)(2,1)S(1)} %get-tuple-element.39.fld_ref), custom_call_target="tpu_custom_call" | custom-call | flops 805306368 | bytes 4194304 | tf_op jit(solution)/shard_map/spread/pallas_call | solution.py:312
  27.6 1.8 %collective-permute-done.10.b_ref = bf16[16,512]{1,0:T(8,128)(2,1)S(1)} collective-permute-done((bf16[16,512]{1,0:T(8,128)(2,1)S(1)}, bf16[16,512]{1,0:T(8,128)(2,1)S(1)}, u32[]{:S(2)}, u32[]{:S(2)}) %collective-permute-start.10) | collective-permute-done | bytes 16416 | tf_op jit(solution)/shard_map/ppermute | solution.py:508
  29.4 0.8 %edges.1 = bf16[16,544]{1,0:T(8,128)(2,1)S(1)} custom-call(s32[2]{0:T(128)S(1)} %pad_add_fusion.pos_ref, bf16[512,512]{1,0:T(8,128)(2,1)S(1)} %get-tuple-element.39.fld_ref, bf16[16,512]{1,0:T(8,128)(2,1)S(1)} %collective-permute-done.9.a_ref, bf16[16,512]{1,0:T(8,128)(2,1)S(1)} %collective-permute-done.10.b_ref), custom_call_target="tpu_custom_call" | custom-call | bytes 1048576 | tf_op jit(solution)/shard_map/edges/pallas_call | solution.py:276
  30.2 0.1 collective-permute-start.12
  30.2 0.9 %collective-permute-start.11 = (bf16[16,544]{1,0:T(8,128)(2,1)S(1)}, bf16[16,544]{1,0:T(8,128)(2,1)S(1)}, u32[]{:S(2)}, u32[]{:S(2)}) collective-permute-start(bf16[16,544]{1,0:T(8,128)(2,1)S(1)} %edges.1), channel_id=1, source_target_pairs={{0,1},{1,0},{2,3},{3,2},{4,5},{5,4},{6,7},{7,6},{8,9},{9,8},{10,11... | collective-permute-start | bytes 52232 | tf_op jit(solution)/shard_map/ppermute | solution.py:508
  31.2 1.2 %prep.1 = (bf16[256,1536]{1,0:T(8,128)(2,1)S(1)}, f32[1,256]{1,0:T(1,128)S(1)}, bf16[4,512,256]{2,1,0:T(8,128)(2,1)S(1)}) custom-call(bf16[9,8,128]{2,1,0:T(8,128)(2,1)} %stem_ref.1, f32[1,128]{1,0:T(1,128)} %bitcast.16, bf16[9,128,128]{2,1,0:T(8,128)(2,1)} %mix_ref.1), custom_call_target="tpu_custom_call" | custom-call | bytes 2097152 | tf_op jit(solution)/shard_map/prep/pallas_call | solution.py:156
  32.4 1.0 %collective-permute-done.12.x_ref = bf16[16,544]{1,0:T(8,128)(2,1)S(1)} collective-permute-done((bf16[16,544]{1,0:T(8,128)(2,1)S(1)}, bf16[16,544]{1,0:T(8,128)(2,1)S(1)}, u32[]{:S(2)}, u32[]{:S(2)}) %collective-permute-start.12) | collective-permute-done | bytes 17440 | tf_op jit(solution)/shard_map/ppermute | solution.py:508
  33.4 17.8 %conv.1 = bf16[64,512,128]{2,1,0:T(8,128)(2,1)} custom-call(s32[2]{0:T(128)S(1)} %pad_add_fusion.pos_ref, bf16[11,256,384]{2,1,0:T(8,128)(2,1)S(1)} %get-tuple-element.42.g_ref, bf16[16,512]{1,0:T(8,128)(2,1)S(1)} %collective-permute-done.9.a_ref, bf16[16,512]{1,0:T(8,128)(2,1)S(1)} %collective-permute-done.10.b_ref, ...), custom_call_target="tpu_custom_call" | custom-call | flops 9663676416 | bytes 12582912 | tf_op jit(solution)/shard_map/conv/pallas_call | solution.py:480
  (14 shorter events, 0.0 us)
Async XLA Ops:
  2.7 6.4 %collective-permute-start = (bf16[32,8,128]{2,1,0:T(8,128)(2,1)S(1)}, bf16[32,8,128]{2,1,0:T(8,128)(2,1)S(1)}, u32[]{:S(2)}, u32[]{:S(2)}) collective-permute-start(bf16[32,8,128]{2,1,0:T(8,128)(2,1)S(1)} %get-tuple-element.27), channel_id=1, source_target_pairs={{0,4},{1,5},{2,6},{3,7},{4,0},{5,1},{6,2},{7,3},{8,12},{9,13},{10,... | collective-permute-start | bytes 196616 | tf_op jit(solution)/shard_map/ppermute | solution.py:508
  5.8 4.8 %collective-permute-start.1 = (bf16[32,8,128]{2,1,0:T(8,128)(2,1)S(1)}, bf16[32,8,128]{2,1,0:T(8,128)(2,1)S(1)}, u32[]{:S(2)}, u32[]{:S(2)}) collective-permute-start(bf16[32,8,128]{2,1,0:T(8,128)(2,1)S(1)} %get-tuple-element.28), channel_id=1, source_target_pairs={{0,5},{1,4},{2,7},{3,6},{4,1},{5,0},{6,3},{7,2},{8,13},{9,12},{10,... | collective-permute-start | bytes 196616 | tf_op jit(solution)/shard_map/ppermute | solution.py:508
  5.8 5.6 %collective-permute-start.7 = (bf16[32,8,128]{2,1,0:T(8,128)(2,1)S(1)}, bf16[32,8,128]{2,1,0:T(8,128)(2,1)S(1)}, u32[]{:S(2)}, u32[]{:S(2)}) collective-permute-start(bf16[32,8,128]{2,1,0:T(8,128)(2,1)S(1)} %get-tuple-element.35), channel_id=1, source_target_pairs={{0,1},{1,0},{2,3},{3,2},{4,5},{5,4},{6,7},{7,6},{8,9},{9,8},{10,11... | collective-permute-start | bytes 196616 | tf_op jit(solution)/shard_map/ppermute | solution.py:508
  5.9 6.7 %collective-permute-start.8 = (bf16[32,8,128]{2,1,0:T(8,128)(2,1)S(1)}, bf16[32,8,128]{2,1,0:T(8,128)(2,1)S(1)}, u32[]{:S(2)}, u32[]{:S(2)}) collective-permute-start(bf16[32,8,128]{2,1,0:T(8,128)(2,1)S(1)} %get-tuple-element.36), channel_id=1, source_target_pairs={{0,3},{1,2},{2,1},{3,0},{4,7},{5,6},{6,5},{7,4},{8,11},{9,10},{10,... | collective-permute-start | bytes 196616 | tf_op jit(solution)/shard_map/ppermute | solution.py:508
  7.5 11.9 %collective-permute-start.2 = (bf16[32,8,128]{2,1,0:T(8,128)(2,1)S(1)}, bf16[32,8,128]{2,1,0:T(8,128)(2,1)S(1)}, u32[]{:S(2)}, u32[]{:S(2)}) collective-permute-start(bf16[32,8,128]{2,1,0:T(8,128)(2,1)S(1)} %get-tuple-element.29), channel_id=1, source_target_pairs={{0,7},{1,6},{2,5},{3,4},{4,3},{5,2},{6,1},{7,0},{8,15},{9,14},{10,... | collective-permute-start | bytes 196616 | tf_op jit(solution)/shard_map/ppermute | solution.py:508
  9.1 10.3 %collective-permute-start.3 = (bf16[32,8,128]{2,1,0:T(8,128)(2,1)S(1)}, bf16[32,8,128]{2,1,0:T(8,128)(2,1)S(1)}, u32[]{:S(2)}, u32[]{:S(2)}) collective-permute-start(bf16[32,8,128]{2,1,0:T(8,128)(2,1)S(1)} %get-tuple-element.30), channel_id=1, source_target_pairs={{0,2},{1,3},{2,0},{3,1},{4,8},{5,9},{6,10},{7,11},{8,4},{9,5},{10,... | collective-permute-start | bytes 196616 | tf_op jit(solution)/shard_map/ppermute | solution.py:508
  10.6 8.8 %collective-permute-start.4 = (bf16[32,8,128]{2,1,0:T(8,128)(2,1)S(1)}, bf16[32,8,128]{2,1,0:T(8,128)(2,1)S(1)}, u32[]{:S(2)}, u32[]{:S(2)}) collective-permute-start(bf16[32,8,128]{2,1,0:T(8,128)(2,1)S(1)} %get-tuple-element.31), channel_id=1, source_target_pairs={{0,2},{1,3},{2,0},{3,1},{4,9},{5,8},{6,11},{7,10},{8,5},{9,4},{10,... | collective-permute-start | bytes 196616 | tf_op jit(solution)/shard_map/ppermute | solution.py:508
  11.4 8.0 %collective-permute-start.5 = (bf16[32,8,128]{2,1,0:T(8,128)(2,1)S(1)}, bf16[32,8,128]{2,1,0:T(8,128)(2,1)S(1)}, u32[]{:S(2)}, u32[]{:S(2)}) collective-permute-start(bf16[32,8,128]{2,1,0:T(8,128)(2,1)S(1)} %get-tuple-element.32), channel_id=1, source_target_pairs={{0,2},{1,3},{2,0},{3,1},{4,11},{5,10},{6,9},{7,8},{8,7},{9,6},{10,... | collective-permute-start | bytes 196616 | tf_op jit(solution)/shard_map/ppermute | solution.py:508
  12.6 6.8 %collective-permute-start.6 = (bf16[32,8,128]{2,1,0:T(8,128)(2,1)S(1)}, bf16[32,8,128]{2,1,0:T(8,128)(2,1)S(1)}, u32[]{:S(2)}, u32[]{:S(2)}) collective-permute-start(bf16[32,8,128]{2,1,0:T(8,128)(2,1)S(1)} %get-tuple-element.33), channel_id=1, source_target_pairs={{0,6},{1,7},{2,4},{3,5},{4,2},{5,3},{6,0},{7,1},{8,14},{9,15},{10,... | collective-permute-start | bytes 196616 | tf_op jit(solution)/shard_map/ppermute | solution.py:508
  19.3 14.1 %copy-start = (f32[128]{0:T(128)S(1)}, f32[128]{0:T(128)}, u32[]{:S(2)}) copy-start(f32[128]{0:T(128)} %param.15) | copy-start | bytes 1540
  23.6 3.9 %collective-permute-start.9 = (bf16[16,512]{1,0:T(8,128)(2,1)S(1)}, bf16[16,512]{1,0:T(8,128)(2,1)S(1)}, u32[]{:S(2)}, u32[]{:S(2)}) collective-permute-start(bf16[16,512]{1,0:T(8,128)(2,1)S(1)} %get-tuple-element.37), channel_id=1, source_target_pairs={{0,4},{1,5},{2,6},{3,7},{4,0},{5,1},{6,2},{7,3},{8,12},{9,13},{10,... | collective-permute-start | bytes 49160 | tf_op jit(solution)/shard_map/ppermute | solution.py:508
  25.6 3.7 %collective-permute-start.10 = (bf16[16,512]{1,0:T(8,128)(2,1)S(1)}, bf16[16,512]{1,0:T(8,128)(2,1)S(1)}, u32[]{:S(2)}, u32[]{:S(2)}) collective-permute-start(bf16[16,512]{1,0:T(8,128)(2,1)S(1)} %get-tuple-element.38), channel_id=1, source_target_pairs={{0,2},{1,3},{2,0},{3,1},{4,8},{5,9},{6,10},{7,11},{8,4},{9,5},{10,... | collective-permute-start | bytes 49160 | tf_op jit(solution)/shard_map/ppermute | solution.py:508
  30.2 3.3 %collective-permute-start.12 = (bf16[16,544]{1,0:T(8,128)(2,1)S(1)}, bf16[16,544]{1,0:T(8,128)(2,1)S(1)}, u32[]{:S(2)}, u32[]{:S(2)}) collective-permute-start(bf16[16,544]{1,0:T(8,128)(2,1)S(1)} %edges.1), channel_id=1, source_target_pairs={{0,3},{1,2},{2,1},{3,0},{4,7},{5,6},{6,5},{7,4},{8,11},{9,10},{10,... | collective-permute-start | bytes 52232 | tf_op jit(solution)/shard_map/ppermute | solution.py:508
  30.2 3.2 %collective-permute-start.11 = (bf16[16,544]{1,0:T(8,128)(2,1)S(1)}, bf16[16,544]{1,0:T(8,128)(2,1)S(1)}, u32[]{:S(2)}, u32[]{:S(2)}) collective-permute-start(bf16[16,544]{1,0:T(8,128)(2,1)S(1)} %edges.1), channel_id=1, source_target_pairs={{0,1},{1,0},{2,3},{3,2},{4,5},{5,4},{6,7},{7,6},{8,9},{9,8},{10,11... | collective-permute-start | bytes 52232 | tf_op jit(solution)/shard_map/ppermute | solution.py:508

commit v4 on v3

--- a/solution.py
+++ b/solution.py
@@ -15,6 +15,8 @@
 PITCH = 2 * SUB + 1
 LANES = 384
 CHUNK = 256
+NEAR, FAR = 3, 7
+EARLY = 4
 STEP = 6
 BLOCKS = (ROWS + 2) // STEP
 SCALE = 1.0 / 2.0
@@ -46,7 +48,8 @@
         for l in range(n_lon):
             target = {"stay": l, "core": l ^ 1, "x": n_lon - 1 - l, "across": (l + 2) % n_lon}[turn]
             if not 0 <= partner < n_band:
-                pairs.append((b * n_lon + l, b * n_lon + (l + 2) % n_lon))
+                spare = (l + 2) % n_lon if turn == "stay" else l ^ 1
+                pairs.append((b * n_lon + l, b * n_lon + spare))
             else:
                 pairs.append((b * n_lon + l, partner * n_lon + target))
     return pairs
@@ -56,18 +59,15 @@
     return [pltpu.with_memory_space_constraint(a, pltpu.HBM) for a in arrays]
 
 
-def pack_kernel(
-    pos_ref, routes_hbm, src_hbm, *refs
-):
-    outs, (routes_ref, src_ref, buf, table, count, sem) = refs[:10], refs[10:]
+def pack_kernel(routes_hbm, src_hbm, *refs):
+    outs, (routes_ref, src_ref, buf, place, sem) = refs[:10], refs[10:]
     copies = [
         pltpu.make_async_copy(routes_hbm, routes_ref, sem.at[0]),
         pltpu.make_async_copy(src_hbm, src_ref, sem.at[1]),
     ]
     for copy in copies:
         copy.start()
-    band = pos_ref[0]
-    lon = pos_ref[1]
+    band, lon = lax.axis_index("band"), lax.axis_index("lon")
     a_dir = 1 - 2 * (band % 2)
     core_dl = 1 + 2 * (lon % 2)
     for q in range(12):
@@ -82,8 +82,7 @@
             group = 6 if db == 0 else 9
         else:
             group = jnp.where(core_dl == dl, 1, 2) + way
-        table[q] = group * 32
-        count[q] = 0
+        place[q] = group * 32
     buf[...] = jnp.zeros_like(buf)
     for copy in copies:
         copy.wait()
@@ -92,9 +91,9 @@
         block = src_ref[j]
         for t in range(2):
             q = routes_ref[t, j]
-            rank = count[q]
-            count[q] = rank + 1
-            buf[table[q] + rank] = block
+            at = place[q]
+            place[q] = at + 1
+            buf[at] = block
         return carry
 
     lax.fori_loop(0, src_ref.shape[0], one, 0, unroll=8)
@@ -102,12 +101,12 @@
         out[...] = buf[group * 32 : group * 32 + 32]
 
 
-def pack(pos, routes, source):
+def pack(routes, source):
     fields, cells = source.shape[1:]
     shape = lambda n: jax.ShapeDtypeStruct((n, fields, cells), BF)
     return pl.pallas_call(
         pack_kernel,
-        in_specs=[SM, HBM, HBM],
+        in_specs=[HBM, HBM],
         out_specs=[VM] * 10,
         out_shape=[shape(32)] * 10,
         scratch_shapes=[
@@ -115,13 +114,12 @@
             pltpu.VMEM(source.shape, BF),
             pltpu.VMEM((320, fields, cells), BF),
             pltpu.SMEM((12,), jnp.int32),
-            pltpu.SMEM((12,), jnp.int32),
             pltpu.SemaphoreType.DMA((2,)),
         ],
         compiler_params=params(16),
         cost_estimate=cost(0, 1 << 20),
         name="pack",
-    )(pos, *in_hbm(routes, source))
+    )(*in_hbm(routes, source))
 
 
 def prep_kernel(stem_ref, bias_ref, mix_ref, ws_ref, bs_ref, wm_ref):
@@ -168,73 +166,128 @@
     )(*in_hbm(stem_weight, stem_bias[None], mix_weight))
 
 
-def add_groups(codes_ref, win_ref, w_hbm, w_ref, sem, inc, acc, arrays, first):
-    def copy(g):
-        return pltpu.make_async_copy(w_hbm.at[0, codes_ref[first + g]], w_ref.at[g], sem.at[g])
-
-    for g in range(len(arrays)):
-        copy(g).start()
-    for g, array in enumerate(arrays):
-        inc[g] = array[...]
-
-    def group(g, carry):
-        copy(g).wait()
-        q = codes_ref[first + g]
+def group_codes(last, codes_ref):
+    band, lon = lax.axis_index("band"), lax.axis_index("lon")
+    core_dl = jnp.where(lon % 2 == 0, 3, 1)
+    x_dl = 4 - core_dl
+    a_base = jnp.where(band % 2 == 0, 0, 8)
+    b_base = 8 - a_base
+    rim = (band == 0) | (band == last)
+    codes = [4, 4 + core_dl, 4 + x_dl]
+    codes += [a_base, a_base + core_dl, a_base + x_dl]
+    codes += [jnp.where(rim, 6, b_base), b_base + core_dl, b_base + x_dl]
+    codes.append(jnp.where(band < (last + 1) // 2, 10, 2))
+    for g, code in enumerate(codes):
+        codes_ref[g] = jnp.int32(code)
+
+
+def add_groups(codes_ref, win_ref, w_ref, inc, acc, first, begin, count, ready=None):
+    def group(i, carry):
+        if ready is not None:
+            ready(i)
+        q = codes_ref[first + begin + i]
         for s in range(0, 32, 2):
             pair = jnp.dot(
-                inc[g, s : s + 2].reshape(16, 128),
-                jnp.concatenate([w_ref[g, s], w_ref[g, s + 1]], axis=1),
+                inc[begin + i, s : s + 2].reshape(16, 128),
+                jnp.concatenate([w_ref[i, s], w_ref[i, s + 1]], axis=1),
                 preferred_element_type=F32,
             )
-            for i in range(2):
-                part = pair[8 * i : 8 * i + 8, 128 * i : 128 * i + 128]
-                w = win_ref[0, q, s + i]
+            for k in range(2):
+                part = pair[8 * k : 8 * k + 8, 128 * k : 128 * k + 128]
+                w = win_ref[q, 0, s + k]
                 place = (w % 4) * ROWS + w // 4
                 acc[place] = acc[place] + part.astype(BF).astype(F32)
         return carry
 
-    lax.fori_loop(0, len(arrays), group, 0)
-
-
-def near_kernel(codes_ref, win_ref, own_ref, core_ref, x_ref, w_hbm, acc, w_ref, inc, sem):
+    lax.fori_loop(0, count, group, 0)
+
+
+def near_kernel(last, win_hbm, own_ref, core_ref, x_ref, w_hbm, acc, early_ref, w_ref, inc, codes_ref, win_ref, sem, early_sem, win_sem):
+    group_codes(last, codes_ref)
+    window = pltpu.make_async_copy(win_hbm, win_ref, win_sem)
+    window.start()
+
+    def copy(g):
+        return pltpu.make_async_copy(w_hbm.at[0, codes_ref[g]], w_ref.at[g], sem.at[g])
+
+    early = [
+        pltpu.make_async_copy(w_hbm.at[0, codes_ref[NEAR + g]], early_ref.at[g], early_sem.at[g])
+        for g in range(EARLY)
+    ]
+    for g in range(NEAR):
+        copy(g).start()
+    for transfer in early:
+        transfer.start()
     acc[...] = jnp.zeros_like(acc)
-    add_groups(codes_ref, win_ref, w_hbm, w_ref, sem, inc, acc, [own_ref, core_ref, x_ref], 0)
-
-
-def far_kernel(codes_ref, win_ref, pos_ref, *refs):
-    arrays, (near_ref, w_hbm, fld_ref, a_ref, b_ref, acc, w_ref, inc, sem) = refs[:7], refs[7:]
+    for g, array in enumerate((own_ref, core_ref, x_ref)):
+        inc[g] = array[...]
+    window.wait()
+    add_groups(codes_ref, win_ref, w_ref, inc, acc, 0, 0, NEAR, lambda g: copy(g).wait())
+    for transfer in early:
+        transfer.wait()
+
+
+def far_kernel(last, win_hbm, *refs):
+    arrays, (near_ref, early_ref, w_hbm, fld_ref, a_ref, b_ref) = refs[:7], refs[7:13]
+    acc, w_ref, inc, codes_ref, win_ref, sem, win_sem = refs[13:]
+    group_codes(last, codes_ref)
+    window = pltpu.make_async_copy(win_hbm, win_ref, win_sem)
+    window.start()
+
+    def copy(g):
+        return pltpu.make_async_copy(
+            w_hbm.at[0, codes_ref[NEAR + EARLY + g]], w_ref.at[g], sem.at[g]
+        )
+
+    for g in range(FAR - EARLY):
+        copy(g).start()
     acc[...] = near_ref[...]
-    add_groups(codes_ref, win_ref, w_hbm, w_ref, sem, inc, acc, arrays, 3)
+    for g, array in enumerate(arrays):
+        inc[g] = array[...]
+    window.wait()
+    add_groups(codes_ref, win_ref, early_ref, inc, acc, NEAR, 0, EARLY)
+    add_groups(
+        codes_ref, win_ref, w_ref, inc, acc, NEAR, EARLY, FAR - EARLY, lambda g: copy(g).wait()
+    )
     for cb in range(4):
         rows = acc[cb * ROWS : (cb + 1) * ROWS].reshape(ROWS * 8, 128)
         fld_ref[:, cb * 128 : cb * 128 + 128] = rows.astype(BF)
-    even = pos_ref[0] % 2 == 0
+    even = lax.axis_index("band") % 2 == 0
     top, bottom = fld_ref[0:16], fld_ref[ROWS * 8 - 16 : ROWS * 8]
     a_ref[...] = jnp.where(even, bottom, top)
     b_ref[...] = jnp.where(even, top, bottom)
 
 
-def near_part(codes, win, own, core, x, weights):
+def near_part(n_band, win, own, core, x, weights):
+    group = weights.shape[2:]
     return pl.pallas_call(
-        near_kernel,
-        in_specs=[SM, SM] + [VM] * 3 + [HBM],
-        out_specs=VM,
-        out_shape=jax.ShapeDtypeStruct((ROWS * 4, 8, 128), F32),
+        functools.partial(near_kernel, n_band - 1),
+        in_specs=[HBM] + [VM] * 3 + [HBM],
+        out_specs=[VM] * 2,
+        out_shape=[
+            jax.ShapeDtypeStruct((ROWS * 4, 8, 128), F32),
+            jax.ShapeDtypeStruct((EARLY,) + group, BF),
+        ],
         scratch_shapes=[
-            pltpu.VMEM((3,) + weights.shape[2:], BF),
-            pltpu.VMEM((3, 32, 8, 128), BF),
-            pltpu.SemaphoreType.DMA((3,)),
-        ],
-        compiler_params=params(12),
-        cost_estimate=cost(96 * 2 * 8 * 128 * 128, 4 << 20),
+            pltpu.VMEM((NEAR,) + group, BF),
+            pltpu.VMEM((NEAR, 32, 8, 128), BF),
+            pltpu.SMEM((NEAR + FAR,), jnp.int32),
+            pltpu.SMEM(win.shape, jnp.int32),
+            pltpu.SemaphoreType.DMA((NEAR,)),
+            pltpu.SemaphoreType.DMA((EARLY,)),
+            pltpu.SemaphoreType.DMA,
+        ],
+        compiler_params=params(14),
+        cost_estimate=cost(96 * 2 * 8 * 128 * 128, 12 << 20),
         name="near",
-    )(codes, win, own, core, x, *in_hbm(weights))
-
-
-def far_part(codes, win, pos, arrays, near, weights):
+    )(*in_hbm(win), own, core, x, *in_hbm(weights))
+
+
+def far_part(n_band, win, arrays, near, early, weights):
+    group = weights.shape[2:]
     return pl.pallas_call(
-        far_kernel,
-        in_specs=[SM, SM, SM] + [VM] * 8 + [HBM],
+        functools.partial(far_kernel, n_band - 1),
+        in_specs=[HBM] + [VM] * 9 + [HBM],
         out_specs=[VM] * 3,
         out_shape=[
             jax.ShapeDtypeStruct((ROWS * 8, COLS), BF),
@@ -243,45 +296,49 @@
         ],
         scratch_shapes=[
             pltpu.VMEM((ROWS * 4, 8, 128), F32),
-            pltpu.VMEM((7,) + weights.shape[2:], BF),
-            pltpu.VMEM((7, 32, 8, 128), BF),
-            pltpu.SemaphoreType.DMA((7,)),
-        ],
-        compiler_params=params(16),
+            pltpu.VMEM((FAR - EARLY,) + group, BF),
+            pltpu.VMEM((FAR, 32, 8, 128), BF),
+            pltpu.SMEM((NEAR + FAR,), jnp.int32),
+            pltpu.SMEM(win.shape, jnp.int32),
+            pltpu.SemaphoreType.DMA((FAR - EARLY,)),
+            pltpu.SemaphoreType.DMA,
+        ],
+        compiler_params=params(14),
         cost_estimate=cost(224 * 2 * 8 * 128 * 128, 8 << 20),
         name="far",
-    )(codes, win, pos, *arrays, near, *in_hbm(weights))
-
-
-def tall(fld_ref, a, b, band, last):
+    )(*in_hbm(win), *arrays, near, early, *in_hbm(weights))
+
+
+def edge_kernel(last, fld_ref, a_ref, b_ref, edge_ref):
+    band = lax.axis_index("band")
+    a, b = a_ref[...], b_ref[...]
+    b = jnp.where((band == 0) | (band == last), jnp.zeros_like(b), b)
     even = band % 2 == 0
-    b = jnp.where((band == 0) | (band == last), jnp.zeros_like(b), b)
-    north = jnp.where(even, b, a)
-    south = jnp.where(even, a, b)
-    return jnp.concatenate([north, fld_ref[...], south], axis=0)
-
-
-def edge_kernel(last, pos_ref, fld_ref, a_ref, b_ref, edge_ref):
-    whole = tall(fld_ref, a_ref[...], b_ref[...], pos_ref[0], last)
-    rank = lax.broadcasted_iota(jnp.int32, (16, COLS), 0)
-    col = lax.broadcasted_iota(jnp.int32, (16, COLS), 1)
-    pick = ((rank < 2) & (col == rank)) | ((rank >= 2) & (rank < 4) & (col == COLS - 4 + rank))
-    pick = jnp.where(pick, 1.0, 0.0).astype(BF)
+    north, south = jnp.where(even, b, a), jnp.where(even, a, b)
+    ends = []
+    for lanes in (slice(0, 128), slice(COLS - 128, COLS)):
+        ends.append(jnp.concatenate([north[:, lanes], fld_ref[:, lanes], south[:, lanes]], axis=0))
+    rank = lax.broadcasted_iota(jnp.int32, (16, 256), 0)
+    col = lax.broadcasted_iota(jnp.int32, (16, 256), 1)
+    pick = ((rank < 2) & (col == rank)) | ((rank >= 2) & (rank < 4) & (col == 252 + rank))
     edge_ref[...] = lax.dot_general(
-        pick, whole, (((1,), (1,)), ((), ())), preferred_element_type=F32
+        jnp.where(pick, 1.0, 0.0).astype(BF),
+        jnp.concatenate(ends, axis=1),
+        (((1,), (1,)), ((), ())),
+        preferred_element_type=F32,
     ).astype(BF)
 
 
-def edges(n_band, pos, fld, a, b):
+def edges(n_band, fld, a, b):
     return pl.pallas_call(
         functools.partial(edge_kernel, n_band - 1),
-        in_specs=[SM, VM, VM, VM],
+        in_specs=[VM, VM, VM],
         out_specs=VM,
         out_shape=jax.ShapeDtypeStruct((16, (ROWS + 4) * 8), BF),
         compiler_params=params(8),
         cost_estimate=cost(0, 1 << 20),
         name="edges",
-    )(pos, fld, a, b)
+    )(fld, a, b)
 
 
 def spread_kernel(fld_ref, g_ref, hot_ref):
@@ -323,8 +380,8 @@
     )(fld)
 
 
-def halos(last, pos_ref, a_ref, b_ref, core_ref, x_ref, hot_ref, rim, left_ref, right_ref):
-    band = pos_ref[0]
+def halos(last, a_ref, b_ref, core_ref, x_ref, hot_ref, rim, left_ref, right_ref):
+    band = lax.axis_index("band")
     a, b = a_ref[...], b_ref[...]
     b = jnp.where((band == 0) | (band == last), jnp.zeros_like(b), b)
     even = band % 2 == 0
@@ -340,7 +397,7 @@
                 part = value[:, half * 128 : half * 128 + 128]
                 rim[0, d0 : d0 + 16, lanes] = part[0:16]
                 rim[1, d0 + 48 : d0 + 64, lanes] = part[16:32]
-    even = pos_ref[1] % 2 == 0
+    even = lax.axis_index("lon") % 2 == 0
     core, x = core_ref[...].astype(F32), x_ref[...].astype(F32)
     right, left = jnp.where(even, core, x), jnp.where(even, x, core)
     hr = lax.broadcasted_iota(jnp.int32, (16, 256), 0)
@@ -362,7 +419,6 @@
 
 def conv_kernel(
     last,
-    pos_ref,
     g_ref,
     a_ref,
     b_ref,
@@ -382,7 +438,7 @@
     yb,
     sem,
 ):
-    band = pos_ref[0]
+    band = lax.axis_index("band")
 
     def stem(block, which, low, high):
         block_in = jnp.minimum(block, BLOCKS - 1)
@@ -406,7 +462,7 @@
                 h = h * high
             hs[block % 2, i] = h.astype(BF)
 
-    halos(last, pos_ref, a_ref, b_ref, core_ref, x_ref, hot_ref, rim, left_ref, right_ref)
+    halos(last, a_ref, b_ref, core_ref, x_ref, hot_ref, rim, left_ref, right_ref)
     stem(0, range(STEP), jnp.where(band == 0, 0.0, 1.0), None)
 
     def copy(at, slot):
@@ -475,11 +531,11 @@
     copy(BLOCKS - 1, (BLOCKS - 1) % 2).wait()
 
 
-def conv(n_band, pos, g, a, b, core, x, ws, bs, wm, bm, hot):
+def conv(n_band, g, a, b, core, x, ws, bs, wm, bm, hot):
     channels = bm.shape[-1]
     return pl.pallas_call(
         functools.partial(conv_kernel, n_band - 1),
-        in_specs=[SM] + [VM] * 10,
+        in_specs=[VM] * 10,
         out_specs=ANY,
         out_shape=jax.ShapeDtypeStruct((ROWS, COLS, channels), BF),
         scratch_shapes=[
@@ -494,49 +550,36 @@
         compiler_params=params(20),
         cost_estimate=cost(2 * ROWS * COLS * 9 * 128 * 128, 12 << 20),
         name="conv",
-    )(pos, g, a, b, core, x, ws, bs, wm, bm, hot)
+    )(g, a, b, core, x, ws, bs, wm, bm, hot)
 
 
 def on_device(source, routes, slot_weights, window, stem_weight, stem_bias, mix_weight, mix_bias):
     n_band = lax.axis_size("band")
     n_lon = lax.axis_size("lon")
     axes = ("band", "lon")
-    band = lax.axis_index("band")
-    lon = lax.axis_index("lon")
 
     def move(value, way, turn):
         return lax.ppermute(value, axes, swap(n_band, n_lon, way, turn))
 
-    pos = jnp.stack([band, lon]).astype(jnp.int32)
-    core_dl = jnp.where(lon % 2 == 0, 3, 1)
-    x_dl = 4 - core_dl
-    a_base = jnp.where(band % 2 == 0, 0, 8)
-    b_base = 8 - a_base
-    rim = (band == 0) | (band == n_band - 1)
-    far_code = jnp.where(band < n_band // 2, 10, 2)
-    near = [4 + 0 * lon, 4 + core_dl, 4 + x_dl]
-    along_a = [a_base, a_base + core_dl, a_base + x_dl]
-    along_b = [jnp.where(rim, 6, b_base), b_base + core_dl, b_base + x_dl]
-    codes = jnp.stack(near + along_a + along_b + [far_code]).astype(jnp.int32)
-
     turns = ("stay", "core", "x")
-    out = pack(pos, routes.T, source)
+    out = pack(routes.T, source)
+    win = window.transpose(1, 0, 2)
     arrays = [move(out[3 + i], "a", turn) for i, turn in enumerate(turns)]
     arrays += [move(out[6 + i], "b", turn) for i, turn in enumerate(turns)]
     arrays.append(move(out[9], "a", "across"))
     core, x = move(out[1], "", "core"), move(out[2], "", "x")
-    near = near_part(codes, window, out[0], core, x, slot_weights)
-    fld, a_row, b_row = far_part(codes, window, pos, arrays, near, slot_weights)
+    near, early = near_part(n_band, win, out[0], core, x, slot_weights)
+    fld, a_row, b_row = far_part(n_band, win, arrays, near, early, slot_weights)
     a_halo = move(a_row, "a", "stay")
     b_halo = move(b_row, "b", "stay")
     g, hot = spread(fld)
     a_halo, b_halo, g, hot = lax.optimization_barrier((a_halo, b_halo, g, hot))
-    edge = edges(n_band, pos, fld, a_halo, b_halo)
+    edge = edges(n_band, fld, a_halo, b_halo)
     core_edge = move(edge, "", "core")
     x_edge = move(edge, "", "x")
     ws, bs, wm = prep(stem_weight, stem_bias, mix_weight)
     return conv(
-        n_band, pos, g, a_halo, b_halo, core_edge, x_edge, ws, bs, wm, mix_bias[None], hot
+        n_band, g, a_halo, b_halo, core_edge, x_edge, ws, bs, wm, mix_bias[None], hot
     )
 
 

time: 51.5 us -> 47.7 us (0.926)
  Pallas kernels: 30.7 us -> 27.7 us
  local copies, waits for them, and re-layouts: 0.78 us -> 0.01 us
  waiting for transfers between devices: 2.82 us -> 3.38 us
    pallas_call x5, Pallas kernels: 28.3 us -> 25.4 us  [the longest x1 16.9 us: conv(): pl.pallas_call(functools.partial(conv_kernel, n_band - 1), in_specs=[VM]...]
    unnamed x3 -> x2, local copies, waits for them, and re-layouts: 0.7 us -> 0.01 us
    ppermute x13, waiting for transfers between devices: 2.82 us -> 3.38 us  [move(): return lax.ppermute(value, axes, swap(n_band, n_lon, way, turn))]
  transfers between devices with their start and end apart: 13 -> 13, of which waited for: 2 -> 3; matrix products, arithmetic and copies ran while one was open for 2% -> 0% of each run, Pallas kernels for 10% -> 12%
where the time goes in v4:
time: 47.7 us; the launch traced here: 47.6 us
  Pallas kernels  27.7 us (58%)
  starting transfers between devices  16.4 us (34%)
  waiting for transfers between devices  3.38 us (7%)
    pallas_call x1, Pallas kernels, conv(): pl.pallas_call(functools.partial(conv_kernel, n_band - 1), in_specs=[VM]...  16.9 us
    ppermute x13, starting transfers between devices, move(): return lax.ppermute(value, axes, swap(n_band, n_lon, way, turn))  16.4 us
    ppermute x13, waiting for transfers between devices, move(): return lax.ppermute(value, axes, swap(n_band, n_lon, way, turn))  3.38 us
    pallas_call x1, Pallas kernels, near_part(): pl.pallas_call(functools.partial(near_kernel, n_band - 1), in_specs=[HBM]...  3.18 us
    pallas_call x1, Pallas kernels, far_part(): pl.pallas_call(functools.partial(far_kernel, n_band - 1), in_specs=[HBM]...  3.02 us
    pallas_call x1, Pallas kernels, pack(): pl.pallas_call(pack_kernel, in_specs=[HBM, HBM], out_specs=[VM] * 10, out...  2.09 us
    pallas_call x1, Pallas kernels, prep(): pl.pallas_call(prep_kernel, in_specs=[VM] * 3, out_specs=[VM] * 3, out_sh...  1.25 us
    pallas_call x1, Pallas kernels, spread(): pl.pallas_call(spread_kernel, in_specs=[VM], out_specs=[VM] * 2, out_shap...  1.08 us
  transfers between devices with their start and end apart: 13, of which 3 were waited for; matrix products, arithmetic and copies ran while one was open for 0% of the time, Pallas kernels for 12%

profile of v4, /device:TPU:0, one launch (start us, length us, event | category | flops | bytes accessed | tf_op | source)
XLA Modules:
  0.0 47.6 jit_solution(4528567709097652509)
XLA Ops:
  0.0 2.1 %pack.1 = (bf16[32,8,128]{2,1,0:T(8,128)(2,1)S(1)}, bf16[32,8,128]{2,1,0:T(8,128)(2,1)S(1)}, bf16[32,8,128]{2,1,0:T(8,128)(2,1)S(1)}, bf16[32,8,128]{2,1,0:T(8,1...) custom-call(s32[2,128]{1,0:T(2,128)} %bitcast.7, ...), custom_call_target="tpu_custom_call" | custom-call | bytes 1048576 | tf_op jit(solution)/shard_map/pack/pallas_call | solution.py:107
  2.1 3.0 %collective-permute-start = (bf16[32,8,128]{2,1,0:T(8,128)(2,1)S(1)}, bf16[32,8,128]{2,1,0:T(8,128)(2,1)S(1)}, u32[]{:S(2)}, u32[]{:S(2)}) collective-permute-start(bf16[32,8,128]{2,1,0:T(8,128)(2,1)S(1)} %get-tuple-element.29), channel_id=1, source_target_pairs={{0,4},{1,5},{2,6},{3,7},{4,0},{5,1},{6,2},{7,3},{8,12},{9,13},{10,... | collective-permute-start | bytes 196616 | tf_op jit(solution)/shard_map/ppermute | solution.py:562
  5.1 0.2 collective-permute-start.7
  5.3 1.5 %collective-permute-start.8 = (bf16[32,8,128]{2,1,0:T(8,128)(2,1)S(1)}, bf16[32,8,128]{2,1,0:T(8,128)(2,1)S(1)}, u32[]{:S(2)}, u32[]{:S(2)}) collective-permute-start(bf16[32,8,128]{2,1,0:T(8,128)(2,1)S(1)} %get-tuple-element.38), channel_id=1, source_target_pairs={{0,3},{1,2},{2,1},{3,0},{4,7},{5,6},{6,5},{7,4},{8,11},{9,10},{10,... | collective-permute-start | bytes 196616 | tf_op jit(solution)/shard_map/ppermute | solution.py:562
  6.9 1.6 %collective-permute-start.2 = (bf16[32,8,128]{2,1,0:T(8,128)(2,1)S(1)}, bf16[32,8,128]{2,1,0:T(8,128)(2,1)S(1)}, u32[]{:S(2)}, u32[]{:S(2)}) collective-permute-start(bf16[32,8,128]{2,1,0:T(8,128)(2,1)S(1)} %get-tuple-element.31), channel_id=1, source_target_pairs={{0,7},{1,6},{2,5},{3,4},{4,3},{5,2},{6,1},{7,0},{8,15},{9,14},{10,... | collective-permute-start | bytes 196616 | tf_op jit(solution)/shard_map/ppermute | solution.py:562
  8.5 1.5 %collective-permute-start.3 = (bf16[32,8,128]{2,1,0:T(8,128)(2,1)S(1)}, bf16[32,8,128]{2,1,0:T(8,128)(2,1)S(1)}, u32[]{:S(2)}, u32[]{:S(2)}) collective-permute-start(bf16[32,8,128]{2,1,0:T(8,128)(2,1)S(1)} %get-tuple-element.32), channel_id=1, source_target_pairs={{0,2},{1,3},{2,0},{3,1},{4,8},{5,9},{6,10},{7,11},{8,4},{9,5},{10,... | collective-permute-start | bytes 196616 | tf_op jit(solution)/shard_map/ppermute | solution.py:562
  10.0 0.0 collective-permute-done.1.refs_1_
  10.0 0.0 collective-permute-start.4
  10.0 0.5 %collective-permute-start.5 = (bf16[32,8,128]{2,1,0:T(8,128)(2,1)S(1)}, bf16[32,8,128]{2,1,0:T(8,128)(2,1)S(1)}, u32[]{:S(2)}, u32[]{:S(2)}) collective-permute-start(bf16[32,8,128]{2,1,0:T(8,128)(2,1)S(1)} %get-tuple-element.34), channel_id=1, source_target_pairs={{0,1},{1,0},{2,3},{3,2},{4,11},{5,10},{6,9},{7,8},{8,7},{9,6},{10,... | collective-permute-start | bytes 196616 | tf_op jit(solution)/shard_map/ppermute | solution.py:562
  10.5 4.6 %collective-permute-start.6 = (bf16[32,8,128]{2,1,0:T(8,128)(2,1)S(1)}, bf16[32,8,128]{2,1,0:T(8,128)(2,1)S(1)}, u32[]{:S(2)}, u32[]{:S(2)}) collective-permute-start(bf16[32,8,128]{2,1,0:T(8,128)(2,1)S(1)} %get-tuple-element.35), channel_id=1, source_target_pairs={{0,6},{1,7},{2,4},{3,5},{4,2},{5,3},{6,0},{7,1},{8,14},{9,15},{10,... | collective-permute-start | bytes 196616 | tf_op jit(solution)/shard_map/ppermute | solution.py:562
  15.1 3.2 %near.1 = (f32[256,8,128]{2,1,0:T(8,128)S(1)}, bf16[4,32,128,128]{3,2,1,0:T(8,128)(2,1)S(1)}) custom-call(s32[12,1,32]{2,1,0:T(1,128)} %bitcast.5, bf16[32,8,128]{2,1,0:T(8,128)(2,1)S(1)} %get-tuple-element.36.own_ref, bf16[32,8,128]{2,1,0:T(8,128)(2,1)S(1)} %collective-permute-done.7.core_ref, bf16[32,8,128]{2,1,0:T(8,128)(2,1)S(1)} %collective-permute-done.8.x_ref, ...), custom_call_target="tpu_custom_call" | custom-call | flops 25165824 | bytes 12582912 | tf_op jit(solution)/shard_map/near/pallas_call | solution.py:263
  18.3 0.0 copy-start
  18.3 3.0 %far.1 = (bf16[512,512]{1,0:T(8,128)(2,1)S(1)}, bf16[16,512]{1,0:T(8,128)(2,1)S(1)}, bf16[16,512]{1,0:T(8,128)(2,1)S(1)}) custom-call(s32[12,1,32]{2,1,0:T(1,128)} %bitcast.6, bf16[32,8,128]{2,1,0:T(8,128)(2,1)S(1)} %collective-permute-done.refs_0_, bf16[32,8,128]{2,1,0:T(8,128)(2,1)S(1)} %collective-permute-done.1.refs_1_, ...), custom_call_target="tpu_custom_call" | custom-call | flops 58720256 | bytes 8388608 | tf_op jit(solution)/shard_map/far/pallas_call | solution.py:288
  21.3 2.2 %collective-permute-start.9 = (bf16[16,512]{1,0:T(8,128)(2,1)S(1)}, bf16[16,512]{1,0:T(8,128)(2,1)S(1)}, u32[]{:S(2)}, u32[]{:S(2)}) collective-permute-start(bf16[16,512]{1,0:T(8,128)(2,1)S(1)} %get-tuple-element.41), channel_id=1, source_target_pairs={{0,4},{1,5},{2,6},{3,7},{4,0},{5,1},{6,2},{7,3},{8,12},{9,13},{10,... | collective-permute-start | bytes 49160 | tf_op jit(solution)/shard_map/ppermute | solution.py:562
  23.5 0.6 %collective-permute-start.10 = (bf16[16,512]{1,0:T(8,128)(2,1)S(1)}, bf16[16,512]{1,0:T(8,128)(2,1)S(1)}, u32[]{:S(2)}, u32[]{:S(2)}) collective-permute-start(bf16[16,512]{1,0:T(8,128)(2,1)S(1)} %get-tuple-element.42), channel_id=1, source_target_pairs={{0,2},{1,3},{2,0},{3,1},{4,8},{5,9},{6,10},{7,11},{8,4},{9,5},{10,... | collective-permute-start | bytes 49160 | tf_op jit(solution)/shard_map/ppermute | solution.py:562
  24.1 1.1 %spread.1 = (bf16[11,256,384]{2,1,0:T(8,128)(2,1)S(1)}, bf16[512,1536]{1,0:T(8,128)(2,1)S(1)}) custom-call(bf16[512,512]{1,0:T(8,128)(2,1)S(1)} %get-tuple-element.43.fld_ref), custom_call_target="tpu_custom_call" | custom-call | flops 805306368 | bytes 4194304 | tf_op jit(solution)/shard_map/spread/pallas_call | solution.py:369
  25.2 0.1 collective-permute-done.9.a_ref
  25.2 2.0 %collective-permute-done.10.b_ref = bf16[16,512]{1,0:T(8,128)(2,1)S(1)} collective-permute-done((bf16[16,512]{1,0:T(8,128)(2,1)S(1)}, bf16[16,512]{1,0:T(8,128)(2,1)S(1)}, u32[]{:S(2)}, u32[]{:S(2)}) %collective-permute-start.10) | collective-permute-done | bytes 16416 | tf_op jit(solution)/shard_map/ppermute | solution.py:562
  27.3 0.2 edges.1
  27.4 0.1 collective-permute-start.12
  27.5 0.7 %collective-permute-start.11 = (bf16[16,544]{1,0:T(8,128)(2,1)S(1)}, bf16[16,544]{1,0:T(8,128)(2,1)S(1)}, u32[]{:S(2)}, u32[]{:S(2)}) collective-permute-start(bf16[16,544]{1,0:T(8,128)(2,1)S(1)} %edges.1), channel_id=1, source_target_pairs={{0,1},{1,0},{2,3},{3,2},{4,5},{5,4},{6,7},{7,6},{8,9},{9,8},{10,11... | collective-permute-start | bytes 52232 | tf_op jit(solution)/shard_map/ppermute | solution.py:562
  28.2 1.2 %prep.1 = (bf16[256,1536]{1,0:T(8,128)(2,1)S(1)}, f32[1,256]{1,0:T(1,128)S(1)}, bf16[4,512,256]{2,1,0:T(8,128)(2,1)S(1)}) custom-call(bf16[9,8,128]{2,1,0:T(8,128)(2,1)} %stem_ref.1, f32[1,128]{1,0:T(1,128)} %bitcast.8, bf16[9,128,128]{2,1,0:T(8,128)(2,1)} %mix_ref.1), custom_call_target="tpu_custom_call" | custom-call | bytes 2097152 | tf_op jit(solution)/shard_map/prep/pallas_call | solution.py:154
  29.4 1.3 %collective-permute-done.12.x_ref = bf16[16,544]{1,0:T(8,128)(2,1)S(1)} collective-permute-done((bf16[16,544]{1,0:T(8,128)(2,1)S(1)}, bf16[16,544]{1,0:T(8,128)(2,1)S(1)}, u32[]{:S(2)}, u32[]{:S(2)}) %collective-permute-start.12) | collective-permute-done | bytes 17440 | tf_op jit(solution)/shard_map/ppermute | solution.py:562
  30.7 16.9 %conv.1 = bf16[64,512,128]{2,1,0:T(8,128)(2,1)} custom-call(bf16[11,256,384]{2,1,0:T(8,128)(2,1)S(1)} %get-tuple-element.46.g_ref, bf16[16,512]{1,0:T(8,128)(2,1)S(1)} %collective-permute-done.9.a_ref, bf16[16,512]{1,0:T(8,128)(2,1)S(1)} %collective-permute-done.10.b_ref, bf16[16,544]{1,0:T(8,128)(2,1)S(1)} %collective-permute-done.11.core_ref, ...), custom_call_target="tpu_custom_call" | custom-call | flops 9663676416 | bytes 12582912 | tf_op jit(solution)/shard_map/conv/pallas_call | solution.py:536
  (11 shorter events, 0.0 us)
Async XLA Ops:
  2.1 6.4 %collective-permute-start = (bf16[32,8,128]{2,1,0:T(8,128)(2,1)S(1)}, bf16[32,8,128]{2,1,0:T(8,128)(2,1)S(1)}, u32[]{:S(2)}, u32[]{:S(2)}) collective-permute-start(bf16[32,8,128]{2,1,0:T(8,128)(2,1)S(1)} %get-tuple-element.29), channel_id=1, source_target_pairs={{0,4},{1,5},{2,6},{3,7},{4,0},{5,1},{6,2},{7,3},{8,12},{9,13},{10,... | collective-permute-start | bytes 196616 | tf_op jit(solution)/shard_map/ppermute | solution.py:562
  5.1 4.8 %collective-permute-start.1 = (bf16[32,8,128]{2,1,0:T(8,128)(2,1)S(1)}, bf16[32,8,128]{2,1,0:T(8,128)(2,1)S(1)}, u32[]{:S(2)}, u32[]{:S(2)}) collective-permute-start(bf16[32,8,128]{2,1,0:T(8,128)(2,1)S(1)} %get-tuple-element.30), channel_id=1, source_target_pairs={{0,5},{1,4},{2,7},{3,6},{4,1},{5,0},{6,3},{7,2},{8,13},{9,12},{10,... | collective-permute-start | bytes 196616 | tf_op jit(solution)/shard_map/ppermute | solution.py:562
  5.1 4.8 %collective-permute-start.7 = (bf16[32,8,128]{2,1,0:T(8,128)(2,1)S(1)}, bf16[32,8,128]{2,1,0:T(8,128)(2,1)S(1)}, u32[]{:S(2)}, u32[]{:S(2)}) collective-permute-start(bf16[32,8,128]{2,1,0:T(8,128)(2,1)S(1)} %get-tuple-element.37), channel_id=1, source_target_pairs={{0,1},{1,0},{2,3},{3,2},{4,5},{5,4},{6,7},{7,6},{8,9},{9,8},{10,11... | collective-permute-start | bytes 196616 | tf_op jit(solution)/shard_map/ppermute | solution.py:562
  5.3 5.1 %collective-permute-start.8 = (bf16[32,8,128]{2,1,0:T(8,128)(2,1)S(1)}, bf16[32,8,128]{2,1,0:T(8,128)(2,1)S(1)}, u32[]{:S(2)}, u32[]{:S(2)}) collective-permute-start(bf16[32,8,128]{2,1,0:T(8,128)(2,1)S(1)} %get-tuple-element.38), channel_id=1, source_target_pairs={{0,3},{1,2},{2,1},{3,0},{4,7},{5,6},{6,5},{7,4},{8,11},{9,10},{10,... | collective-permute-start | bytes 196616 | tf_op jit(solution)/shard_map/ppermute | solution.py:562
  6.9 11.4 %collective-permute-start.2 = (bf16[32,8,128]{2,1,0:T(8,128)(2,1)S(1)}, bf16[32,8,128]{2,1,0:T(8,128)(2,1)S(1)}, u32[]{:S(2)}, u32[]{:S(2)}) collective-permute-start(bf16[32,8,128]{2,1,0:T(8,128)(2,1)S(1)} %get-tuple-element.31), channel_id=1, source_target_pairs={{0,7},{1,6},{2,5},{3,4},{4,3},{5,2},{6,1},{7,0},{8,15},{9,14},{10,... | collective-permute-start | bytes 196616 | tf_op jit(solution)/shard_map/ppermute | solution.py:562
  8.5 9.8 %collective-permute-start.3 = (bf16[32,8,128]{2,1,0:T(8,128)(2,1)S(1)}, bf16[32,8,128]{2,1,0:T(8,128)(2,1)S(1)}, u32[]{:S(2)}, u32[]{:S(2)}) collective-permute-start(bf16[32,8,128]{2,1,0:T(8,128)(2,1)S(1)} %get-tuple-element.32), channel_id=1, source_target_pairs={{0,2},{1,3},{2,0},{3,1},{4,8},{5,9},{6,10},{7,11},{8,4},{9,5},{10,... | collective-permute-start | bytes 196616 | tf_op jit(solution)/shard_map/ppermute | solution.py:562
  10.0 8.3 %collective-permute-start.4 = (bf16[32,8,128]{2,1,0:T(8,128)(2,1)S(1)}, bf16[32,8,128]{2,1,0:T(8,128)(2,1)S(1)}, u32[]{:S(2)}, u32[]{:S(2)}) collective-permute-start(bf16[32,8,128]{2,1,0:T(8,128)(2,1)S(1)} %get-tuple-element.33), channel_id=1, source_target_pairs={{0,1},{1,0},{2,3},{3,2},{4,9},{5,8},{6,11},{7,10},{8,5},{9,4},{10,... | collective-permute-start | bytes 196616 | tf_op jit(solution)/shard_map/ppermute | solution.py:562
  10.0 8.3 %collective-permute-start.5 = (bf16[32,8,128]{2,1,0:T(8,128)(2,1)S(1)}, bf16[32,8,128]{2,1,0:T(8,128)(2,1)S(1)}, u32[]{:S(2)}, u32[]{:S(2)}) collective-permute-start(bf16[32,8,128]{2,1,0:T(8,128)(2,1)S(1)} %get-tuple-element.34), channel_id=1, source_target_pairs={{0,1},{1,0},{2,3},{3,2},{4,11},{5,10},{6,9},{7,8},{8,7},{9,6},{10,... | collective-permute-start | bytes 196616 | tf_op jit(solution)/shard_map/ppermute | solution.py:562
  10.5 7.8 %collective-permute-start.6 = (bf16[32,8,128]{2,1,0:T(8,128)(2,1)S(1)}, bf16[32,8,128]{2,1,0:T(8,128)(2,1)S(1)}, u32[]{:S(2)}, u32[]{:S(2)}) collective-permute-start(bf16[32,8,128]{2,1,0:T(8,128)(2,1)S(1)} %get-tuple-element.35), channel_id=1, source_target_pairs={{0,6},{1,7},{2,4},{3,5},{4,2},{5,3},{6,0},{7,1},{8,14},{9,15},{10,... | collective-permute-start | bytes 196616 | tf_op jit(solution)/shard_map/ppermute | solution.py:562
  18.3 12.4 %copy-start = (f32[128]{0:T(128)S(1)}, f32[128]{0:T(128)}, u32[]{:S(2)}) copy-start(f32[128]{0:T(128)} %param.15) | copy-start | bytes 1540
  21.3 3.9 %collective-permute-start.9 = (bf16[16,512]{1,0:T(8,128)(2,1)S(1)}, bf16[16,512]{1,0:T(8,128)(2,1)S(1)}, u32[]{:S(2)}, u32[]{:S(2)}) collective-permute-start(bf16[16,512]{1,0:T(8,128)(2,1)S(1)} %get-tuple-element.41), channel_id=1, source_target_pairs={{0,4},{1,5},{2,6},{3,7},{4,0},{5,1},{6,2},{7,3},{8,12},{9,13},{10,... | collective-permute-start | bytes 49160 | tf_op jit(solution)/shard_map/ppermute | solution.py:562
  23.5 3.7 %collective-permute-start.10 = (bf16[16,512]{1,0:T(8,128)(2,1)S(1)}, bf16[16,512]{1,0:T(8,128)(2,1)S(1)}, u32[]{:S(2)}, u32[]{:S(2)}) collective-permute-start(bf16[16,512]{1,0:T(8,128)(2,1)S(1)} %get-tuple-element.42), channel_id=1, source_target_pairs={{0,2},{1,3},{2,0},{3,1},{4,8},{5,9},{6,10},{7,11},{8,4},{9,5},{10,... | collective-permute-start | bytes 49160 | tf_op jit(solution)/shard_map/ppermute | solution.py:562
  27.4 3.3 %collective-permute-start.12 = (bf16[16,544]{1,0:T(8,128)(2,1)S(1)}, bf16[16,544]{1,0:T(8,128)(2,1)S(1)}, u32[]{:S(2)}, u32[]{:S(2)}) collective-permute-start(bf16[16,544]{1,0:T(8,128)(2,1)S(1)} %edges.1), channel_id=1, source_target_pairs={{0,3},{1,2},{2,1},{3,0},{4,7},{5,6},{6,5},{7,4},{8,11},{9,10},{10,... | collective-permute-start | bytes 52232 | tf_op jit(solution)/shard_map/ppermute | solution.py:562
  27.5 3.2 %collective-permute-start.11 = (bf16[16,544]{1,0:T(8,128)(2,1)S(1)}, bf16[16,544]{1,0:T(8,128)(2,1)S(1)}, u32[]{:S(2)}, u32[]{:S(2)}) collective-permute-start(bf16[16,544]{1,0:T(8,128)(2,1)S(1)} %edges.1), channel_id=1, source_target_pairs={{0,1},{1,0},{2,3},{3,2},{4,5},{5,4},{6,7},{7,6},{8,9},{9,8},{10,11... | collective-permute-start | bytes 52232 | tf_op jit(solution)/shard_map/ppermute | solution.py:562

commit v5 on v4

--- a/solution.py
+++ b/solution.py
@@ -16,7 +16,7 @@
 LANES = 384
 CHUNK = 256
 NEAR, FAR = 3, 7
-EARLY = 4
+EARLY = 2
 STEP = 6
 BLOCKS = (ROWS + 2) // STEP
 SCALE = 1.0 / 2.0
@@ -46,10 +46,9 @@
         else:
             partner = b
         for l in range(n_lon):
-            target = {"stay": l, "core": l ^ 1, "x": n_lon - 1 - l, "across": (l + 2) % n_lon}[turn]
-            if not 0 <= partner < n_band:
-                spare = (l + 2) % n_lon if turn == "stay" else l ^ 1
-                pairs.append((b * n_lon + l, b * n_lon + spare))
+            target = {"stay": l, "core": l ^ 1, "x": n_lon - 1 - l, "x_rim": n_lon - 1 - l}[turn]
+            if not 0 <= partner < n_band or (turn == "x_rim" and 2 <= b < n_band - 2):
+                pairs.append((b * n_lon + l, b * n_lon + (l ^ 1)))
             else:
                 pairs.append((b * n_lon + l, partner * n_lon + target))
     return pairs
@@ -59,8 +58,11 @@
     return [pltpu.with_memory_space_constraint(a, pltpu.HBM) for a in arrays]
 
 
+PARTS = ((0, 1), (1, 5), (6, 1), (7, 1), (8, 1), (9, 1), (10, 1))
+
+
 def pack_kernel(routes_hbm, src_hbm, *refs):
-    outs, (routes_ref, src_ref, buf, place, sem) = refs[:10], refs[10:]
+    outs, (routes_ref, src_ref, buf, place, sem) = refs[:7], refs[7:]
     copies = [
         pltpu.make_async_copy(routes_hbm, routes_ref, sem.at[0]),
         pltpu.make_async_copy(src_hbm, src_ref, sem.at[1]),
@@ -72,16 +74,14 @@
     core_dl = 1 + 2 * (lon % 2)
     for q in range(12):
         db, dl = q // 4 - 1, q % 4
-        if db == 0:
-            way = 0
+        if dl == 2:
+            group = 5 if db == 0 else 4
+        elif db == 0:
+            group = 0 if dl == 0 else jnp.where(core_dl == dl, 1, 6)
+        elif dl == 0:
+            group = jnp.where(a_dir == db, 7, 9)
         else:
-            way = jnp.where(a_dir == db, 3, 6)
-        if dl == 0:
-            group = way
-        elif dl == 2:
-            group = 6 if db == 0 else 9
-        else:
-            group = jnp.where(core_dl == dl, 1, 2) + way
+            group = jnp.where(core_dl == dl, jnp.where(a_dir == db, 2, 3), jnp.where(a_dir == db, 8, 10))
         place[q] = group * 32
     buf[...] = jnp.zeros_like(buf)
     for copy in copies:
@@ -97,8 +97,8 @@
         return carry
 
     lax.fori_loop(0, src_ref.shape[0], one, 0, unroll=8)
-    for group, out in enumerate(outs):
-        out[...] = buf[group * 32 : group * 32 + 32]
+    for out, (begin, groups) in zip(outs, PARTS):
+        out[...] = buf[begin * 32 : (begin + groups) * 32]
 
 
 def pack(routes, source):
@@ -107,12 +107,12 @@
     return pl.pallas_call(
         pack_kernel,
         in_specs=[HBM, HBM],
-        out_specs=[VM] * 10,
-        out_shape=[shape(32)] * 10,
+        out_specs=[VM] * 7,
+        out_shape=[shape(32 * groups) for _, groups in PARTS],
         scratch_shapes=[
             pltpu.SMEM(routes.shape, jnp.int32),
             pltpu.VMEM(source.shape, BF),
-            pltpu.VMEM((320, fields, cells), BF),
+            pltpu.VMEM((352, fields, cells), BF),
             pltpu.SMEM((12,), jnp.int32),
             pltpu.SemaphoreType.DMA((2,)),
         ],
@@ -120,6 +120,26 @@
         cost_estimate=cost(0, 1 << 20),
         name="pack",
     )(*in_hbm(routes, source))
+
+
+def merge_kernel(core_ref, x_ref, a_ref, b_ref, x_out, a_out, b_out, far_out):
+    for out, mine, group in ((x_out, x_ref, 4), (a_out, a_ref, 1), (b_out, b_ref, 2)):
+        out[0:32] = mine[...]
+        out[32:64] = core_ref[group * 32 : group * 32 + 32]
+    far_out[...] = core_ref[96:128]
+
+
+def merge(core, x, a, b):
+    shape = lambda n: jax.ShapeDtypeStruct((n,) + a.shape[1:], BF)
+    return pl.pallas_call(
+        merge_kernel,
+        in_specs=[VM] * 4,
+        out_specs=[VM] * 4,
+        out_shape=[shape(64), shape(64), shape(64), shape(32)],
+        compiler_params=params(8),
+        cost_estimate=cost(0, 1 << 20),
+        name="merge",
+    )(core, x, a, b)
 
 
 def prep_kernel(stem_ref, bias_ref, mix_ref, ws_ref, bs_ref, wm_ref):
@@ -174,9 +194,9 @@
     b_base = 8 - a_base
     rim = (band == 0) | (band == last)
     codes = [4, 4 + core_dl, 4 + x_dl]
-    codes += [a_base, a_base + core_dl, a_base + x_dl]
+    codes += [a_base, a_base + core_dl]
+    codes += [a_base + x_dl, jnp.where(band < (last + 1) // 2, 10, 2)]
     codes += [jnp.where(rim, 6, b_base), b_base + core_dl, b_base + x_dl]
-    codes.append(jnp.where(band < (last + 1) // 2, 10, 2))
     for g, code in enumerate(codes):
         codes_ref[g] = jnp.int32(code)
 
@@ -220,7 +240,7 @@
         transfer.start()
     acc[...] = jnp.zeros_like(acc)
     for g, array in enumerate((own_ref, core_ref, x_ref)):
-        inc[g] = array[...]
+        inc[g] = array[0:32]
     window.wait()
     add_groups(codes_ref, win_ref, w_ref, inc, acc, 0, 0, NEAR, lambda g: copy(g).wait())
     for transfer in early:
@@ -228,8 +248,9 @@
 
 
 def far_kernel(last, win_hbm, *refs):
-    arrays, (near_ref, early_ref, w_hbm, fld_ref, a_ref, b_ref) = refs[:7], refs[7:13]
-    acc, w_ref, inc, codes_ref, win_ref, sem, win_sem = refs[13:]
+    (x_in, a_in, ax_in, far_in, b_in, bx_in), refs = refs[:6], refs[6:]
+    near_ref, early_ref, w_hbm, fld_ref, a_ref, b_ref = refs[:6]
+    acc, w_ref, inc, codes_ref, win_ref, sem, win_sem = refs[6:]
     group_codes(last, codes_ref)
     window = pltpu.make_async_copy(win_hbm, win_ref, win_sem)
     window.start()
@@ -242,8 +263,12 @@
     for g in range(FAR - EARLY):
         copy(g).start()
     acc[...] = near_ref[...]
-    for g, array in enumerate(arrays):
-        inc[g] = array[...]
+    band = lax.axis_index("band")
+    rim = (band == 0) | (band == last)
+    blocks = [a_in[0:32], a_in[32:64], ax_in[...], far_in[...]]
+    blocks += [jnp.where(rim, x_in[32:64], b_in[0:32]), b_in[32:64], bx_in[...]]
+    for g, value in enumerate(blocks):
+        inc[g] = value
     window.wait()
     add_groups(codes_ref, win_ref, early_ref, inc, acc, NEAR, 0, EARLY)
     add_groups(
@@ -287,7 +312,7 @@
     group = weights.shape[2:]
     return pl.pallas_call(
         functools.partial(far_kernel, n_band - 1),
-        in_specs=[HBM] + [VM] * 9 + [HBM],
+        in_specs=[HBM] + [VM] * 8 + [HBM],
         out_specs=[VM] * 3,
         out_shape=[
             jax.ShapeDtypeStruct((ROWS * 8, COLS), BF),
@@ -561,14 +586,14 @@
     def move(value, way, turn):
         return lax.ppermute(value, axes, swap(n_band, n_lon, way, turn))
 
-    turns = ("stay", "core", "x")
-    out = pack(routes.T, source)
+    own, to_core, to_x, to_a, to_ax, to_b, to_bx = pack(routes.T, source)
     win = window.transpose(1, 0, 2)
-    arrays = [move(out[3 + i], "a", turn) for i, turn in enumerate(turns)]
-    arrays += [move(out[6 + i], "b", turn) for i, turn in enumerate(turns)]
-    arrays.append(move(out[9], "a", "across"))
-    core, x = move(out[1], "", "core"), move(out[2], "", "x")
-    near, early = near_part(n_band, win, out[0], core, x, slot_weights)
+    core = move(to_core, "", "core")
+    bx, ax = move(to_bx, "b", "x"), move(to_ax, "a", "x")
+    x_both, a_both, b_both, far = merge(core, to_x, to_a, to_b)
+    x, a, b = move(x_both, "", "x"), move(a_both, "a", "stay"), move(b_both, "b", "stay")
+    arrays = [x, a, ax, move(far, "a", "x_rim"), b, bx]
+    near, early = near_part(n_band, win, own, core, x, slot_weights)
     fld, a_row, b_row = far_part(n_band, win, arrays, near, early, slot_weights)
     a_halo = move(a_row, "a", "stay")
     b_halo = move(b_row, "b", "stay")

time: 47.7 us -> 46.5 us (0.975)
  starting transfers between devices: 16.4 us -> 14 us
  waiting for transfers between devices: 3.38 us -> 4.97 us
  Pallas kernels: 27.7 us -> 27.2 us
    ppermute x13 -> x11, starting transfers between devices: 16.4 us -> 14 us  [move(): return lax.ppermute(value, axes, swap(n_band, n_lon, way, turn))]
    ppermute x13 -> x11, waiting for transfers between devices: 3.38 us -> 4.97 us  [move(): return lax.ppermute(value, axes, swap(n_band, n_lon, way, turn))]
    pallas_call x1, Pallas kernels: 3.18 us -> 2.55 us  [near_part(): pl.pallas_call(functools.partial(near_kernel, n_band - 1), in_specs=[HBM]...]
    pallas_call x1 -> x2, Pallas kernels: 2.09 us -> 2.13 us  [the longest x1 2.1 us: pack(): pl.pallas_call(pack_kernel, in_specs=[HBM, HBM], out_specs=[VM] * 7, out_...]
  transfers between devices with their start and end apart: 13 -> 11, of which waited for: 3 -> 4; matrix products, arithmetic and copies ran while one was open for 0% -> 0% of each run, Pallas kernels for 12% -> 11%
where the time goes in v5:
time: 46.5 us; the launch traced here: 46.3 us
  Pallas kernels  27.2 us (58%)
  starting transfers between devices  14 us (30%)
  waiting for transfers between devices  4.97 us (11%)
    pallas_call x1, Pallas kernels, conv(): pl.pallas_call(functools.partial(conv_kernel, n_band - 1), in_specs=[VM]...  16.9 us
    ppermute x11, starting transfers between devices, move(): return lax.ppermute(value, axes, swap(n_band, n_lon, way, turn))  14 us
    ppermute x11, waiting for transfers between devices, move(): return lax.ppermute(value, axes, swap(n_band, n_lon, way, turn))  4.97 us
    pallas_call x1, Pallas kernels, far_part(): pl.pallas_call(functools.partial(far_kernel, n_band - 1), in_specs=[HBM]...  3.15 us
    pallas_call x1, Pallas kernels, near_part(): pl.pallas_call(functools.partial(near_kernel, n_band - 1), in_specs=[HBM]...  2.55 us
    pallas_call x1, Pallas kernels, pack(): pl.pallas_call(pack_kernel, in_specs=[HBM, HBM], out_specs=[VM] * 7, out_...  2.1 us
    pallas_call x1, Pallas kernels, prep(): pl.pallas_call(prep_kernel, in_specs=[VM] * 3, out_specs=[VM] * 3, out_sh...  1.25 us
    pallas_call x1, Pallas kernels, spread(): pl.pallas_call(spread_kernel, in_specs=[VM], out_specs=[VM] * 2, out_shap...  1.08 us
  transfers between devices with their start and end apart: 11, of which 4 were waited for; matrix products, arithmetic and copies ran while one was open for 0% of the time, Pallas kernels for 11%

profile of v5, /device:TPU:0, one launch (start us, length us, event | category | flops | bytes accessed | tf_op | source)
XLA Modules:
  0.0 46.3 jit_solution(6510595298307525097)
XLA Ops:
  0.0 2.1 %pack.1 = (bf16[32,8,128]{2,1,0:T(8,128)(2,1)S(1)}, bf16[160,8,128]{2,1,0:T(8,128)(2,1)S(1)}, bf16[32,8,128]{2,1,0:T(8,128)(2,1)S(1)}, bf16[32,8,128]{2,1,0:T(8,...) custom-call(s32[2,128]{1,0:T(2,128)} %bitcast.7, ...), custom_call_target="tpu_custom_call" | custom-call | bytes 1048576 | tf_op jit(solution)/shard_map/pack/pallas_call | solution.py:107
  2.1 0.5 %collective-permute-start = (bf16[160,8,128]{2,1,0:T(8,128)(2,1)S(1)}, bf16[160,8,128]{2,1,0:T(8,128)(2,1)S(1)}, u32[]{:S(2)}, u32[]{:S(2)}) collective-permute-start(bf16[160,8,128]{2,1,0:T(8,128)(2,1)S(1)} %get-tuple-element.30), channel_id=1, source_target_pairs={{0,1},{1,0},{2,3},{3,2},{4,5},{5,4},{6,7},{7,6},{8,9},{9,8},{10,11... | collective-permute-start | bytes 983048 | tf_op jit(solution)/shard_map/ppermute | solution.py:587
  2.6 1.3 %collective-permute-done.core_ref = bf16[160,8,128]{2,1,0:T(8,128)(2,1)S(1)} collective-permute-done((bf16[160,8,128]{2,1,0:T(8,128)(2,1)S(1)}, bf16[160,8,128]{2,1,0:T(8,128)(2,1)S(1)}, u32[]{:S(2)}, u32[]{:S(2)}) %collective-permute-start) | collective-permute-done | bytes 327712 | tf_op jit(solution)/shard_map/ppermute | solution.py:587
  3.9 2.7 %collective-permute-start.1 = (bf16[64,8,128]{2,1,0:T(8,128)(2,1)S(1)}, bf16[64,8,128]{2,1,0:T(8,128)(2,1)S(1)}, u32[]{:S(2)}, u32[]{:S(2)}) collective-permute-start(bf16[64,8,128]{2,1,0:T(8,128)(2,1)S(1)} %get-tuple-element.34), channel_id=1, source_target_pairs={{0,3},{1,2},{2,1},{3,0},{4,7},{5,6},{6,5},{7,4},{8,11},{9,10},{10,... | collective-permute-start | bytes 393224 | tf_op jit(solution)/shard_map/ppermute | solution.py:587
  6.6 1.5 %collective-permute-start.2 = (bf16[64,8,128]{2,1,0:T(8,128)(2,1)S(1)}, bf16[64,8,128]{2,1,0:T(8,128)(2,1)S(1)}, u32[]{:S(2)}, u32[]{:S(2)}) collective-permute-start(bf16[64,8,128]{2,1,0:T(8,128)(2,1)S(1)} %get-tuple-element.35), channel_id=1, source_target_pairs={{0,4},{1,5},{2,6},{3,7},{4,0},{5,1},{6,2},{7,3},{8,12},{9,13},{10,... | collective-permute-start | bytes 393224 | tf_op jit(solution)/shard_map/ppermute | solution.py:587
  8.1 0.1 collective-permute-start.5
  8.2 2.3 %collective-permute-start.3 = (bf16[32,8,128]{2,1,0:T(8,128)(2,1)S(1)}, bf16[32,8,128]{2,1,0:T(8,128)(2,1)S(1)}, u32[]{:S(2)}, u32[]{:S(2)}) collective-permute-start(bf16[32,8,128]{2,1,0:T(8,128)(2,1)S(1)} %get-tuple-element.36), channel_id=1, source_target_pairs={{0,7},{1,6},{2,5},{3,4},{4,3},{5,2},{6,1},{7,0},{8,15},{9,14},{10,... | collective-permute-start | bytes 196616 | tf_op jit(solution)/shard_map/ppermute | solution.py:587
  10.5 0.7 %collective-permute-start.6 = (bf16[32,8,128]{2,1,0:T(8,128)(2,1)S(1)}, bf16[32,8,128]{2,1,0:T(8,128)(2,1)S(1)}, u32[]{:S(2)}, u32[]{:S(2)}) collective-permute-start(bf16[32,8,128]{2,1,0:T(8,128)(2,1)S(1)} %get-tuple-element.39), channel_id=1, source_target_pairs={{0,1},{1,0},{2,3},{3,2},{4,11},{5,10},{6,9},{7,8},{8,7},{9,6},{10,... | collective-permute-start | bytes 196616 | tf_op jit(solution)/shard_map/ppermute | solution.py:587
  11.2 0.0 collective-permute-done.1.x_ref.refs_0_
  11.2 2.9 %collective-permute-start.4 = (bf16[32,8,128]{2,1,0:T(8,128)(2,1)S(1)}, bf16[32,8,128]{2,1,0:T(8,128)(2,1)S(1)}, u32[]{:S(2)}, u32[]{:S(2)}) collective-permute-start(bf16[32,8,128]{2,1,0:T(8,128)(2,1)S(1)} %get-tuple-element.37), channel_id=1, source_target_pairs={{0,7},{1,6},{2,5},{3,4},{4,3},{5,2},{6,1},{7,0},{8,9},{9,8},{10,11... | collective-permute-start | bytes 196616 | tf_op jit(solution)/shard_map/ppermute | solution.py:587
  14.2 2.5 %near.1 = (f32[256,8,128]{2,1,0:T(8,128)S(1)}, bf16[2,32,128,128]{3,2,1,0:T(8,128)(2,1)S(1)}) custom-call(s32[12,1,32]{2,1,0:T(1,128)} %bitcast.5, bf16[32,8,128]{2,1,0:T(8,128)(2,1)S(1)} %get-tuple-element.40.own_ref, bf16[160,8,128]{2,1,0:T(8,128)(2,1)S(1)} %collective-permute-done.core_ref, bf16[64,8,128]{2,1,0:T(8,128)(2,1)S(1)} %collective-permute-done.1.x_ref.refs_0_, ...), custom_call_target="tpu_custom_call" | custom-call | flops 25165824 | bytes 12582912 | tf_op jit(solution)/shard_map/near/pallas_call | solution.py:288
  16.8 0.0 collective-permute-done.4.refs_3_
  16.8 1.6 %collective-permute-done.2.refs_1_ = bf16[64,8,128]{2,1,0:T(8,128)(2,1)S(1)} collective-permute-done((bf16[64,8,128]{2,1,0:T(8,128)(2,1)S(1)}, bf16[64,8,128]{2,1,0:T(8,128)(2,1)S(1)}, u32[]{:S(2)}, u32[]{:S(2)}) %collective-permute-start.2) | collective-permute-done | bytes 131104 | tf_op jit(solution)/shard_map/ppermute | solution.py:587
  18.4 3.2 %far.1 = (bf16[512,512]{1,0:T(8,128)(2,1)S(1)}, bf16[16,512]{1,0:T(8,128)(2,1)S(1)}, bf16[16,512]{1,0:T(8,128)(2,1)S(1)}) custom-call(s32[12,1,32]{2,1,0:T(1,128)} %bitcast.6, bf16[64,8,128]{2,1,0:T(8,128)(2,1)S(1)} %collective-permute-done.1.x_ref.refs_0_, bf16[64,8,128]{2,1,0:T(8,128)(2,1)S(1)} %collective-permute-done.2.refs_1_, ...), custom_call_target="tpu_custom_call" | custom-call | flops 58720256 | bytes 8388608 | tf_op jit(solution)/shard_map/far/pallas_call | solution.py:313
  21.6 0.0 copy-start
  21.6 2.5 %collective-permute-start.7 = (bf16[16,512]{1,0:T(8,128)(2,1)S(1)}, bf16[16,512]{1,0:T(8,128)(2,1)S(1)}, u32[]{:S(2)}, u32[]{:S(2)}) collective-permute-start(bf16[16,512]{1,0:T(8,128)(2,1)S(1)} %get-tuple-element.43), channel_id=1, source_target_pairs={{0,4},{1,5},{2,6},{3,7},{4,0},{5,1},{6,2},{7,3},{8,12},{9,13},{10,... | collective-permute-start | bytes 49160 | tf_op jit(solution)/shard_map/ppermute | solution.py:587
  24.1 1.1 %spread.1 = (bf16[11,256,384]{2,1,0:T(8,128)(2,1)S(1)}, bf16[512,1536]{1,0:T(8,128)(2,1)S(1)}) custom-call(bf16[512,512]{1,0:T(8,128)(2,1)S(1)} %get-tuple-element.45.fld_ref), custom_call_target="tpu_custom_call" | custom-call | flops 805306368 | bytes 4194304 | tf_op jit(solution)/shard_map/spread/pallas_call | solution.py:394
  25.2 0.6 %collective-permute-done.7.a_ref = bf16[16,512]{1,0:T(8,128)(2,1)S(1)} collective-permute-done((bf16[16,512]{1,0:T(8,128)(2,1)S(1)}, bf16[16,512]{1,0:T(8,128)(2,1)S(1)}, u32[]{:S(2)}, u32[]{:S(2)}) %collective-permute-start.7) | collective-permute-done | bytes 16416 | tf_op jit(solution)/shard_map/ppermute | solution.py:587
  25.9 0.2 edges.1
  26.0 0.1 collective-permute-start.10
  26.1 0.6 %collective-permute-start.9 = (bf16[16,544]{1,0:T(8,128)(2,1)S(1)}, bf16[16,544]{1,0:T(8,128)(2,1)S(1)}, u32[]{:S(2)}, u32[]{:S(2)}) collective-permute-start(bf16[16,544]{1,0:T(8,128)(2,1)S(1)} %edges.1), channel_id=1, source_target_pairs={{0,1},{1,0},{2,3},{3,2},{4,5},{5,4},{6,7},{7,6},{8,9},{9,8},{10,11... | collective-permute-start | bytes 52232 | tf_op jit(solution)/shard_map/ppermute | solution.py:587
  26.7 1.2 %prep.1 = (bf16[256,1536]{1,0:T(8,128)(2,1)S(1)}, f32[1,256]{1,0:T(1,128)S(1)}, bf16[4,512,256]{2,1,0:T(8,128)(2,1)S(1)}) custom-call(bf16[9,8,128]{2,1,0:T(8,128)(2,1)} %stem_ref.1, f32[1,128]{1,0:T(1,128)} %bitcast.8, bf16[9,128,128]{2,1,0:T(8,128)(2,1)} %mix_ref.1), custom_call_target="tpu_custom_call" | custom-call | bytes 2097152 | tf_op jit(solution)/shard_map/prep/pallas_call | solution.py:174
  28.0 1.4 %collective-permute-done.10.x_ref = bf16[16,544]{1,0:T(8,128)(2,1)S(1)} collective-permute-done((bf16[16,544]{1,0:T(8,128)(2,1)S(1)}, bf16[16,544]{1,0:T(8,128)(2,1)S(1)}, u32[]{:S(2)}, u32[]{:S(2)}) %collective-permute-start.10) | collective-permute-done | bytes 17440 | tf_op jit(solution)/shard_map/ppermute | solution.py:587
  29.4 16.9 %conv.1 = bf16[64,512,128]{2,1,0:T(8,128)(2,1)} custom-call(bf16[11,256,384]{2,1,0:T(8,128)(2,1)S(1)} %get-tuple-element.48.g_ref, bf16[16,512]{1,0:T(8,128)(2,1)S(1)} %collective-permute-done.7.a_ref, bf16[16,512]{1,0:T(8,128)(2,1)S(1)} %collective-permute-done.8.b_ref, bf16[16,544]{1,0:T(8,128)(2,1)S(1)} %collective-permute-done.9.core_ref, ...), custom_call_target="tpu_custom_call" | custom-call | flops 9663676416 | bytes 12582912 | tf_op jit(solution)/shard_map/conv/pallas_call | solution.py:561
  (8 shorter events, 0.0 us)
Async XLA Ops:
  2.1 1.8 %collective-permute-start = (bf16[160,8,128]{2,1,0:T(8,128)(2,1)S(1)}, bf16[160,8,128]{2,1,0:T(8,128)(2,1)S(1)}, u32[]{:S(2)}, u32[]{:S(2)}) collective-permute-start(bf16[160,8,128]{2,1,0:T(8,128)(2,1)S(1)} %get-tuple-element.30), channel_id=1, source_target_pairs={{0,1},{1,0},{2,3},{3,2},{4,5},{5,4},{6,7},{7,6},{8,9},{9,8},{10,11... | collective-permute-start | bytes 983048 | tf_op jit(solution)/shard_map/ppermute | solution.py:587
  3.9 7.3 %collective-permute-start.1 = (bf16[64,8,128]{2,1,0:T(8,128)(2,1)S(1)}, bf16[64,8,128]{2,1,0:T(8,128)(2,1)S(1)}, u32[]{:S(2)}, u32[]{:S(2)}) collective-permute-start(bf16[64,8,128]{2,1,0:T(8,128)(2,1)S(1)} %get-tuple-element.34), channel_id=1, source_target_pairs={{0,3},{1,2},{2,1},{3,0},{4,7},{5,6},{6,5},{7,4},{8,11},{9,10},{10,... | collective-permute-start | bytes 393224 | tf_op jit(solution)/shard_map/ppermute | solution.py:587
  6.6 11.8 %collective-permute-start.2 = (bf16[64,8,128]{2,1,0:T(8,128)(2,1)S(1)}, bf16[64,8,128]{2,1,0:T(8,128)(2,1)S(1)}, u32[]{:S(2)}, u32[]{:S(2)}) collective-permute-start(bf16[64,8,128]{2,1,0:T(8,128)(2,1)S(1)} %get-tuple-element.35), channel_id=1, source_target_pairs={{0,4},{1,5},{2,6},{3,7},{4,0},{5,1},{6,2},{7,3},{8,12},{9,13},{10,... | collective-permute-start | bytes 393224 | tf_op jit(solution)/shard_map/ppermute | solution.py:587
  8.1 10.3 %collective-permute-start.5 = (bf16[64,8,128]{2,1,0:T(8,128)(2,1)S(1)}, bf16[64,8,128]{2,1,0:T(8,128)(2,1)S(1)}, u32[]{:S(2)}, u32[]{:S(2)}) collective-permute-start(bf16[64,8,128]{2,1,0:T(8,128)(2,1)S(1)} %get-tuple-element.38), channel_id=1, source_target_pairs={{0,1},{1,0},{2,3},{3,2},{4,8},{5,9},{6,10},{7,11},{8,4},{9,5},{10,... | collective-permute-start | bytes 393224 | tf_op jit(solution)/shard_map/ppermute | solution.py:587
  8.2 8.6 %collective-permute-start.3 = (bf16[32,8,128]{2,1,0:T(8,128)(2,1)S(1)}, bf16[32,8,128]{2,1,0:T(8,128)(2,1)S(1)}, u32[]{:S(2)}, u32[]{:S(2)}) collective-permute-start(bf16[32,8,128]{2,1,0:T(8,128)(2,1)S(1)} %get-tuple-element.36), channel_id=1, source_target_pairs={{0,7},{1,6},{2,5},{3,4},{4,3},{5,2},{6,1},{7,0},{8,15},{9,14},{10,... | collective-permute-start | bytes 196616 | tf_op jit(solution)/shard_map/ppermute | solution.py:587
  10.5 6.2 %collective-permute-start.6 = (bf16[32,8,128]{2,1,0:T(8,128)(2,1)S(1)}, bf16[32,8,128]{2,1,0:T(8,128)(2,1)S(1)}, u32[]{:S(2)}, u32[]{:S(2)}) collective-permute-start(bf16[32,8,128]{2,1,0:T(8,128)(2,1)S(1)} %get-tuple-element.39), channel_id=1, source_target_pairs={{0,1},{1,0},{2,3},{3,2},{4,11},{5,10},{6,9},{7,8},{8,7},{9,6},{10,... | collective-permute-start | bytes 196616 | tf_op jit(solution)/shard_map/ppermute | solution.py:587
  11.2 5.5 %collective-permute-start.4 = (bf16[32,8,128]{2,1,0:T(8,128)(2,1)S(1)}, bf16[32,8,128]{2,1,0:T(8,128)(2,1)S(1)}, u32[]{:S(2)}, u32[]{:S(2)}) collective-permute-start(bf16[32,8,128]{2,1,0:T(8,128)(2,1)S(1)} %get-tuple-element.37), channel_id=1, source_target_pairs={{0,7},{1,6},{2,5},{3,4},{4,3},{5,2},{6,1},{7,0},{8,9},{9,8},{10,11... | collective-permute-start | bytes 196616 | tf_op jit(solution)/shard_map/ppermute | solution.py:587
  21.6 7.9 %copy-start = (f32[128]{0:T(128)S(1)}, f32[128]{0:T(128)}, u32[]{:S(2)}) copy-start(f32[128]{0:T(128)} %param.15) | copy-start | bytes 1540
  21.6 4.3 %collective-permute-start.7 = (bf16[16,512]{1,0:T(8,128)(2,1)S(1)}, bf16[16,512]{1,0:T(8,128)(2,1)S(1)}, u32[]{:S(2)}, u32[]{:S(2)}) collective-permute-start(bf16[16,512]{1,0:T(8,128)(2,1)S(1)} %get-tuple-element.43), channel_id=1, source_target_pairs={{0,4},{1,5},{2,6},{3,7},{4,0},{5,1},{6,2},{7,3},{8,12},{9,13},{10,... | collective-permute-start | bytes 49160 | tf_op jit(solution)/shard_map/ppermute | solution.py:587
  24.1 1.7 %collective-permute-start.8 = (bf16[16,512]{1,0:T(8,128)(2,1)S(1)}, bf16[16,512]{1,0:T(8,128)(2,1)S(1)}, u32[]{:S(2)}, u32[]{:S(2)}) collective-permute-start(bf16[16,512]{1,0:T(8,128)(2,1)S(1)} %get-tuple-element.44), channel_id=1, source_target_pairs={{0,1},{1,0},{2,3},{3,2},{4,8},{5,9},{6,10},{7,11},{8,4},{9,5},{10,... | collective-permute-start | bytes 49160 | tf_op jit(solution)/shard_map/ppermute | solution.py:587
  26.0 3.4 %collective-permute-start.10 = (bf16[16,544]{1,0:T(8,128)(2,1)S(1)}, bf16[16,544]{1,0:T(8,128)(2,1)S(1)}, u32[]{:S(2)}, u32[]{:S(2)}) collective-permute-start(bf16[16,544]{1,0:T(8,128)(2,1)S(1)} %edges.1), channel_id=1, source_target_pairs={{0,3},{1,2},{2,1},{3,0},{4,7},{5,6},{6,5},{7,4},{8,11},{9,10},{10,... | collective-permute-start | bytes 52232 | tf_op jit(solution)/shard_map/ppermute | solution.py:587
  26.1 3.3 %collective-permute-start.9 = (bf16[16,544]{1,0:T(8,128)(2,1)S(1)}, bf16[16,544]{1,0:T(8,128)(2,1)S(1)}, u32[]{:S(2)}, u32[]{:S(2)}) collective-permute-start(bf16[16,544]{1,0:T(8,128)(2,1)S(1)} %edges.1), channel_id=1, source_target_pairs={{0,1},{1,0},{2,3},{3,2},{4,5},{5,4},{6,7},{7,6},{8,9},{9,8},{10,11... | collective-permute-start | bytes 52232 | tf_op jit(solution)/shard_map/ppermute | solution.py:587

commit v6 on v5

--- a/solution.py
+++ b/solution.py
@@ -142,7 +142,24 @@
     )(core, x, a, b)
 
 
-def prep_kernel(stem_ref, bias_ref, mix_ref, ws_ref, bs_ref, wm_ref):
+def prep_kernel(last, stem_ref, bias_ref, mix_ref, a_ref, b_ref, hot_ref, ws_ref, bs_ref, wm_ref, rim):
+    band = lax.axis_index("band")
+    a, b = a_ref[...], b_ref[...]
+    b = jnp.where((band == 0) | (band == last), jnp.zeros_like(b), b)
+    even = band % 2 == 0
+    rows = jnp.concatenate([jnp.where(even, b, a), jnp.where(even, a, b)], axis=0)
+    rim[...] = jnp.zeros_like(rim)
+    for pair in range(2):
+        for tile in range(3):
+            at = (2 * tile + pair) * 256
+            value = jnp.dot(rows, hot_ref[:, at : at + 256], preferred_element_type=F32).astype(BF)
+            for half in range(2):
+                d0 = (2 * pair + half) * 64
+                lanes = slice(tile * 128, tile * 128 + 128)
+                part = value[:, half * 128 : half * 128 + 128]
+                rim[0, d0 : d0 + 16, lanes] = part[0:16]
+                rim[1, d0 + 48 : d0 + 64, lanes] = part[16:32]
+
     for par in range(2):
         bs_ref[:, par * 128 : par * 128 + 128] = bias_ref[...] * SCALE
     zero8 = jnp.zeros((8, 128), F32)
@@ -170,20 +187,21 @@
         wm_ref[k, 384:512, 0:128] = zero
 
 
-def prep(stem_weight, stem_bias, mix_weight):
-    return pl.pallas_call(
-        prep_kernel,
-        in_specs=[VM] * 3,
-        out_specs=[VM] * 3,
+def prep(n_band, stem_weight, stem_bias, mix_weight, a, b, hot):
+    return pl.pallas_call(
+        functools.partial(prep_kernel, n_band - 1),
+        in_specs=[VM] * 6,
+        out_specs=[VM] * 4,
         out_shape=[
             jax.ShapeDtypeStruct((256, STEP * 256), BF),
             jax.ShapeDtypeStruct((1, 256), F32),
             jax.ShapeDtypeStruct((4, 512, 256), BF),
+            jax.ShapeDtypeStruct((3, 256, LANES), BF),
         ],
         compiler_params=params(12),
         cost_estimate=cost(0, 2 << 20),
         name="prep",
-    )(*in_hbm(stem_weight, stem_bias[None], mix_weight))
+    )(*in_hbm(stem_weight, stem_bias[None], mix_weight), a, b, hot)
 
 
 def group_codes(last, codes_ref):
@@ -223,9 +241,9 @@
 
 
 def near_kernel(last, win_hbm, own_ref, core_ref, x_ref, w_hbm, acc, early_ref, w_ref, inc, codes_ref, win_ref, sem, early_sem, win_sem):
-    group_codes(last, codes_ref)
     window = pltpu.make_async_copy(win_hbm, win_ref, win_sem)
     window.start()
+    group_codes(last, codes_ref)
 
     def copy(g):
         return pltpu.make_async_copy(w_hbm.at[0, codes_ref[g]], w_ref.at[g], sem.at[g])
@@ -251,9 +269,9 @@
     (x_in, a_in, ax_in, far_in, b_in, bx_in), refs = refs[:6], refs[6:]
     near_ref, early_ref, w_hbm, fld_ref, a_ref, b_ref = refs[:6]
     acc, w_ref, inc, codes_ref, win_ref, sem, win_sem = refs[6:]
-    group_codes(last, codes_ref)
     window = pltpu.make_async_copy(win_hbm, win_ref, win_sem)
     window.start()
+    group_codes(last, codes_ref)
 
     def copy(g):
         return pltpu.make_async_copy(
@@ -405,23 +423,7 @@
     )(fld)
 
 
-def halos(last, a_ref, b_ref, core_ref, x_ref, hot_ref, rim, left_ref, right_ref):
-    band = lax.axis_index("band")
-    a, b = a_ref[...], b_ref[...]
-    b = jnp.where((band == 0) | (band == last), jnp.zeros_like(b), b)
-    even = band % 2 == 0
-    rows = jnp.concatenate([jnp.where(even, b, a), jnp.where(even, a, b)], axis=0)
-    rim[...] = jnp.zeros_like(rim)
-    for pair in range(2):
-        for tile in range(3):
-            at = (2 * tile + pair) * 256
-            value = jnp.dot(rows, hot_ref[:, at : at + 256], preferred_element_type=F32).astype(BF)
-            for half in range(2):
-                d0 = (2 * pair + half) * 64
-                lanes = slice(tile * 128, tile * 128 + 128)
-                part = value[:, half * 128 : half * 128 + 128]
-                rim[0, d0 : d0 + 16, lanes] = part[0:16]
-                rim[1, d0 + 48 : d0 + 64, lanes] = part[16:32]
+def halos(core_ref, x_ref, left_ref, right_ref):
     even = lax.axis_index("lon") % 2 == 0
     core, x = core_ref[...].astype(F32), x_ref[...].astype(F32)
     right, left = jnp.where(even, core, x), jnp.where(even, x, core)
@@ -445,17 +447,14 @@
 def conv_kernel(
     last,
     g_ref,
-    a_ref,
-    b_ref,
     core_ref,
     x_ref,
     ws_ref,
     bs_ref,
     wm_ref,
     bm_ref,
-    hot_ref,
+    rim,
     out_ref,
-    rim,
     left_ref,
     right_ref,
     hs,
@@ -487,7 +486,7 @@
                 h = h * high
             hs[block % 2, i] = h.astype(BF)
 
-    halos(last, a_ref, b_ref, core_ref, x_ref, hot_ref, rim, left_ref, right_ref)
+    halos(core_ref, x_ref, left_ref, right_ref)
     stem(0, range(STEP), jnp.where(band == 0, 0.0, 1.0), None)
 
     def copy(at, slot):
@@ -524,11 +523,12 @@
                 h = [both(r) for r in range(4)]
                 v = [h[0] - h[2], h[1] + h[2], h[2] - h[1], h[1] - h[3]]
                 m = [jnp.dot(v[k], wm_ref[k], preferred_element_type=F32) for k in range(4)]
+                m[1] = m[1] + jnp.concatenate([bm_ref[...], bm_ref[...]], axis=1)
                 plus, minus = m[1] + m[2], m[1] - m[2]
                 for q, y in enumerate([plus + m[0], minus - m[3]]):
                     row = 2 * t + q
                     for par in range(2):
-                        part = y[:, par * 128 : par * 128 + 128] + bm_ref[...]
+                        part = y[:, par * 128 : par * 128 + 128]
                         for k in range(CHUNK // SUB):
                             to = pl.ds(2 * (c * CHUNK // SUB + k) + par, SUB, stride=PITCH)
                             ys[row, to, :] = part[k * SUB : k * SUB + SUB]
@@ -556,15 +556,14 @@
     copy(BLOCKS - 1, (BLOCKS - 1) % 2).wait()
 
 
-def conv(n_band, g, a, b, core, x, ws, bs, wm, bm, hot):
+def conv(n_band, g, core, x, ws, bs, wm, bm, rim):
     channels = bm.shape[-1]
     return pl.pallas_call(
         functools.partial(conv_kernel, n_band - 1),
-        in_specs=[VM] * 10,
+        in_specs=[VM] * 8,
         out_specs=ANY,
         out_shape=jax.ShapeDtypeStruct((ROWS, COLS, channels), BF),
         scratch_shapes=[
-            pltpu.VMEM((3, 256, LANES), BF),
             pltpu.VMEM((BLOCKS, 128, 128), BF),
             pltpu.VMEM((BLOCKS, 128, 128), BF),
             pltpu.VMEM((2, STEP, HROWS, 256), BF),
@@ -575,7 +574,7 @@
         compiler_params=params(20),
         cost_estimate=cost(2 * ROWS * COLS * 9 * 128 * 128, 12 << 20),
         name="conv",
-    )(g, a, b, core, x, ws, bs, wm, bm, hot)
+    )(g, core, x, ws, bs, wm, bm, rim)
 
 
 def on_device(source, routes, slot_weights, window, stem_weight, stem_bias, mix_weight, mix_bias):
@@ -602,10 +601,8 @@
     edge = edges(n_band, fld, a_halo, b_halo)
     core_edge = move(edge, "", "core")
     x_edge = move(edge, "", "x")
-    ws, bs, wm = prep(stem_weight, stem_bias, mix_weight)
-    return conv(
-        n_band, g, a_halo, b_halo, core_edge, x_edge, ws, bs, wm, mix_bias[None], hot
-    )
+    ws, bs, wm, rim = prep(n_band, stem_weight, stem_bias, mix_weight, a_halo, b_halo, hot)
+    return conv(n_band, g, core_edge, x_edge, ws, bs, wm, mix_bias[None], rim)
 
 
 def solution(mesh):

time: 46.5 us -> 46.1 us (level)
  transfers between devices with their start and end apart: 11 -> 11, of which waited for: 4 -> 4; matrix products, arithmetic and copies ran while one was open for 0% -> 0% of each run, Pallas kernels for 11% -> 12%
where the time goes in v6:
time: 46.1 us; the launch traced here: 46 us
  Pallas kernels  27.3 us (59%)
  starting transfers between devices  14 us (30%)
  waiting for transfers between devices  4.56 us (10%)
    pallas_call x1, Pallas kernels, conv(): pl.pallas_call(functools.partial(conv_kernel, n_band - 1), in_specs=[VM]...  16.5 us
    ppermute x11, starting transfers between devices, move(): return lax.ppermute(value, axes, swap(n_band, n_lon, way, turn))  14 us
    ppermute x11, waiting for transfers between devices, move(): return lax.ppermute(value, axes, swap(n_band, n_lon, way, turn))  4.56 us
    pallas_call x1, Pallas kernels, far_part(): pl.pallas_call(functools.partial(far_kernel, n_band - 1), in_specs=[HBM]...  3.15 us
    pallas_call x1, Pallas kernels, near_part(): pl.pallas_call(functools.partial(near_kernel, n_band - 1), in_specs=[HBM]...  2.55 us
    pallas_call x1, Pallas kernels, pack(): pl.pallas_call(pack_kernel, in_specs=[HBM, HBM], out_specs=[VM] * 7, out_...  2.1 us
    pallas_call x1, Pallas kernels, prep(): pl.pallas_call(functools.partial(prep_kernel, n_band - 1), in_specs=[VM]...  1.66 us
    pallas_call x1, Pallas kernels, spread(): pl.pallas_call(spread_kernel, in_specs=[VM], out_specs=[VM] * 2, out_shap...  1.08 us
  transfers between devices with their start and end apart: 11, of which 4 were waited for; matrix products, arithmetic and copies ran while one was open for 0% of the time, Pallas kernels for 12%

profile of v6, /device:TPU:0, one launch (start us, length us, event | category | flops | bytes accessed | tf_op | source)
XLA Modules:
  0.0 46.0 jit_solution(12359953268837832107)
XLA Ops:
  0.0 2.1 %pack.1 = (bf16[32,8,128]{2,1,0:T(8,128)(2,1)S(1)}, bf16[160,8,128]{2,1,0:T(8,128)(2,1)S(1)}, bf16[32,8,128]{2,1,0:T(8,128)(2,1)S(1)}, bf16[32,8,128]{2,1,0:T(8,...) custom-call(s32[2,128]{1,0:T(2,128)} %bitcast.7, ...), custom_call_target="tpu_custom_call" | custom-call | bytes 1048576 | tf_op jit(solution)/shard_map/pack/pallas_call | solution.py:107
  2.1 0.5 %collective-permute-start = (bf16[160,8,128]{2,1,0:T(8,128)(2,1)S(1)}, bf16[160,8,128]{2,1,0:T(8,128)(2,1)S(1)}, u32[]{:S(2)}, u32[]{:S(2)}) collective-permute-start(bf16[160,8,128]{2,1,0:T(8,128)(2,1)S(1)} %get-tuple-element.31), channel_id=1, source_target_pairs={{0,1},{1,0},{2,3},{3,2},{4,5},{5,4},{6,7},{7,6},{8,9},{9,8},{10,11... | collective-permute-start | bytes 983048 | tf_op jit(solution)/shard_map/ppermute | solution.py:586
  2.6 1.3 %collective-permute-done.core_ref = bf16[160,8,128]{2,1,0:T(8,128)(2,1)S(1)} collective-permute-done((bf16[160,8,128]{2,1,0:T(8,128)(2,1)S(1)}, bf16[160,8,128]{2,1,0:T(8,128)(2,1)S(1)}, u32[]{:S(2)}, u32[]{:S(2)}) %collective-permute-start) | collective-permute-done | bytes 327712 | tf_op jit(solution)/shard_map/ppermute | solution.py:586
  3.9 2.7 %collective-permute-start.1 = (bf16[64,8,128]{2,1,0:T(8,128)(2,1)S(1)}, bf16[64,8,128]{2,1,0:T(8,128)(2,1)S(1)}, u32[]{:S(2)}, u32[]{:S(2)}) collective-permute-start(bf16[64,8,128]{2,1,0:T(8,128)(2,1)S(1)} %get-tuple-element.35), channel_id=1, source_target_pairs={{0,3},{1,2},{2,1},{3,0},{4,7},{5,6},{6,5},{7,4},{8,11},{9,10},{10,... | collective-permute-start | bytes 393224 | tf_op jit(solution)/shard_map/ppermute | solution.py:586
  6.6 1.5 %collective-permute-start.2 = (bf16[64,8,128]{2,1,0:T(8,128)(2,1)S(1)}, bf16[64,8,128]{2,1,0:T(8,128)(2,1)S(1)}, u32[]{:S(2)}, u32[]{:S(2)}) collective-permute-start(bf16[64,8,128]{2,1,0:T(8,128)(2,1)S(1)} %get-tuple-element.36), channel_id=1, source_target_pairs={{0,4},{1,5},{2,6},{3,7},{4,0},{5,1},{6,2},{7,3},{8,12},{9,13},{10,... | collective-permute-start | bytes 393224 | tf_op jit(solution)/shard_map/ppermute | solution.py:586
  8.1 0.1 collective-permute-start.5
  8.2 2.3 %collective-permute-start.3 = (bf16[32,8,128]{2,1,0:T(8,128)(2,1)S(1)}, bf16[32,8,128]{2,1,0:T(8,128)(2,1)S(1)}, u32[]{:S(2)}, u32[]{:S(2)}) collective-permute-start(bf16[32,8,128]{2,1,0:T(8,128)(2,1)S(1)} %get-tuple-element.37), channel_id=1, source_target_pairs={{0,7},{1,6},{2,5},{3,4},{4,3},{5,2},{6,1},{7,0},{8,15},{9,14},{10,... | collective-permute-start | bytes 196616 | tf_op jit(solution)/shard_map/ppermute | solution.py:586
  10.5 0.7 %collective-permute-start.6 = (bf16[32,8,128]{2,1,0:T(8,128)(2,1)S(1)}, bf16[32,8,128]{2,1,0:T(8,128)(2,1)S(1)}, u32[]{:S(2)}, u32[]{:S(2)}) collective-permute-start(bf16[32,8,128]{2,1,0:T(8,128)(2,1)S(1)} %get-tuple-element.40), channel_id=1, source_target_pairs={{0,1},{1,0},{2,3},{3,2},{4,11},{5,10},{6,9},{7,8},{8,7},{9,6},{10,... | collective-permute-start | bytes 196616 | tf_op jit(solution)/shard_map/ppermute | solution.py:586
  11.2 0.0 collective-permute-done.1.x_ref.refs_0_
  11.2 2.9 %collective-permute-start.4 = (bf16[32,8,128]{2,1,0:T(8,128)(2,1)S(1)}, bf16[32,8,128]{2,1,0:T(8,128)(2,1)S(1)}, u32[]{:S(2)}, u32[]{:S(2)}) collective-permute-start(bf16[32,8,128]{2,1,0:T(8,128)(2,1)S(1)} %get-tuple-element.38), channel_id=1, source_target_pairs={{0,7},{1,6},{2,5},{3,4},{4,3},{5,2},{6,1},{7,0},{8,9},{9,8},{10,11... | collective-permute-start | bytes 196616 | tf_op jit(solution)/shard_map/ppermute | solution.py:586
  14.2 2.5 %near.1 = (f32[256,8,128]{2,1,0:T(8,128)S(1)}, bf16[2,32,128,128]{3,2,1,0:T(8,128)(2,1)S(1)}) custom-call(s32[12,1,32]{2,1,0:T(1,128)} %bitcast.5, bf16[32,8,128]{2,1,0:T(8,128)(2,1)S(1)} %get-tuple-element.41.own_ref, bf16[160,8,128]{2,1,0:T(8,128)(2,1)S(1)} %collective-permute-done.core_ref, bf16[64,8,128]{2,1,0:T(8,128)(2,1)S(1)} %collective-permute-done.1.x_ref.refs_0_, ...), custom_call_target="tpu_custom_call" | custom-call | flops 25165824 | bytes 12582912 | tf_op jit(solution)/shard_map/near/pallas_call | solution.py:306
  16.7 0.0 collective-permute-done.3.refs_2_
  16.8 1.6 %collective-permute-done.2.refs_1_ = bf16[64,8,128]{2,1,0:T(8,128)(2,1)S(1)} collective-permute-done((bf16[64,8,128]{2,1,0:T(8,128)(2,1)S(1)}, bf16[64,8,128]{2,1,0:T(8,128)(2,1)S(1)}, u32[]{:S(2)}, u32[]{:S(2)}) %collective-permute-start.2) | collective-permute-done | bytes 131104 | tf_op jit(solution)/shard_map/ppermute | solution.py:586
  18.4 3.2 %far.1 = (bf16[512,512]{1,0:T(8,128)(2,1)S(1)}, bf16[16,512]{1,0:T(8,128)(2,1)S(1)}, bf16[16,512]{1,0:T(8,128)(2,1)S(1)}) custom-call(s32[12,1,32]{2,1,0:T(1,128)} %bitcast.6, bf16[64,8,128]{2,1,0:T(8,128)(2,1)S(1)} %collective-permute-done.1.x_ref.refs_0_, bf16[64,8,128]{2,1,0:T(8,128)(2,1)S(1)} %collective-permute-done.2.refs_1_, ...), custom_call_target="tpu_custom_call" | custom-call | flops 58720256 | bytes 8388608 | tf_op jit(solution)/shard_map/far/pallas_call | solution.py:331
  21.6 2.5 %collective-permute-start.7 = (bf16[16,512]{1,0:T(8,128)(2,1)S(1)}, bf16[16,512]{1,0:T(8,128)(2,1)S(1)}, u32[]{:S(2)}, u32[]{:S(2)}) collective-permute-start(bf16[16,512]{1,0:T(8,128)(2,1)S(1)} %get-tuple-element.44), channel_id=1, source_target_pairs={{0,4},{1,5},{2,6},{3,7},{4,0},{5,1},{6,2},{7,3},{8,12},{9,13},{10,... | collective-permute-start | bytes 49160 | tf_op jit(solution)/shard_map/ppermute | solution.py:586
  24.1 0.0 collective-permute-start.8
  24.1 1.1 %spread.1 = (bf16[11,256,384]{2,1,0:T(8,128)(2,1)S(1)}, bf16[512,1536]{1,0:T(8,128)(2,1)S(1)}) custom-call(bf16[512,512]{1,0:T(8,128)(2,1)S(1)} %get-tuple-element.46.fld_ref), custom_call_target="tpu_custom_call" | custom-call | flops 805306368 | bytes 4194304 | tf_op jit(solution)/shard_map/spread/pallas_call | solution.py:412
  25.2 0.6 %collective-permute-done.7.a_ref = bf16[16,512]{1,0:T(8,128)(2,1)S(1)} collective-permute-done((bf16[16,512]{1,0:T(8,128)(2,1)S(1)}, bf16[16,512]{1,0:T(8,128)(2,1)S(1)}, u32[]{:S(2)}, u32[]{:S(2)}) %collective-permute-start.7) | collective-permute-done | bytes 16416 | tf_op jit(solution)/shard_map/ppermute | solution.py:586
  25.8 0.2 edges.1
  26.0 0.1 collective-permute-start.10
  26.1 0.6 %collective-permute-start.9 = (bf16[16,544]{1,0:T(8,128)(2,1)S(1)}, bf16[16,544]{1,0:T(8,128)(2,1)S(1)}, u32[]{:S(2)}, u32[]{:S(2)}) collective-permute-start(bf16[16,544]{1,0:T(8,128)(2,1)S(1)} %edges.1), channel_id=1, source_target_pairs={{0,1},{1,0},{2,3},{3,2},{4,5},{5,4},{6,7},{7,6},{8,9},{9,8},{10,11... | collective-permute-start | bytes 52232 | tf_op jit(solution)/shard_map/ppermute | solution.py:586
  26.7 1.7 %prep.1 = (bf16[256,1536]{1,0:T(8,128)(2,1)S(1)}, f32[1,256]{1,0:T(1,128)S(1)}, bf16[4,512,256]{2,1,0:T(8,128)(2,1)S(1)}, bf16[3,256,384]{2,1,0:T(8,128)(2,1)S(1)}) custom-call(bf16[9,8,128]{2,1,0:T(8,128)(2,1)} %stem_ref.1, f32[1,128]{1,0:T(1,128)} %bitcast.8, bf16[9,128,128]{2,1,0:T(8,128)(2,1)} %mix_ref.1, ...), custom_call_target="tpu_custom_call" | custom-call | bytes 2097152 | tf_op jit(solution)/shard_map/prep/pallas_call | solution.py:191
  28.4 1.0 %collective-permute-done.10.x_ref = bf16[16,544]{1,0:T(8,128)(2,1)S(1)} collective-permute-done((bf16[16,544]{1,0:T(8,128)(2,1)S(1)}, bf16[16,544]{1,0:T(8,128)(2,1)S(1)}, u32[]{:S(2)}, u32[]{:S(2)}) %collective-permute-start.10) | collective-permute-done | bytes 17440 | tf_op jit(solution)/shard_map/ppermute | solution.py:586
  29.4 16.5 %conv.1 = bf16[64,512,128]{2,1,0:T(8,128)(2,1)} custom-call(bf16[11,256,384]{2,1,0:T(8,128)(2,1)S(1)} %get-tuple-element.49.g_ref, bf16[16,544]{1,0:T(8,128)(2,1)S(1)} %collective-permute-done.9.core_ref, bf16[16,544]{1,0:T(8,128)(2,1)S(1)} %collective-permute-done.10.x_ref, bf16[256,1536]{1,0:T(8,128)(2,1)S(1)} %get-tuple-element.53.ws_ref, ...), custom_call_target="tpu_custom_call" | custom-call | flops 9663676416 | bytes 12582912 | tf_op jit(solution)/shard_map/conv/pallas_call | solution.py:561
  (8 shorter events, 0.0 us)
Async XLA Ops:
  2.1 1.8 %collective-permute-start = (bf16[160,8,128]{2,1,0:T(8,128)(2,1)S(1)}, bf16[160,8,128]{2,1,0:T(8,128)(2,1)S(1)}, u32[]{:S(2)}, u32[]{:S(2)}) collective-permute-start(bf16[160,8,128]{2,1,0:T(8,128)(2,1)S(1)} %get-tuple-element.31), channel_id=1, source_target_pairs={{0,1},{1,0},{2,3},{3,2},{4,5},{5,4},{6,7},{7,6},{8,9},{9,8},{10,11... | collective-permute-start | bytes 983048 | tf_op jit(solution)/shard_map/ppermute | solution.py:586
  3.9 7.3 %collective-permute-start.1 = (bf16[64,8,128]{2,1,0:T(8,128)(2,1)S(1)}, bf16[64,8,128]{2,1,0:T(8,128)(2,1)S(1)}, u32[]{:S(2)}, u32[]{:S(2)}) collective-permute-start(bf16[64,8,128]{2,1,0:T(8,128)(2,1)S(1)} %get-tuple-element.35), channel_id=1, source_target_pairs={{0,3},{1,2},{2,1},{3,0},{4,7},{5,6},{6,5},{7,4},{8,11},{9,10},{10,... | collective-permute-start | bytes 393224 | tf_op jit(solution)/shard_map/ppermute | solution.py:586
  6.6 11.8 %collective-permute-start.2 = (bf16[64,8,128]{2,1,0:T(8,128)(2,1)S(1)}, bf16[64,8,128]{2,1,0:T(8,128)(2,1)S(1)}, u32[]{:S(2)}, u32[]{:S(2)}) collective-permute-start(bf16[64,8,128]{2,1,0:T(8,128)(2,1)S(1)} %get-tuple-element.36), channel_id=1, source_target_pairs={{0,4},{1,5},{2,6},{3,7},{4,0},{5,1},{6,2},{7,3},{8,12},{9,13},{10,... | collective-permute-start | bytes 393224 | tf_op jit(solution)/shard_map/ppermute | solution.py:586
  8.1 10.3 %collective-permute-start.5 = (bf16[64,8,128]{2,1,0:T(8,128)(2,1)S(1)}, bf16[64,8,128]{2,1,0:T(8,128)(2,1)S(1)}, u32[]{:S(2)}, u32[]{:S(2)}) collective-permute-start(bf16[64,8,128]{2,1,0:T(8,128)(2,1)S(1)} %get-tuple-element.39), channel_id=1, source_target_pairs={{0,1},{1,0},{2,3},{3,2},{4,8},{5,9},{6,10},{7,11},{8,4},{9,5},{10,... | collective-permute-start | bytes 393224 | tf_op jit(solution)/shard_map/ppermute | solution.py:586
  8.2 8.6 %collective-permute-start.3 = (bf16[32,8,128]{2,1,0:T(8,128)(2,1)S(1)}, bf16[32,8,128]{2,1,0:T(8,128)(2,1)S(1)}, u32[]{:S(2)}, u32[]{:S(2)}) collective-permute-start(bf16[32,8,128]{2,1,0:T(8,128)(2,1)S(1)} %get-tuple-element.37), channel_id=1, source_target_pairs={{0,7},{1,6},{2,5},{3,4},{4,3},{5,2},{6,1},{7,0},{8,15},{9,14},{10,... | collective-permute-start | bytes 196616 | tf_op jit(solution)/shard_map/ppermute | solution.py:586
  10.5 6.2 %collective-permute-start.6 = (bf16[32,8,128]{2,1,0:T(8,128)(2,1)S(1)}, bf16[32,8,128]{2,1,0:T(8,128)(2,1)S(1)}, u32[]{:S(2)}, u32[]{:S(2)}) collective-permute-start(bf16[32,8,128]{2,1,0:T(8,128)(2,1)S(1)} %get-tuple-element.40), channel_id=1, source_target_pairs={{0,1},{1,0},{2,3},{3,2},{4,11},{5,10},{6,9},{7,8},{8,7},{9,6},{10,... | collective-permute-start | bytes 196616 | tf_op jit(solution)/shard_map/ppermute | solution.py:586
  11.2 5.5 %collective-permute-start.4 = (bf16[32,8,128]{2,1,0:T(8,128)(2,1)S(1)}, bf16[32,8,128]{2,1,0:T(8,128)(2,1)S(1)}, u32[]{:S(2)}, u32[]{:S(2)}) collective-permute-start(bf16[32,8,128]{2,1,0:T(8,128)(2,1)S(1)} %get-tuple-element.38), channel_id=1, source_target_pairs={{0,7},{1,6},{2,5},{3,4},{4,3},{5,2},{6,1},{7,0},{8,9},{9,8},{10,11... | collective-permute-start | bytes 196616 | tf_op jit(solution)/shard_map/ppermute | solution.py:586
  21.6 4.3 %collective-permute-start.7 = (bf16[16,512]{1,0:T(8,128)(2,1)S(1)}, bf16[16,512]{1,0:T(8,128)(2,1)S(1)}, u32[]{:S(2)}, u32[]{:S(2)}) collective-permute-start(bf16[16,512]{1,0:T(8,128)(2,1)S(1)} %get-tuple-element.44), channel_id=1, source_target_pairs={{0,4},{1,5},{2,6},{3,7},{4,0},{5,1},{6,2},{7,3},{8,12},{9,13},{10,... | collective-permute-start | bytes 49160 | tf_op jit(solution)/shard_map/ppermute | solution.py:586
  24.1 1.7 %collective-permute-start.8 = (bf16[16,512]{1,0:T(8,128)(2,1)S(1)}, bf16[16,512]{1,0:T(8,128)(2,1)S(1)}, u32[]{:S(2)}, u32[]{:S(2)}) collective-permute-start(bf16[16,512]{1,0:T(8,128)(2,1)S(1)} %get-tuple-element.45), channel_id=1, source_target_pairs={{0,1},{1,0},{2,3},{3,2},{4,8},{5,9},{6,10},{7,11},{8,4},{9,5},{10,... | collective-permute-start | bytes 49160 | tf_op jit(solution)/shard_map/ppermute | solution.py:586
  24.1 5.3 %copy-start = (f32[128]{0:T(128)S(1)}, f32[128]{0:T(128)}, u32[]{:S(2)}) copy-start(f32[128]{0:T(128)} %param.15) | copy-start | bytes 1540
  26.0 3.4 %collective-permute-start.10 = (bf16[16,544]{1,0:T(8,128)(2,1)S(1)}, bf16[16,544]{1,0:T(8,128)(2,1)S(1)}, u32[]{:S(2)}, u32[]{:S(2)}) collective-permute-start(bf16[16,544]{1,0:T(8,128)(2,1)S(1)} %edges.1), channel_id=1, source_target_pairs={{0,3},{1,2},{2,1},{3,0},{4,7},{5,6},{6,5},{7,4},{8,11},{9,10},{10,... | collective-permute-start | bytes 52232 | tf_op jit(solution)/shard_map/ppermute | solution.py:586
  26.1 3.3 %collective-permute-start.9 = (bf16[16,544]{1,0:T(8,128)(2,1)S(1)}, bf16[16,544]{1,0:T(8,128)(2,1)S(1)}, u32[]{:S(2)}, u32[]{:S(2)}) collective-permute-start(bf16[16,544]{1,0:T(8,128)(2,1)S(1)} %edges.1), channel_id=1, source_target_pairs={{0,1},{1,0},{2,3},{3,2},{4,5},{5,4},{6,7},{7,6},{8,9},{9,8},{10,11... | collective-permute-start | bytes 52232 | tf_op jit(solution)/shard_map/ppermute | solution.py:586

commit v7 on v6

--- a/solution.py
+++ b/solution.py
@@ -567,7 +567,7 @@
             pltpu.VMEM((BLOCKS, 128, 128), BF),
             pltpu.VMEM((BLOCKS, 128, 128), BF),
             pltpu.VMEM((2, STEP, HROWS, 256), BF),
-            pltpu.VMEM((STEP, SUB * PITCH, channels), F32),
+            pltpu.VMEM((STEP, (SUB + 1) * PITCH + 7, channels), F32),
             pltpu.VMEM((2, STEP, COLS, channels), BF),
             pltpu.SemaphoreType.DMA((2,)),
         ],

time: 46.1 us -> 46.1 us (level)
  no operation moved by 1% of the time
where the time goes in v7:
time: 46.1 us; the launch traced here: 45.9 us
  Pallas kernels  27.2 us (59%)
  starting transfers between devices  14 us (30%)
  waiting for transfers between devices  4.56 us (10%)
    pallas_call x1, Pallas kernels, conv(): pl.pallas_call(functools.partial(conv_kernel, n_band - 1), in_specs=[VM]...  16.5 us
    ppermute x11, starting transfers between devices, move(): return lax.ppermute(value, axes, swap(n_band, n_lon, way, turn))  14 us
    ppermute x11, waiting for transfers between devices, move(): return lax.ppermute(value, axes, swap(n_band, n_lon, way, turn))  4.56 us
    pallas_call x1, Pallas kernels, far_part(): pl.pallas_call(functools.partial(far_kernel, n_band - 1), in_specs=[HBM]...  3.15 us
    pallas_call x1, Pallas kernels, near_part(): pl.pallas_call(functools.partial(near_kernel, n_band - 1), in_specs=[HBM]...  2.55 us
    pallas_call x1, Pallas kernels, pack(): pl.pallas_call(pack_kernel, in_specs=[HBM, HBM], out_specs=[VM] * 7, out_...  2.1 us
    pallas_call x1, Pallas kernels, prep(): pl.pallas_call(functools.partial(prep_kernel, n_band - 1), in_specs=[VM]...  1.66 us
    pallas_call x1, Pallas kernels, spread(): pl.pallas_call(spread_kernel, in_specs=[VM], out_specs=[VM] * 2, out_shap...  1.08 us
  transfers between devices with their start and end apart: 11, of which 4 were waited for; matrix products, arithmetic and copies ran while one was open for 0% of the time, Pallas kernels for 12%

profile of v7, /device:TPU:0, one launch (start us, length us, event | category | flops | bytes accessed | tf_op | source)
XLA Modules:
  0.0 45.9 jit_solution(10272425979501100820)
XLA Ops:
  0.0 2.1 %pack.1 = (bf16[32,8,128]{2,1,0:T(8,128)(2,1)S(1)}, bf16[160,8,128]{2,1,0:T(8,128)(2,1)S(1)}, bf16[32,8,128]{2,1,0:T(8,128)(2,1)S(1)}, bf16[32,8,128]{2,1,0:T(8,...) custom-call(s32[2,128]{1,0:T(2,128)} %bitcast.7, ...), custom_call_target="tpu_custom_call" | custom-call | bytes 1048576 | tf_op jit(solution)/shard_map/pack/pallas_call | solution.py:107
  2.1 0.5 %collective-permute-start = (bf16[160,8,128]{2,1,0:T(8,128)(2,1)S(1)}, bf16[160,8,128]{2,1,0:T(8,128)(2,1)S(1)}, u32[]{:S(2)}, u32[]{:S(2)}) collective-permute-start(bf16[160,8,128]{2,1,0:T(8,128)(2,1)S(1)} %get-tuple-element.31), channel_id=1, source_target_pairs={{0,1},{1,0},{2,3},{3,2},{4,5},{5,4},{6,7},{7,6},{8,9},{9,8},{10,11... | collective-permute-start | bytes 983048 | tf_op jit(solution)/shard_map/ppermute | solution.py:586
  2.6 1.3 %collective-permute-done.core_ref = bf16[160,8,128]{2,1,0:T(8,128)(2,1)S(1)} collective-permute-done((bf16[160,8,128]{2,1,0:T(8,128)(2,1)S(1)}, bf16[160,8,128]{2,1,0:T(8,128)(2,1)S(1)}, u32[]{:S(2)}, u32[]{:S(2)}) %collective-permute-start) | collective-permute-done | bytes 327712 | tf_op jit(solution)/shard_map/ppermute | solution.py:586
  3.9 2.7 %collective-permute-start.1 = (bf16[64,8,128]{2,1,0:T(8,128)(2,1)S(1)}, bf16[64,8,128]{2,1,0:T(8,128)(2,1)S(1)}, u32[]{:S(2)}, u32[]{:S(2)}) collective-permute-start(bf16[64,8,128]{2,1,0:T(8,128)(2,1)S(1)} %get-tuple-element.35), channel_id=1, source_target_pairs={{0,3},{1,2},{2,1},{3,0},{4,7},{5,6},{6,5},{7,4},{8,11},{9,10},{10,... | collective-permute-start | bytes 393224 | tf_op jit(solution)/shard_map/ppermute | solution.py:586
  6.6 1.5 %collective-permute-start.2 = (bf16[64,8,128]{2,1,0:T(8,128)(2,1)S(1)}, bf16[64,8,128]{2,1,0:T(8,128)(2,1)S(1)}, u32[]{:S(2)}, u32[]{:S(2)}) collective-permute-start(bf16[64,8,128]{2,1,0:T(8,128)(2,1)S(1)} %get-tuple-element.36), channel_id=1, source_target_pairs={{0,4},{1,5},{2,6},{3,7},{4,0},{5,1},{6,2},{7,3},{8,12},{9,13},{10,... | collective-permute-start | bytes 393224 | tf_op jit(solution)/shard_map/ppermute | solution.py:586
  8.1 0.1 collective-permute-start.5
  8.2 2.3 %collective-permute-start.3 = (bf16[32,8,128]{2,1,0:T(8,128)(2,1)S(1)}, bf16[32,8,128]{2,1,0:T(8,128)(2,1)S(1)}, u32[]{:S(2)}, u32[]{:S(2)}) collective-permute-start(bf16[32,8,128]{2,1,0:T(8,128)(2,1)S(1)} %get-tuple-element.37), channel_id=1, source_target_pairs={{0,7},{1,6},{2,5},{3,4},{4,3},{5,2},{6,1},{7,0},{8,15},{9,14},{10,... | collective-permute-start | bytes 196616 | tf_op jit(solution)/shard_map/ppermute | solution.py:586
  10.5 0.7 %collective-permute-start.6 = (bf16[32,8,128]{2,1,0:T(8,128)(2,1)S(1)}, bf16[32,8,128]{2,1,0:T(8,128)(2,1)S(1)}, u32[]{:S(2)}, u32[]{:S(2)}) collective-permute-start(bf16[32,8,128]{2,1,0:T(8,128)(2,1)S(1)} %get-tuple-element.40), channel_id=1, source_target_pairs={{0,1},{1,0},{2,3},{3,2},{4,11},{5,10},{6,9},{7,8},{8,7},{9,6},{10,... | collective-permute-start | bytes 196616 | tf_op jit(solution)/shard_map/ppermute | solution.py:586
  11.2 0.0 collective-permute-done.1.x_ref.refs_0_
  11.2 2.9 %collective-permute-start.4 = (bf16[32,8,128]{2,1,0:T(8,128)(2,1)S(1)}, bf16[32,8,128]{2,1,0:T(8,128)(2,1)S(1)}, u32[]{:S(2)}, u32[]{:S(2)}) collective-permute-start(bf16[32,8,128]{2,1,0:T(8,128)(2,1)S(1)} %get-tuple-element.38), channel_id=1, source_target_pairs={{0,7},{1,6},{2,5},{3,4},{4,3},{5,2},{6,1},{7,0},{8,9},{9,8},{10,11... | collective-permute-start | bytes 196616 | tf_op jit(solution)/shard_map/ppermute | solution.py:586
  14.2 2.5 %near.1 = (f32[256,8,128]{2,1,0:T(8,128)S(1)}, bf16[2,32,128,128]{3,2,1,0:T(8,128)(2,1)S(1)}) custom-call(s32[12,1,32]{2,1,0:T(1,128)} %bitcast.5, bf16[32,8,128]{2,1,0:T(8,128)(2,1)S(1)} %get-tuple-element.41.own_ref, bf16[160,8,128]{2,1,0:T(8,128)(2,1)S(1)} %collective-permute-done.core_ref, bf16[64,8,128]{2,1,0:T(8,128)(2,1)S(1)} %collective-permute-done.1.x_ref.refs_0_, ...), custom_call_target="tpu_custom_call" | custom-call | flops 25165824 | bytes 12582912 | tf_op jit(solution)/shard_map/near/pallas_call | solution.py:306
  16.7 0.0 collective-permute-done.3.refs_2_
  16.8 1.6 %collective-permute-done.2.refs_1_ = bf16[64,8,128]{2,1,0:T(8,128)(2,1)S(1)} collective-permute-done((bf16[64,8,128]{2,1,0:T(8,128)(2,1)S(1)}, bf16[64,8,128]{2,1,0:T(8,128)(2,1)S(1)}, u32[]{:S(2)}, u32[]{:S(2)}) %collective-permute-start.2) | collective-permute-done | bytes 131104 | tf_op jit(solution)/shard_map/ppermute | solution.py:586
  18.4 0.0 collective-permute-done.5.refs_4_
  18.4 3.2 %far.1 = (bf16[512,512]{1,0:T(8,128)(2,1)S(1)}, bf16[16,512]{1,0:T(8,128)(2,1)S(1)}, bf16[16,512]{1,0:T(8,128)(2,1)S(1)}) custom-call(s32[12,1,32]{2,1,0:T(1,128)} %bitcast.6, bf16[64,8,128]{2,1,0:T(8,128)(2,1)S(1)} %collective-permute-done.1.x_ref.refs_0_, bf16[64,8,128]{2,1,0:T(8,128)(2,1)S(1)} %collective-permute-done.2.refs_1_, ...), custom_call_target="tpu_custom_call" | custom-call | flops 58720256 | bytes 8388608 | tf_op jit(solution)/shard_map/far/pallas_call | solution.py:331
  21.6 2.5 %collective-permute-start.7 = (bf16[16,512]{1,0:T(8,128)(2,1)S(1)}, bf16[16,512]{1,0:T(8,128)(2,1)S(1)}, u32[]{:S(2)}, u32[]{:S(2)}) collective-permute-start(bf16[16,512]{1,0:T(8,128)(2,1)S(1)} %get-tuple-element.44), channel_id=1, source_target_pairs={{0,4},{1,5},{2,6},{3,7},{4,0},{5,1},{6,2},{7,3},{8,12},{9,13},{10,... | collective-permute-start | bytes 49160 | tf_op jit(solution)/shard_map/ppermute | solution.py:586
  24.1 1.1 %spread.1 = (bf16[11,256,384]{2,1,0:T(8,128)(2,1)S(1)}, bf16[512,1536]{1,0:T(8,128)(2,1)S(1)}) custom-call(bf16[512,512]{1,0:T(8,128)(2,1)S(1)} %get-tuple-element.46.fld_ref), custom_call_target="tpu_custom_call" | custom-call | flops 805306368 | bytes 4194304 | tf_op jit(solution)/shard_map/spread/pallas_call | solution.py:412
  25.2 0.6 %collective-permute-done.7.a_ref = bf16[16,512]{1,0:T(8,128)(2,1)S(1)} collective-permute-done((bf16[16,512]{1,0:T(8,128)(2,1)S(1)}, bf16[16,512]{1,0:T(8,128)(2,1)S(1)}, u32[]{:S(2)}, u32[]{:S(2)}) %collective-permute-start.7) | collective-permute-done | bytes 16416 | tf_op jit(solution)/shard_map/ppermute | solution.py:586
  25.8 0.2 edges.1
  26.0 0.1 collective-permute-start.10
  26.1 0.6 %collective-permute-start.9 = (bf16[16,544]{1,0:T(8,128)(2,1)S(1)}, bf16[16,544]{1,0:T(8,128)(2,1)S(1)}, u32[]{:S(2)}, u32[]{:S(2)}) collective-permute-start(bf16[16,544]{1,0:T(8,128)(2,1)S(1)} %edges.1), channel_id=1, source_target_pairs={{0,1},{1,0},{2,3},{3,2},{4,5},{5,4},{6,7},{7,6},{8,9},{9,8},{10,11... | collective-permute-start | bytes 52232 | tf_op jit(solution)/shard_map/ppermute | solution.py:586
  26.7 1.7 %prep.1 = (bf16[256,1536]{1,0:T(8,128)(2,1)S(1)}, f32[1,256]{1,0:T(1,128)S(1)}, bf16[4,512,256]{2,1,0:T(8,128)(2,1)S(1)}, bf16[3,256,384]{2,1,0:T(8,128)(2,1)S(1)}) custom-call(bf16[9,8,128]{2,1,0:T(8,128)(2,1)} %stem_ref.1, f32[1,128]{1,0:T(1,128)} %bitcast.8, bf16[9,128,128]{2,1,0:T(8,128)(2,1)} %mix_ref.1, ...), custom_call_target="tpu_custom_call" | custom-call | bytes 2097152 | tf_op jit(solution)/shard_map/prep/pallas_call | solution.py:191
  28.4 1.0 %collective-permute-done.10.x_ref = bf16[16,544]{1,0:T(8,128)(2,1)S(1)} collective-permute-done((bf16[16,544]{1,0:T(8,128)(2,1)S(1)}, bf16[16,544]{1,0:T(8,128)(2,1)S(1)}, u32[]{:S(2)}, u32[]{:S(2)}) %collective-permute-start.10) | collective-permute-done | bytes 17440 | tf_op jit(solution)/shard_map/ppermute | solution.py:586
  29.4 16.5 %conv.1 = bf16[64,512,128]{2,1,0:T(8,128)(2,1)} custom-call(bf16[11,256,384]{2,1,0:T(8,128)(2,1)S(1)} %get-tuple-element.49.g_ref, bf16[16,544]{1,0:T(8,128)(2,1)S(1)} %collective-permute-done.9.core_ref, bf16[16,544]{1,0:T(8,128)(2,1)S(1)} %collective-permute-done.10.x_ref, bf16[256,1536]{1,0:T(8,128)(2,1)S(1)} %get-tuple-element.53.ws_ref, ...), custom_call_target="tpu_custom_call" | custom-call | flops 9663676416 | bytes 12582912 | tf_op jit(solution)/shard_map/conv/pallas_call | solution.py:561
  (8 shorter events, 0.0 us)
Async XLA Ops:
  2.1 1.8 %collective-permute-start = (bf16[160,8,128]{2,1,0:T(8,128)(2,1)S(1)}, bf16[160,8,128]{2,1,0:T(8,128)(2,1)S(1)}, u32[]{:S(2)}, u32[]{:S(2)}) collective-permute-start(bf16[160,8,128]{2,1,0:T(8,128)(2,1)S(1)} %get-tuple-element.31), channel_id=1, source_target_pairs={{0,1},{1,0},{2,3},{3,2},{4,5},{5,4},{6,7},{7,6},{8,9},{9,8},{10,11... | collective-permute-start | bytes 983048 | tf_op jit(solution)/shard_map/ppermute | solution.py:586
  3.9 7.3 %collective-permute-start.1 = (bf16[64,8,128]{2,1,0:T(8,128)(2,1)S(1)}, bf16[64,8,128]{2,1,0:T(8,128)(2,1)S(1)}, u32[]{:S(2)}, u32[]{:S(2)}) collective-permute-start(bf16[64,8,128]{2,1,0:T(8,128)(2,1)S(1)} %get-tuple-element.35), channel_id=1, source_target_pairs={{0,3},{1,2},{2,1},{3,0},{4,7},{5,6},{6,5},{7,4},{8,11},{9,10},{10,... | collective-permute-start | bytes 393224 | tf_op jit(solution)/shard_map/ppermute | solution.py:586
  6.6 11.8 %collective-permute-start.2 = (bf16[64,8,128]{2,1,0:T(8,128)(2,1)S(1)}, bf16[64,8,128]{2,1,0:T(8,128)(2,1)S(1)}, u32[]{:S(2)}, u32[]{:S(2)}) collective-permute-start(bf16[64,8,128]{2,1,0:T(8,128)(2,1)S(1)} %get-tuple-element.36), channel_id=1, source_target_pairs={{0,4},{1,5},{2,6},{3,7},{4,0},{5,1},{6,2},{7,3},{8,12},{9,13},{10,... | collective-permute-start | bytes 393224 | tf_op jit(solution)/shard_map/ppermute | solution.py:586
  8.1 10.3 %collective-permute-start.5 = (bf16[64,8,128]{2,1,0:T(8,128)(2,1)S(1)}, bf16[64,8,128]{2,1,0:T(8,128)(2,1)S(1)}, u32[]{:S(2)}, u32[]{:S(2)}) collective-permute-start(bf16[64,8,128]{2,1,0:T(8,128)(2,1)S(1)} %get-tuple-element.39), channel_id=1, source_target_pairs={{0,1},{1,0},{2,3},{3,2},{4,8},{5,9},{6,10},{7,11},{8,4},{9,5},{10,... | collective-permute-start | bytes 393224 | tf_op jit(solution)/shard_map/ppermute | solution.py:586
  8.2 8.6 %collective-permute-start.3 = (bf16[32,8,128]{2,1,0:T(8,128)(2,1)S(1)}, bf16[32,8,128]{2,1,0:T(8,128)(2,1)S(1)}, u32[]{:S(2)}, u32[]{:S(2)}) collective-permute-start(bf16[32,8,128]{2,1,0:T(8,128)(2,1)S(1)} %get-tuple-element.37), channel_id=1, source_target_pairs={{0,7},{1,6},{2,5},{3,4},{4,3},{5,2},{6,1},{7,0},{8,15},{9,14},{10,... | collective-permute-start | bytes 196616 | tf_op jit(solution)/shard_map/ppermute | solution.py:586
  10.5 6.2 %collective-permute-start.6 = (bf16[32,8,128]{2,1,0:T(8,128)(2,1)S(1)}, bf16[32,8,128]{2,1,0:T(8,128)(2,1)S(1)}, u32[]{:S(2)}, u32[]{:S(2)}) collective-permute-start(bf16[32,8,128]{2,1,0:T(8,128)(2,1)S(1)} %get-tuple-element.40), channel_id=1, source_target_pairs={{0,1},{1,0},{2,3},{3,2},{4,11},{5,10},{6,9},{7,8},{8,7},{9,6},{10,... | collective-permute-start | bytes 196616 | tf_op jit(solution)/shard_map/ppermute | solution.py:586
  11.2 5.5 %collective-permute-start.4 = (bf16[32,8,128]{2,1,0:T(8,128)(2,1)S(1)}, bf16[32,8,128]{2,1,0:T(8,128)(2,1)S(1)}, u32[]{:S(2)}, u32[]{:S(2)}) collective-permute-start(bf16[32,8,128]{2,1,0:T(8,128)(2,1)S(1)} %get-tuple-element.38), channel_id=1, source_target_pairs={{0,7},{1,6},{2,5},{3,4},{4,3},{5,2},{6,1},{7,0},{8,9},{9,8},{10,11... | collective-permute-start | bytes 196616 | tf_op jit(solution)/shard_map/ppermute | solution.py:586
  21.6 4.3 %collective-permute-start.7 = (bf16[16,512]{1,0:T(8,128)(2,1)S(1)}, bf16[16,512]{1,0:T(8,128)(2,1)S(1)}, u32[]{:S(2)}, u32[]{:S(2)}) collective-permute-start(bf16[16,512]{1,0:T(8,128)(2,1)S(1)} %get-tuple-element.44), channel_id=1, source_target_pairs={{0,4},{1,5},{2,6},{3,7},{4,0},{5,1},{6,2},{7,3},{8,12},{9,13},{10,... | collective-permute-start | bytes 49160 | tf_op jit(solution)/shard_map/ppermute | solution.py:586
  24.1 1.7 %collective-permute-start.8 = (bf16[16,512]{1,0:T(8,128)(2,1)S(1)}, bf16[16,512]{1,0:T(8,128)(2,1)S(1)}, u32[]{:S(2)}, u32[]{:S(2)}) collective-permute-start(bf16[16,512]{1,0:T(8,128)(2,1)S(1)} %get-tuple-element.45), channel_id=1, source_target_pairs={{0,1},{1,0},{2,3},{3,2},{4,8},{5,9},{6,10},{7,11},{8,4},{9,5},{10,... | collective-permute-start | bytes 49160 | tf_op jit(solution)/shard_map/ppermute | solution.py:586
  24.1 5.3 %copy-start = (f32[128]{0:T(128)S(1)}, f32[128]{0:T(128)}, u32[]{:S(2)}) copy-start(f32[128]{0:T(128)} %param.15) | copy-start | bytes 1540
  26.0 3.4 %collective-permute-start.10 = (bf16[16,544]{1,0:T(8,128)(2,1)S(1)}, bf16[16,544]{1,0:T(8,128)(2,1)S(1)}, u32[]{:S(2)}, u32[]{:S(2)}) collective-permute-start(bf16[16,544]{1,0:T(8,128)(2,1)S(1)} %edges.1), channel_id=1, source_target_pairs={{0,3},{1,2},{2,1},{3,0},{4,7},{5,6},{6,5},{7,4},{8,11},{9,10},{10,... | collective-permute-start | bytes 52232 | tf_op jit(solution)/shard_map/ppermute | solution.py:586
  26.1 3.3 %collective-permute-start.9 = (bf16[16,544]{1,0:T(8,128)(2,1)S(1)}, bf16[16,544]{1,0:T(8,128)(2,1)S(1)}, u32[]{:S(2)}, u32[]{:S(2)}) collective-permute-start(bf16[16,544]{1,0:T(8,128)(2,1)S(1)} %edges.1), channel_id=1, source_target_pairs={{0,1},{1,0},{2,3},{3,2},{4,5},{5,4},{6,7},{7,6},{8,9},{9,8},{10,11... | collective-permute-start | bytes 52232 | tf_op jit(solution)/shard_map/ppermute | solution.py:586

commit v8 on v7

--- a/solution.py
+++ b/solution.py
@@ -96,7 +96,7 @@
             buf[at] = block
         return carry
 
-    lax.fori_loop(0, src_ref.shape[0], one, 0, unroll=8)
+    lax.fori_loop(0, src_ref.shape[0], one, 0, unroll=32)
     for out, (begin, groups) in zip(outs, PARTS):
         out[...] = buf[begin * 32 : (begin + groups) * 32]
 

time: 46.1 us -> 46.1 us (level)
  no operation moved by 1% of the time
where the time goes in v8:
time: 46.1 us; the launch traced here: 45.9 us
  Pallas kernels  27.2 us (59%)
  starting transfers between devices  14 us (30%)
  waiting for transfers between devices  4.55 us (10%)
    pallas_call x1, Pallas kernels, conv(): pl.pallas_call(functools.partial(conv_kernel, n_band - 1), in_specs=[VM]...  16.5 us
    ppermute x11, starting transfers between devices, move(): return lax.ppermute(value, axes, swap(n_band, n_lon, way, turn))  14 us
    ppermute x11, waiting for transfers between devices, move(): return lax.ppermute(value, axes, swap(n_band, n_lon, way, turn))  4.55 us
    pallas_call x1, Pallas kernels, far_part(): pl.pallas_call(functools.partial(far_kernel, n_band - 1), in_specs=[HBM]...  3.15 us
    pallas_call x1, Pallas kernels, near_part(): pl.pallas_call(functools.partial(near_kernel, n_band - 1), in_specs=[HBM]...  2.55 us
    pallas_call x1, Pallas kernels, pack(): pl.pallas_call(pack_kernel, in_specs=[HBM, HBM], out_specs=[VM] * 7, out_...  2.09 us
    pallas_call x1, Pallas kernels, prep(): pl.pallas_call(functools.partial(prep_kernel, n_band - 1), in_specs=[VM]...  1.66 us
    pallas_call x1, Pallas kernels, spread(): pl.pallas_call(spread_kernel, in_specs=[VM], out_specs=[VM] * 2, out_shap...  1.08 us
  transfers between devices with their start and end apart: 11, of which 4 were waited for; matrix products, arithmetic and copies ran while one was open for 0% of the time, Pallas kernels for 12%

profile of v8, /device:TPU:0, one launch (start us, length us, event | category | flops | bytes accessed | tf_op | source)
XLA Modules:
  0.0 45.9 jit_solution(13685680005955225856)
XLA Ops:
  0.0 2.1 %pack.1 = (bf16[32,8,128]{2,1,0:T(8,128)(2,1)S(1)}, bf16[160,8,128]{2,1,0:T(8,128)(2,1)S(1)}, bf16[32,8,128]{2,1,0:T(8,128)(2,1)S(1)}, bf16[32,8,128]{2,1,0:T(8,...) custom-call(s32[2,128]{1,0:T(2,128)} %bitcast.7, ...), custom_call_target="tpu_custom_call" | custom-call | bytes 1048576 | tf_op jit(solution)/shard_map/pack/pallas_call | solution.py:107
  2.1 0.5 %collective-permute-start = (bf16[160,8,128]{2,1,0:T(8,128)(2,1)S(1)}, bf16[160,8,128]{2,1,0:T(8,128)(2,1)S(1)}, u32[]{:S(2)}, u32[]{:S(2)}) collective-permute-start(bf16[160,8,128]{2,1,0:T(8,128)(2,1)S(1)} %get-tuple-element.31), channel_id=1, source_target_pairs={{0,1},{1,0},{2,3},{3,2},{4,5},{5,4},{6,7},{7,6},{8,9},{9,8},{10,11... | collective-permute-start | bytes 983048 | tf_op jit(solution)/shard_map/ppermute | solution.py:586
  2.6 1.3 %collective-permute-done.core_ref = bf16[160,8,128]{2,1,0:T(8,128)(2,1)S(1)} collective-permute-done((bf16[160,8,128]{2,1,0:T(8,128)(2,1)S(1)}, bf16[160,8,128]{2,1,0:T(8,128)(2,1)S(1)}, u32[]{:S(2)}, u32[]{:S(2)}) %collective-permute-start) | collective-permute-done | bytes 327712 | tf_op jit(solution)/shard_map/ppermute | solution.py:586
  3.9 2.7 %collective-permute-start.1 = (bf16[64,8,128]{2,1,0:T(8,128)(2,1)S(1)}, bf16[64,8,128]{2,1,0:T(8,128)(2,1)S(1)}, u32[]{:S(2)}, u32[]{:S(2)}) collective-permute-start(bf16[64,8,128]{2,1,0:T(8,128)(2,1)S(1)} %get-tuple-element.35), channel_id=1, source_target_pairs={{0,3},{1,2},{2,1},{3,0},{4,7},{5,6},{6,5},{7,4},{8,11},{9,10},{10,... | collective-permute-start | bytes 393224 | tf_op jit(solution)/shard_map/ppermute | solution.py:586
  6.6 1.5 %collective-permute-start.2 = (bf16[64,8,128]{2,1,0:T(8,128)(2,1)S(1)}, bf16[64,8,128]{2,1,0:T(8,128)(2,1)S(1)}, u32[]{:S(2)}, u32[]{:S(2)}) collective-permute-start(bf16[64,8,128]{2,1,0:T(8,128)(2,1)S(1)} %get-tuple-element.36), channel_id=1, source_target_pairs={{0,4},{1,5},{2,6},{3,7},{4,0},{5,1},{6,2},{7,3},{8,12},{9,13},{10,... | collective-permute-start | bytes 393224 | tf_op jit(solution)/shard_map/ppermute | solution.py:586
  8.1 0.1 collective-permute-start.5
  8.2 2.3 %collective-permute-start.3 = (bf16[32,8,128]{2,1,0:T(8,128)(2,1)S(1)}, bf16[32,8,128]{2,1,0:T(8,128)(2,1)S(1)}, u32[]{:S(2)}, u32[]{:S(2)}) collective-permute-start(bf16[32,8,128]{2,1,0:T(8,128)(2,1)S(1)} %get-tuple-element.37), channel_id=1, source_target_pairs={{0,7},{1,6},{2,5},{3,4},{4,3},{5,2},{6,1},{7,0},{8,15},{9,14},{10,... | collective-permute-start | bytes 196616 | tf_op jit(solution)/shard_map/ppermute | solution.py:586
  10.5 0.7 %collective-permute-start.6 = (bf16[32,8,128]{2,1,0:T(8,128)(2,1)S(1)}, bf16[32,8,128]{2,1,0:T(8,128)(2,1)S(1)}, u32[]{:S(2)}, u32[]{:S(2)}) collective-permute-start(bf16[32,8,128]{2,1,0:T(8,128)(2,1)S(1)} %get-tuple-element.40), channel_id=1, source_target_pairs={{0,1},{1,0},{2,3},{3,2},{4,11},{5,10},{6,9},{7,8},{8,7},{9,6},{10,... | collective-permute-start | bytes 196616 | tf_op jit(solution)/shard_map/ppermute | solution.py:586
  11.2 0.0 collective-permute-done.1.x_ref.refs_0_
  11.2 2.9 %collective-permute-start.4 = (bf16[32,8,128]{2,1,0:T(8,128)(2,1)S(1)}, bf16[32,8,128]{2,1,0:T(8,128)(2,1)S(1)}, u32[]{:S(2)}, u32[]{:S(2)}) collective-permute-start(bf16[32,8,128]{2,1,0:T(8,128)(2,1)S(1)} %get-tuple-element.38), channel_id=1, source_target_pairs={{0,7},{1,6},{2,5},{3,4},{4,3},{5,2},{6,1},{7,0},{8,9},{9,8},{10,11... | collective-permute-start | bytes 196616 | tf_op jit(solution)/shard_map/ppermute | solution.py:586
  14.2 2.5 %near.1 = (f32[256,8,128]{2,1,0:T(8,128)S(1)}, bf16[2,32,128,128]{3,2,1,0:T(8,128)(2,1)S(1)}) custom-call(s32[12,1,32]{2,1,0:T(1,128)} %bitcast.5, bf16[32,8,128]{2,1,0:T(8,128)(2,1)S(1)} %get-tuple-element.41.own_ref, bf16[160,8,128]{2,1,0:T(8,128)(2,1)S(1)} %collective-permute-done.core_ref, bf16[64,8,128]{2,1,0:T(8,128)(2,1)S(1)} %collective-permute-done.1.x_ref.refs_0_, ...), custom_call_target="tpu_custom_call" | custom-call | flops 25165824 | bytes 12582912 | tf_op jit(solution)/shard_map/near/pallas_call | solution.py:306
  16.7 0.0 collective-permute-done.3.refs_2_
  16.8 0.0 collective-permute-done.6.refs_5_
  16.8 1.6 %collective-permute-done.2.refs_1_ = bf16[64,8,128]{2,1,0:T(8,128)(2,1)S(1)} collective-permute-done((bf16[64,8,128]{2,1,0:T(8,128)(2,1)S(1)}, bf16[64,8,128]{2,1,0:T(8,128)(2,1)S(1)}, u32[]{:S(2)}, u32[]{:S(2)}) %collective-permute-start.2) | collective-permute-done | bytes 131104 | tf_op jit(solution)/shard_map/ppermute | solution.py:586
  18.4 3.2 %far.1 = (bf16[512,512]{1,0:T(8,128)(2,1)S(1)}, bf16[16,512]{1,0:T(8,128)(2,1)S(1)}, bf16[16,512]{1,0:T(8,128)(2,1)S(1)}) custom-call(s32[12,1,32]{2,1,0:T(1,128)} %bitcast.6, bf16[64,8,128]{2,1,0:T(8,128)(2,1)S(1)} %collective-permute-done.1.x_ref.refs_0_, bf16[64,8,128]{2,1,0:T(8,128)(2,1)S(1)} %collective-permute-done.2.refs_1_, ...), custom_call_target="tpu_custom_call" | custom-call | flops 58720256 | bytes 8388608 | tf_op jit(solution)/shard_map/far/pallas_call | solution.py:331
  21.6 2.5 %collective-permute-start.7 = (bf16[16,512]{1,0:T(8,128)(2,1)S(1)}, bf16[16,512]{1,0:T(8,128)(2,1)S(1)}, u32[]{:S(2)}, u32[]{:S(2)}) collective-permute-start(bf16[16,512]{1,0:T(8,128)(2,1)S(1)} %get-tuple-element.44), channel_id=1, source_target_pairs={{0,4},{1,5},{2,6},{3,7},{4,0},{5,1},{6,2},{7,3},{8,12},{9,13},{10,... | collective-permute-start | bytes 49160 | tf_op jit(solution)/shard_map/ppermute | solution.py:586
  24.1 1.1 %spread.1 = (bf16[11,256,384]{2,1,0:T(8,128)(2,1)S(1)}, bf16[512,1536]{1,0:T(8,128)(2,1)S(1)}) custom-call(bf16[512,512]{1,0:T(8,128)(2,1)S(1)} %get-tuple-element.46.fld_ref), custom_call_target="tpu_custom_call" | custom-call | flops 805306368 | bytes 4194304 | tf_op jit(solution)/shard_map/spread/pallas_call | solution.py:412
  25.2 0.6 %collective-permute-done.7.a_ref = bf16[16,512]{1,0:T(8,128)(2,1)S(1)} collective-permute-done((bf16[16,512]{1,0:T(8,128)(2,1)S(1)}, bf16[16,512]{1,0:T(8,128)(2,1)S(1)}, u32[]{:S(2)}, u32[]{:S(2)}) %collective-permute-start.7) | collective-permute-done | bytes 16416 | tf_op jit(solution)/shard_map/ppermute | solution.py:586
  25.8 0.2 edges.1
  26.0 0.1 collective-permute-start.10
  26.1 0.6 %collective-permute-start.9 = (bf16[16,544]{1,0:T(8,128)(2,1)S(1)}, bf16[16,544]{1,0:T(8,128)(2,1)S(1)}, u32[]{:S(2)}, u32[]{:S(2)}) collective-permute-start(bf16[16,544]{1,0:T(8,128)(2,1)S(1)} %edges.1), channel_id=1, source_target_pairs={{0,1},{1,0},{2,3},{3,2},{4,5},{5,4},{6,7},{7,6},{8,9},{9,8},{10,11... | collective-permute-start | bytes 52232 | tf_op jit(solution)/shard_map/ppermute | solution.py:586
  26.7 1.7 %prep.1 = (bf16[256,1536]{1,0:T(8,128)(2,1)S(1)}, f32[1,256]{1,0:T(1,128)S(1)}, bf16[4,512,256]{2,1,0:T(8,128)(2,1)S(1)}, bf16[3,256,384]{2,1,0:T(8,128)(2,1)S(1)}) custom-call(bf16[9,8,128]{2,1,0:T(8,128)(2,1)} %stem_ref.1, f32[1,128]{1,0:T(1,128)} %bitcast.8, bf16[9,128,128]{2,1,0:T(8,128)(2,1)} %mix_ref.1, ...), custom_call_target="tpu_custom_call" | custom-call | bytes 2097152 | tf_op jit(solution)/shard_map/prep/pallas_call | solution.py:191
  28.4 1.0 %collective-permute-done.10.x_ref = bf16[16,544]{1,0:T(8,128)(2,1)S(1)} collective-permute-done((bf16[16,544]{1,0:T(8,128)(2,1)S(1)}, bf16[16,544]{1,0:T(8,128)(2,1)S(1)}, u32[]{:S(2)}, u32[]{:S(2)}) %collective-permute-start.10) | collective-permute-done | bytes 17440 | tf_op jit(solution)/shard_map/ppermute | solution.py:586
  29.4 16.5 %conv.1 = bf16[64,512,128]{2,1,0:T(8,128)(2,1)} custom-call(bf16[11,256,384]{2,1,0:T(8,128)(2,1)S(1)} %get-tuple-element.49.g_ref, bf16[16,544]{1,0:T(8,128)(2,1)S(1)} %collective-permute-done.9.core_ref, bf16[16,544]{1,0:T(8,128)(2,1)S(1)} %collective-permute-done.10.x_ref, bf16[256,1536]{1,0:T(8,128)(2,1)S(1)} %get-tuple-element.53.ws_ref, ...), custom_call_target="tpu_custom_call" | custom-call | flops 9663676416 | bytes 12582912 | tf_op jit(solution)/shard_map/conv/pallas_call | solution.py:561
  (8 shorter events, 0.0 us)
Async XLA Ops:
  2.1 1.8 %collective-permute-start = (bf16[160,8,128]{2,1,0:T(8,128)(2,1)S(1)}, bf16[160,8,128]{2,1,0:T(8,128)(2,1)S(1)}, u32[]{:S(2)}, u32[]{:S(2)}) collective-permute-start(bf16[160,8,128]{2,1,0:T(8,128)(2,1)S(1)} %get-tuple-element.31), channel_id=1, source_target_pairs={{0,1},{1,0},{2,3},{3,2},{4,5},{5,4},{6,7},{7,6},{8,9},{9,8},{10,11... | collective-permute-start | bytes 983048 | tf_op jit(solution)/shard_map/ppermute | solution.py:586
  3.9 7.3 %collective-permute-start.1 = (bf16[64,8,128]{2,1,0:T(8,128)(2,1)S(1)}, bf16[64,8,128]{2,1,0:T(8,128)(2,1)S(1)}, u32[]{:S(2)}, u32[]{:S(2)}) collective-permute-start(bf16[64,8,128]{2,1,0:T(8,128)(2,1)S(1)} %get-tuple-element.35), channel_id=1, source_target_pairs={{0,3},{1,2},{2,1},{3,0},{4,7},{5,6},{6,5},{7,4},{8,11},{9,10},{10,... | collective-permute-start | bytes 393224 | tf_op jit(solution)/shard_map/ppermute | solution.py:586
  6.6 11.8 %collective-permute-start.2 = (bf16[64,8,128]{2,1,0:T(8,128)(2,1)S(1)}, bf16[64,8,128]{2,1,0:T(8,128)(2,1)S(1)}, u32[]{:S(2)}, u32[]{:S(2)}) collective-permute-start(bf16[64,8,128]{2,1,0:T(8,128)(2,1)S(1)} %get-tuple-element.36), channel_id=1, source_target_pairs={{0,4},{1,5},{2,6},{3,7},{4,0},{5,1},{6,2},{7,3},{8,12},{9,13},{10,... | collective-permute-start | bytes 393224 | tf_op jit(solution)/shard_map/ppermute | solution.py:586
  8.1 10.3 %collective-permute-start.5 = (bf16[64,8,128]{2,1,0:T(8,128)(2,1)S(1)}, bf16[64,8,128]{2,1,0:T(8,128)(2,1)S(1)}, u32[]{:S(2)}, u32[]{:S(2)}) collective-permute-start(bf16[64,8,128]{2,1,0:T(8,128)(2,1)S(1)} %get-tuple-element.39), channel_id=1, source_target_pairs={{0,1},{1,0},{2,3},{3,2},{4,8},{5,9},{6,10},{7,11},{8,4},{9,5},{10,... | collective-permute-start | bytes 393224 | tf_op jit(solution)/shard_map/ppermute | solution.py:586
  8.2 8.6 %collective-permute-start.3 = (bf16[32,8,128]{2,1,0:T(8,128)(2,1)S(1)}, bf16[32,8,128]{2,1,0:T(8,128)(2,1)S(1)}, u32[]{:S(2)}, u32[]{:S(2)}) collective-permute-start(bf16[32,8,128]{2,1,0:T(8,128)(2,1)S(1)} %get-tuple-element.37), channel_id=1, source_target_pairs={{0,7},{1,6},{2,5},{3,4},{4,3},{5,2},{6,1},{7,0},{8,15},{9,14},{10,... | collective-permute-start | bytes 196616 | tf_op jit(solution)/shard_map/ppermute | solution.py:586
  10.5 6.2 %collective-permute-start.6 = (bf16[32,8,128]{2,1,0:T(8,128)(2,1)S(1)}, bf16[32,8,128]{2,1,0:T(8,128)(2,1)S(1)}, u32[]{:S(2)}, u32[]{:S(2)}) collective-permute-start(bf16[32,8,128]{2,1,0:T(8,128)(2,1)S(1)} %get-tuple-element.40), channel_id=1, source_target_pairs={{0,1},{1,0},{2,3},{3,2},{4,11},{5,10},{6,9},{7,8},{8,7},{9,6},{10,... | collective-permute-start | bytes 196616 | tf_op jit(solution)/shard_map/ppermute | solution.py:586
  11.2 5.5 %collective-permute-start.4 = (bf16[32,8,128]{2,1,0:T(8,128)(2,1)S(1)}, bf16[32,8,128]{2,1,0:T(8,128)(2,1)S(1)}, u32[]{:S(2)}, u32[]{:S(2)}) collective-permute-start(bf16[32,8,128]{2,1,0:T(8,128)(2,1)S(1)} %get-tuple-element.38), channel_id=1, source_target_pairs={{0,7},{1,6},{2,5},{3,4},{4,3},{5,2},{6,1},{7,0},{8,9},{9,8},{10,11... | collective-permute-start | bytes 196616 | tf_op jit(solution)/shard_map/ppermute | solution.py:586
  21.6 4.3 %collective-permute-start.7 = (bf16[16,512]{1,0:T(8,128)(2,1)S(1)}, bf16[16,512]{1,0:T(8,128)(2,1)S(1)}, u32[]{:S(2)}, u32[]{:S(2)}) collective-permute-start(bf16[16,512]{1,0:T(8,128)(2,1)S(1)} %get-tuple-element.44), channel_id=1, source_target_pairs={{0,4},{1,5},{2,6},{3,7},{4,0},{5,1},{6,2},{7,3},{8,12},{9,13},{10,... | collective-permute-start | bytes 49160 | tf_op jit(solution)/shard_map/ppermute | solution.py:586
  24.1 1.7 %collective-permute-start.8 = (bf16[16,512]{1,0:T(8,128)(2,1)S(1)}, bf16[16,512]{1,0:T(8,128)(2,1)S(1)}, u32[]{:S(2)}, u32[]{:S(2)}) collective-permute-start(bf16[16,512]{1,0:T(8,128)(2,1)S(1)} %get-tuple-element.45), channel_id=1, source_target_pairs={{0,1},{1,0},{2,3},{3,2},{4,8},{5,9},{6,10},{7,11},{8,4},{9,5},{10,... | collective-permute-start | bytes 49160 | tf_op jit(solution)/shard_map/ppermute | solution.py:586
  24.1 5.3 %copy-start = (f32[128]{0:T(128)S(1)}, f32[128]{0:T(128)}, u32[]{:S(2)}) copy-start(f32[128]{0:T(128)} %param.15) | copy-start | bytes 1540
  26.0 3.4 %collective-permute-start.10 = (bf16[16,544]{1,0:T(8,128)(2,1)S(1)}, bf16[16,544]{1,0:T(8,128)(2,1)S(1)}, u32[]{:S(2)}, u32[]{:S(2)}) collective-permute-start(bf16[16,544]{1,0:T(8,128)(2,1)S(1)} %edges.1), channel_id=1, source_target_pairs={{0,3},{1,2},{2,1},{3,0},{4,7},{5,6},{6,5},{7,4},{8,11},{9,10},{10,... | collective-permute-start | bytes 52232 | tf_op jit(solution)/shard_map/ppermute | solution.py:586
  26.1 3.3 %collective-permute-start.9 = (bf16[16,544]{1,0:T(8,128)(2,1)S(1)}, bf16[16,544]{1,0:T(8,128)(2,1)S(1)}, u32[]{:S(2)}, u32[]{:S(2)}) collective-permute-start(bf16[16,544]{1,0:T(8,128)(2,1)S(1)} %edges.1), channel_id=1, source_target_pairs={{0,1},{1,0},{2,3},{3,2},{4,5},{5,4},{6,7},{7,6},{8,9},{9,8},{10,11... | collective-permute-start | bytes 52232 | tf_op jit(solution)/shard_map/ppermute | solution.py:586
